TPU v7x, 512 devices: a whole 4x8x8 slice. The times are simulated.
512 devices in a mesh: leaf: 8 (over z), wide: 64 (over y, x, core).
Axes of the slice: x: 4, y: 8, z: 8, core: 2. Of those that a mesh axis runs over, the one named last changes fastest.
Arguments:
- models: bfloat16 [64, 8, 256, 1024], P('wide', 'leaf'), may hold values from -6 to 6
- leaf_slot: int32 [64, 8], P('wide'), may hold values from 0 to 7, each once within a row
- diag_blocks: bfloat16 [64, 8, 1024, 1024], P('wide', 'leaf'), may hold values from -0.1875 to 0.1875
- leaf_in: bfloat16 [64, 8, 1024, 128], P('wide', 'leaf'), may hold values from -0.1875 to 0.1875
- leaf_out: bfloat16 [64, 8, 128, 1024], P('wide', 'leaf'), may hold values from -0.25 to 0.25
- leaf_up: bfloat16 [64, 8, 128, 128], P('wide', 'leaf'), may hold values from -0.1875 to 0.1875
- leaf_down: bfloat16 [64, 8, 128, 128], P('wide', 'leaf'), may hold values from -0.5 to 0.5
- leaf_couple: bfloat16 [64, 8, 8, 128, 128], P('wide', 'leaf'), may hold values from -0.1875 to 0.1875
- upper_up: bfloat16 [64, 2, 128, 128], P('wide'), as said below
- upper_down: bfloat16 [64, 2, 128, 128], P('wide'), as said below
- upper_couple: bfloat16 [64, 3, 4, 128, 128], P('wide'), as said below
Outputs:
- response: float32 [64, 8, 256, 1024], P('wide', 'leaf')
Inputs may be any that keep to these rules, and one draw needn't show every extreme that they name: Each row of leaf_slot is a permutation; device j of group w holds the leaf at tree position w * 8 + leaf_slot[w, j]. `upper_up`: entries at w and v of level l agree whenever w // 4**l == v // 4**l. `upper_down`: entries at w and v of level l agree whenever w // 4**l == v // 4**l. `upper_couple`: entries at w and v of level l agree whenever w // 4**l == v // 4**l.
All inputs are finite; a program needn't handle non-finite values.
Results may differ from a plain program's by a relative error of at most 0.012.
Values may be sent and summed in bfloat16 or wider, within the bound.
No kernel may reach another device: no remote copies, remote signals or barrier semaphores. Data moves between devices by JAX's collectives and lax.ppermute only.
A program may use at most 64 MiB of HBM per device.

v0:
```python
import jax
import jax.numpy as jnp
from jax import lax
from jax.sharding import PartitionSpec as P


def from_partner(x, axis, stride):
    return lax.ppermute(x, axis, [(i, i ^ 1 << stride) for i in range(lax.axis_size(axis))])


def shards(
    models,
    leaf_slot,
    diag_blocks,
    leaf_in,
    leaf_out,
    leaf_up,
    leaf_down,
    leaf_couple,
    upper_up,
    upper_down,
    upper_couple,
):
    inputs = models[0, 0]
    coeff = jnp.dot(inputs, leaf_in[0, 0], preferred_element_type=jnp.float32)
    lifted = jnp.dot(coeff.astype(jnp.bfloat16), leaf_up[0, 0], preferred_element_type=jnp.float32)
    every_coeff = lax.all_gather(coeff[None].astype(jnp.bfloat16), "leaf", axis=0, tiled=True)
    current = lax.psum(lifted, "leaf")
    group_size = lax.axis_size("leaf")
    partners = jnp.arange(group_size)
    keep_leaf = (partners != lax.axis_index("leaf")).astype(jnp.bfloat16)
    neighbours = every_coeff * keep_leaf[:, None, None]
    select = (leaf_slot[0][:, None] == partners[None, :]).astype(jnp.bfloat16)
    blocks = jnp.einsum(
        "kt,trq->krq", select, leaf_couple[0, 0], preferred_element_type=jnp.float32
    ).astype(jnp.bfloat16)
    near_leaf = jnp.einsum("kmr,krq->mq", neighbours, blocks, preferred_element_type=jnp.float32)
    wide_index = lax.axis_index("wide")
    levels = (lax.axis_size("wide").bit_length() - 1) // 2
    nears = []
    for level in range(levels):
        rounded = current.astype(jnp.bfloat16)
        position = wide_index >> 2 * level & 3
        if level + 1 < levels:
            upward = jnp.dot(rounded, upper_up[0, level], preferred_element_type=jnp.float32)
            stacked = jnp.stack([current, upward])[:, None]
            for half in range(2):
                other = from_partner(stacked, "wide", 2 * level + half)
                higher = wide_index >> 2 * level + half & 1 == 1
                stacked = jnp.where(
                    higher,
                    jnp.concatenate([other, stacked], 1),
                    jnp.concatenate([stacked, other], 1),
                )
            siblings = stacked[0]
            following = jnp.sum(stacked[1], axis=0)
        else:
            stacked = current[None]
            for half in range(2):
                other = from_partner(stacked.astype(jnp.bfloat16), "wide", 2 * level + half).astype(
                    stacked.dtype
                )
                higher = wide_index >> 2 * level + half & 1 == 1
                stacked = jnp.where(
                    higher,
                    jnp.concatenate([other, stacked], 0),
                    jnp.concatenate([stacked, other], 0),
                )
            siblings = stacked
            following = current
        keep_node = (jnp.arange(4) != position).astype(jnp.bfloat16)
        masked = siblings.astype(jnp.bfloat16) * keep_node[:, None, None]
        nears.append(
            jnp.einsum(
                "smr,srq->mq", masked, upper_couple[0, level], preferred_element_type=jnp.float32
            )
        )
        current = following
    field = nears[levels - 1]
    for level in range(levels - 2, -1, -1):
        field = nears[level] + jnp.dot(
            field.astype(jnp.bfloat16), upper_down[0, level], preferred_element_type=jnp.float32
        )
    field_rounded = field.astype(jnp.bfloat16)
    leaf_field = near_leaf + jnp.dot(
        field_rounded, leaf_down[0, 0], preferred_element_type=jnp.float32
    )
    dense = jnp.dot(inputs, diag_blocks[0, 0], preferred_element_type=jnp.float32)
    response = dense + jnp.dot(
        leaf_field.astype(jnp.bfloat16), leaf_out[0, 0], preferred_element_type=jnp.float32
    )
    return response[None, None]


def solution(mesh):
    placed = (
        P("wide", "leaf", None, None),
        P("wide", None),
        P("wide", "leaf", None, None),
        P("wide", "leaf", None, None),
        P("wide", "leaf", None, None),
        P("wide", "leaf", None, None),
        P("wide", "leaf", None, None),
        P("wide", "leaf", None, None, None),
        P("wide", None, None, None),
        P("wide", None, None, None),
        P("wide", None, None, None, None),
    )
    return jax.shard_map(
        shards, mesh=mesh, in_specs=placed, out_specs=P("wide", "leaf", None, None), check_vma=False
    )
```

profile of v0, /device:TPU:28, one launch (start us, length us, event | category | flops | bytes accessed | tf_op | source)
XLA Modules:
  0.0 190.5 jit_solution(16151710143141267529)
XLA Ops:
  6.5 1.5 convolution_convert_fusion
  8.1 1.6 fusion.47
  9.7 82.5 %all-reduce.2.cloned.1.call-done = f32[256,128]{1,0:T(8,128)} async-done(((f32[256,128]{1,0:T(8,128)}), f32[256,128]{1,0:T(8,128)}) %all-reduce.2.cloned.1.call-update) | async-done | bytes 131088 | tf_op jit(solution)/shard_map/psum | solution.py:28
  92.2 1.0 convolution_bitcast_fusion.5
  94.2 1.9 %collective-permute-start = (f32[2,1,256,128]{3,2,0,1:T(8,128)S(1)}, f32[2,1,256,128]{3,2,0,1:T(8,128)S(1)}, u32[]{:S(2)}, u32[]{:S(2)}) collective-permute-start(f32[2,1,256,128]{3,2,0,1:T(8,128)S(1)} %maximum_bitcast_fusion), channel_id=1, source_target_pairs={{0,1},{1,0},{2,3},{3,2},{4,5},{5,4},{6,7},{7,6},{8,9},{9,8},{10,11... | collective-permute-start | bytes 786440 | tf_op jit(solution)/shard_map/ppermute | solution.py:8
  96.1 1.5 collective-permute-done
  97.7 3.1 %collective-permute-start.1 = (f32[2,2,256,128]{3,2,0,1:T(8,128)S(1)}, f32[2,2,256,128]{3,2,0,1:T(8,128)S(1)}, u32[]{:S(2)}, u32[]{:S(2)}) collective-permute-start(f32[2,2,256,128]{3,2,0,1:T(8,128)S(1)} %maximum_select_fusion.2), channel_id=1, source_target_pairs={{0,2},{1,3},{2,0},{3,1},{4,6},{5,7},{6,4},{7,5},{8,10},{9,11},{10,... | collective-permute-start | bytes 1572872 | tf_op jit(solution)/shard_map/ppermute | solution.py:8
  100.8 27.5 %all-gather = bf16[2048,128]{1,0:T(8,128)(2,1)} all-gather(bf16[256,128]{1,0:T(8,128)(2,1)S(1)} %convolution_convert_fusion), channel_id=2, replica_groups=mesh['leaf'=8,'wide'=64] {'leaf'}, dimensions={0}, use_global_device_ids=true | all-gather | bytes 589824 | tf_op jit(solution)/shard_map/all_gather | solution.py:27
  128.4 1.0 copy-done.1
  129.6 2.8 %collective-permute-start.2 = (f32[2,1,256,128]{3,2,0,1:T(8,128)S(1)}, f32[2,1,256,128]{3,2,0,1:T(8,128)}, u32[]{:S(2)}, u32[]{:S(2)}) collective-permute-start(f32[2,1,256,128]{3,2,0,1:T(8,128)S(1)} %maximum_bitcast_fusion.1), channel_id=1, source_target_pairs={{0,4},{1,5},{2,6},{3,7},{4,0},{5,1},{6,2},{7,3},{8,12},{9,13},{10,... | collective-permute-start | bytes 786440 | tf_op jit(solution)/shard_map/ppermute | solution.py:8
  132.7 6.8 %collective-permute-done.2 = f32[2,1,256,128]{3,2,0,1:T(8,128)} collective-permute-done((f32[2,1,256,128]{3,2,0,1:T(8,128)S(1)}, f32[2,1,256,128]{3,2,0,1:T(8,128)}, u32[]{:S(2)}, u32[]{:S(2)}) %collective-permute-start.2) | collective-permute-done | bytes 262176 | tf_op jit(solution)/shard_map/ppermute | solution.py:8
  139.4 1.9 maximum_select_fusion.3
  141.3 2.4 %collective-permute-start.3 = (f32[2,2,256,128]{3,2,0,1:T(8,128)}, f32[2,2,256,128]{3,2,0,1:T(8,128)}, u32[]{:S(2)}, u32[]{:S(2)}) collective-permute-start(f32[2,2,256,128]{3,2,0,1:T(8,128)} %maximum_select_fusion.3), channel_id=1, source_target_pairs={{0,8},{1,9},{2,10},{3,11},{4,12},{5,13},{6,14},{7,15},{8,0},{9,1},... | collective-permute-start | bytes 1572872 | tf_op jit(solution)/shard_map/ppermute | solution.py:8
  143.8 1.0 convolution_bitcast_fusion.3
  144.8 1.7 fusion
  146.5 6.8 %collective-permute-done.3 = f32[2,2,256,128]{3,2,0,1:T(8,128)} collective-permute-done((f32[2,2,256,128]{3,2,0,1:T(8,128)}, f32[2,2,256,128]{3,2,0,1:T(8,128)}, u32[]{:S(2)}, u32[]{:S(2)}) %collective-permute-start.3) | collective-permute-done | bytes 524320 | tf_op jit(solution)/shard_map/ppermute | solution.py:8
  153.4 1.7 maximum_select_fusion.1
  155.1 2.6 %collective-permute-start.4 = (bf16[1,256,128]{2,1,0:T(8,128)(2,1)S(1)}, bf16[1,256,128]{2,1,0:T(8,128)(2,1)S(1)}, u32[]{:S(2)}, u32[]{:S(2)}) collective-permute-start(bf16[1,256,128]{2,1,0:T(8,128)(2,1)S(1)} %bitcast.93), channel_id=1, source_target_pairs={{0,16},{1,17},{2,18},{3,19},{4,20},{5,21},{6,22},{7,23},{8,24},{9,... | collective-permute-start | bytes 196616 | tf_op jit(solution)/shard_map/ppermute | solution.py:8
  158.0 7.5 %collective-permute-done.4 = bf16[1,256,128]{2,1,0:T(8,128)(2,1)S(1)} collective-permute-done((bf16[1,256,128]{2,1,0:T(8,128)(2,1)S(1)}, bf16[1,256,128]{2,1,0:T(8,128)(2,1)S(1)}, u32[]{:S(2)}, u32[]{:S(2)}) %collective-permute-start.4) | collective-permute-done | bytes 65568 | tf_op jit(solution)/shard_map/ppermute | solution.py:8
  165.5 1.9 %collective-permute-start.5 = (bf16[2,256,128]{2,1,0:T(8,128)(2,1)S(1)}, bf16[2,256,128]{2,1,0:T(8,128)(2,1)}, u32[]{:S(2)}, u32[]{:S(2)}) collective-permute-start(bf16[2,256,128]{2,1,0:T(8,128)(2,1)S(1)} %maximum_select_fusion.5), channel_id=1, source_target_pairs={{0,32},{1,33},{2,34},{3,35},{4,36},{5,37},{6,38},{7,39},{8,40},{9,... | collective-permute-start | bytes 393224 | tf_op jit(solution)/shard_map/ppermute | solution.py:8
  168.3 9.1 %collective-permute-done.5 = bf16[2,256,128]{2,1,0:T(8,128)(2,1)} collective-permute-done((bf16[2,256,128]{2,1,0:T(8,128)(2,1)S(1)}, bf16[2,256,128]{2,1,0:T(8,128)(2,1)}, u32[]{:S(2)}, u32[]{:S(2)}) %collective-permute-start.5) | collective-permute-done | bytes 131104 | tf_op jit(solution)/shard_map/ppermute | solution.py:8
  177.4 2.3 %fusion.4 = bf16[256,128]{1,0:T(8,128)(2,1)} fusion(f32[256,128]{1,0:T(8,128)} %convolution_bitcast_fusion.1, bf16[2,256,128]{2,1,0:T(8,128)(2,1)} %collective-permute-done.5, bf16[2,256,128]{2,1,0:T(8,128)(2,1)} %copy-done.7, pred[]{:T(512)S(6)} %eq.41, bf16[1,3,4,128,128]{4,3,2,1,0:T(8,128)(2,1)} %param.21, bf16[4]{0:T(256)(128)(2,1)S(1)} %compare_convert_fusion, ...), kind=kOutput, calls=%fused_computation.15 | convolution fusion | flops 42565632 | bytes 622601 | tf_op jit(solution)/shard_map/dot_general | solution.py:81
  179.7 1.9 fusion.6
  181.6 2.1 %fusion.2 = f32[1,1,256,1024]{3,2,1,0:T(8,128)} fusion(f32[256,1024]{1,0:T(8,128)S(1)} %fusion, bf16[256,128]{1,0:T(8,128)(2,1)} %fusion.6, bf16[1,1,128,1024]{3,2,1,0:T(8,128)(2,1)S(1)} %copy-done.4), kind=kOutput, calls=%fused_computation.3 | convolution fusion | flops 67371008 | bytes 2424832 | tf_op jit(solution)/shard_map/dot_general | solution.py:89
  (37 shorter events, 2.8 us)
Async XLA Ops:
  6.5 138.2 %copy-start = (bf16[1,1,1024,1024]{3,2,1,0:T(8,128)(2,1)S(1)}, bf16[1,1,1024,1024]{3,2,1,0:T(8,128)(2,1)}, u32[]{:S(2)}) copy-start(bf16[1,1,1024,1024]{3,2,1,0:T(8,128)(2,1)} %param.13) | copy-start | bytes 6291460
  6.5 85.7 %all-reduce.2.cloned.1.call-start = ((), (), s32[]{:S(2)}) async-start(), calls=%async_computation | async-start | bytes 262144 | tf_op jit(solution)/shard_map/psum | solution.py:28
  94.2 3.4 %collective-permute-start = (f32[2,1,256,128]{3,2,0,1:T(8,128)S(1)}, f32[2,1,256,128]{3,2,0,1:T(8,128)S(1)}, u32[]{:S(2)}, u32[]{:S(2)}) collective-permute-start(f32[2,1,256,128]{3,2,0,1:T(8,128)S(1)} %maximum_bitcast_fusion), channel_id=1, source_target_pairs={{0,1},{1,0},{2,3},{3,2},{4,5},{5,4},{6,7},{7,6},{8,9},{9,8},{10,11... | collective-permute-start | bytes 786440 | tf_op jit(solution)/shard_map/ppermute | solution.py:8
  96.1 33.3 %copy-start.8 = (bf16[1,2,128,128]{3,2,1,0:T(8,128)(2,1)S(1)}, bf16[1,2,128,128]{3,2,1,0:T(8,128)(2,1)}, u32[]{:S(2)}) copy-start(bf16[1,2,128,128]{3,2,1,0:T(8,128)(2,1)} %param.19) | copy-start | bytes 196612
  97.7 30.6 %collective-permute-start.1 = (f32[2,2,256,128]{3,2,0,1:T(8,128)S(1)}, f32[2,2,256,128]{3,2,0,1:T(8,128)S(1)}, u32[]{:S(2)}, u32[]{:S(2)}) collective-permute-start(f32[2,2,256,128]{3,2,0,1:T(8,128)S(1)} %maximum_select_fusion.2), channel_id=1, source_target_pairs={{0,2},{1,3},{2,0},{3,1},{4,6},{5,7},{6,4},{7,5},{8,10},{9,11},{10,... | collective-permute-start | bytes 1572872 | tf_op jit(solution)/shard_map/ppermute | solution.py:8
  100.8 31.6 %copy-start.5 = (bf16[1,1,8,128,128]{4,3,2,1,0:T(8,128)(2,1)S(1)}, bf16[1,1,8,128,128]{4,3,2,1,0:T(8,128)(2,1)}, u32[]{:S(2)}) copy-start(bf16[1,1,8,128,128]{4,3,2,1,0:T(8,128)(2,1)} %param.18) | copy-start | bytes 786436
  100.8 31.6 %copy-start.9 = (s32[1,8]{1,0:T(1,128)S(1)}, s32[1,8]{1,0:T(1,128)}, u32[]{:S(2)}) copy-start(s32[1,8]{1,0:T(1,128)} %param.12) | copy-start | bytes 100
  128.4 1.0 copy-start.1
  129.3 14.4 %copy-start.3 = (bf16[2048,128]{1,0:T(8,128)(2,1)S(1)}, bf16[2048,128]{1,0:T(8,128)(2,1)}, u32[]{:S(2)}) copy-start(bf16[2048,128]{1,0:T(8,128)(2,1)} %all-gather) | copy-start | bytes 1572868
  129.6 9.9 %collective-permute-start.2 = (f32[2,1,256,128]{3,2,0,1:T(8,128)S(1)}, f32[2,1,256,128]{3,2,0,1:T(8,128)}, u32[]{:S(2)}, u32[]{:S(2)}) collective-permute-start(f32[2,1,256,128]{3,2,0,1:T(8,128)S(1)} %maximum_bitcast_fusion.1), channel_id=1, source_target_pairs={{0,4},{1,5},{2,6},{3,7},{4,0},{5,1},{6,2},{7,3},{8,12},{9,13},{10,... | collective-permute-start | bytes 786440 | tf_op jit(solution)/shard_map/ppermute | solution.py:8
  141.3 12.1 %collective-permute-start.3 = (f32[2,2,256,128]{3,2,0,1:T(8,128)}, f32[2,2,256,128]{3,2,0,1:T(8,128)}, u32[]{:S(2)}, u32[]{:S(2)}) collective-permute-start(f32[2,2,256,128]{3,2,0,1:T(8,128)} %maximum_select_fusion.3), channel_id=1, source_target_pairs={{0,8},{1,9},{2,10},{3,11},{4,12},{5,13},{6,14},{7,15},{8,0},{9,1},... | collective-permute-start | bytes 1572872 | tf_op jit(solution)/shard_map/ppermute | solution.py:8
  146.5 11.2 %copy-start.2 = (f32[2,4,256,128]{3,2,0,1:T(8,128)S(1)}, f32[2,4,256,128]{3,2,0,1:T(8,128)}, u32[]{:S(2)}) copy-start(f32[2,4,256,128]{3,2,0,1:T(8,128)} %copy-done.1) | copy-start | bytes 3145732
  146.5 11.2 %copy-start.6 = (bf16[1,3,4,128,128]{4,3,2,1,0:T(8,128)(2,1)S(1)}, bf16[1,3,4,128,128]{4,3,2,1,0:T(8,128)(2,1)}, u32[]{:S(2)}) copy-start(bf16[1,3,4,128,128]{4,3,2,1,0:T(8,128)(2,1)} %param.21) | copy-start | bytes 1179652
  155.1 26.5 %copy-start.4 = (bf16[1,1,128,1024]{3,2,1,0:T(8,128)(2,1)S(1)}, bf16[1,1,128,1024]{3,2,1,0:T(8,128)(2,1)}, u32[]{:S(2)}) copy-start(bf16[1,1,128,1024]{3,2,1,0:T(8,128)(2,1)} %param.15) | copy-start | bytes 786436
  155.1 10.3 %collective-permute-start.4 = (bf16[1,256,128]{2,1,0:T(8,128)(2,1)S(1)}, bf16[1,256,128]{2,1,0:T(8,128)(2,1)S(1)}, u32[]{:S(2)}, u32[]{:S(2)}) collective-permute-start(bf16[1,256,128]{2,1,0:T(8,128)(2,1)S(1)} %bitcast.93), channel_id=1, source_target_pairs={{0,16},{1,17},{2,18},{3,19},{4,20},{5,21},{6,22},{7,23},{8,24},{9,... | collective-permute-start | bytes 196616 | tf_op jit(solution)/shard_map/ppermute | solution.py:8
  165.5 2.9 %copy-start.7 = (bf16[2,256,128]{2,1,0:T(8,128)(2,1)}, bf16[2,256,128]{2,1,0:T(8,128)(2,1)S(1)}, u32[]{:S(2)}) copy-start(bf16[2,256,128]{2,1,0:T(8,128)(2,1)S(1)} %maximum_select_fusion.5) | copy-start | bytes 393220
  165.5 11.9 %collective-permute-start.5 = (bf16[2,256,128]{2,1,0:T(8,128)(2,1)S(1)}, bf16[2,256,128]{2,1,0:T(8,128)(2,1)}, u32[]{:S(2)}, u32[]{:S(2)}) collective-permute-start(bf16[2,256,128]{2,1,0:T(8,128)(2,1)S(1)} %maximum_select_fusion.5), channel_id=1, source_target_pairs={{0,32},{1,33},{2,34},{3,35},{4,36},{5,37},{6,38},{7,39},{8,40},{9,... | collective-permute-start | bytes 393224 | tf_op jit(solution)/shard_map/ppermute | solution.py:8
Sparse Core Ops, SparseCore 0:
  9.8 82.3 all-reduce.1
where the time goes:
time: 191 us
  waiting for transfers between devices  114 us (60%)
  blocking collectives  27.5 us (14%)
  starting transfers between devices  14.7 us (8%)
  matrix products  14.7 us (8%)
  between operations  13.7 us (7%)
  other arithmetic  4.69 us (2%)
    psum x1, waiting for transfers between devices, shards(): current = lax.psum(lifted, 'leaf')  82.5 us
    ppermute x6, waiting for transfers between devices, from_partner(): lax.ppermute(x, axis, [(i, i ^ 1 << stride) for i in range(lax.axis_size(...  31.6 us
    all_gather x1, blocking collectives, shards(): lax.all_gather(coeff[None].astype(jnp.bfloat16), 'leaf', axis=0, tiled=True)  27.5 us
    ppermute x6, starting transfers between devices, from_partner(): lax.ppermute(x, axis, [(i, i ^ 1 << stride) for i in range(lax.axis_size(...  14.7 us
  transfers between devices with their start and end apart: 7, of which 6 were waited for; matrix products, arithmetic and copies ran while one was open for 2% of the time, Pallas kernels for 0%

commit v1 on v0

v1 whole, which is shorter than its diff:
```python
import jax
import jax.numpy as jnp
from jax import lax
from jax.experimental import pallas as pl
from jax.experimental.pallas import tpu as pltpu
from jax.sharding import PartitionSpec as P

BF = jnp.bfloat16
F32 = jnp.float32


def mm(a, b):
    return jnp.dot(a, b, preferred_element_type=F32)


def call(body, shapes, scalars, arrays, params=(), flops=10**6, grant=32, name=None):
    n_scalars, n_arrays, n_params, n_out = len(scalars), len(arrays), len(params), len(shapes)

    def kernel(*refs):
        inside = n_scalars + n_arrays
        held = refs[inside + n_params + n_out : inside + 2 * n_params + n_out]
        copies = []
        for k in range(n_params):
            copy = pltpu.make_async_copy(refs[inside + k], held[k], refs[-1].at[k])
            copy.start()
            copies.append(copy)

        def fetch(k):
            def get():
                copies[k].wait()
                return held[k]

            return get

        outs = refs[inside + n_params : inside + n_params + n_out]
        body(*refs[:inside], *[fetch(k) for k in range(n_params)], *outs)

    moved = sum(a.size * a.dtype.itemsize for a in (*arrays, *params))
    return pl.pallas_call(
        kernel,
        out_shape=[jax.ShapeDtypeStruct(s, t) for s, t in shapes],
        in_specs=[pl.BlockSpec(memory_space=pltpu.SMEM)] * n_scalars
        + [pl.BlockSpec(memory_space=pltpu.VMEM)] * n_arrays
        + [pl.BlockSpec(memory_space=pltpu.HBM)] * n_params,
        out_specs=[pl.BlockSpec(memory_space=pltpu.VMEM)] * n_out,
        scratch_shapes=[pltpu.VMEM(a.shape, a.dtype) for a in params]
        + [pltpu.SemaphoreType.DMA((max(n_params, 1),))],
        compiler_params=pltpu.CompilerParams(vmem_limit_bytes=grant * 2**20),
        cost_estimate=pl.CostEstimate(flops=flops, bytes_accessed=moved, transcendentals=0),
        name=name,
    )(*scalars, *arrays, *params)


def total_of(ref, start, count):
    total = ref[start].astype(F32)
    for k in range(1, count):
        total = total + ref[start + k].astype(F32)
    return total


def first_kernel(models, leaf_in, leaf_up, lifted_ref, skeleton_ref):
    skeleton = mm(models()[...], leaf_in()[...]).astype(BF)
    skeleton_ref[...] = skeleton
    lifted_ref[...] = mm(skeleton, leaf_up()[...]).astype(BF).reshape(lifted_ref.shape)


def hold_kernel(upper_up_ref, held_ref):
    held_ref[...] = upper_up_ref[...]


def up_kernel(wide_ref, parts_ref, up_ref, sent_ref):
    wide = wide_ref[0]
    own = total_of(parts_ref, 0, parts_ref.shape[0]).astype(BF)
    parent = mm(own, up_ref[0]).astype(BF)
    top = mm(parent, up_ref[1]).astype(BF)
    for k in range(sent_ref.shape[0]):
        sent_ref[k] = top
    for k in range(16):
        sent_ref[wide // 16 * 16 + k] = parent
    for k in range(4):
        sent_ref[wide // 4 * 4 + k] = own


def down_kernel(wide_ref, heard_ref, couple_ref, upper_down, far_ref):
    wide = wide_ref[0]
    sums = []
    for level in range(3):
        step = 4**level
        first = wide // (4 * step) * 4
        for s in range(4):
            block = total_of(heard_ref, (first + s) * step, step)
            block = jnp.where(first + s == wide // step, jnp.zeros_like(block), block)
            sums.append(block.astype(BF))
    down_ref = upper_down()

    def near(level):
        field = None
        for s in range(4):
            term = mm(sums[4 * level + s], couple_ref[level, s])
            field = term if field is None else field + term
        return field

    field = near(2)
    for level in (1, 0):
        field = near(level) + mm(field.astype(BF), down_ref[level])
    rounded = field.astype(BF)
    for k in range(far_ref.shape[0]):
        far_ref[k] = rounded


def pair_kernel(own_ref, next_ref, pair_ref):
    pair_ref[0] = own_ref[...]
    pair_ref[1] = next_ref[...]


def dense_kernel(models_ref, diag_ref, dense_ref):
    dense_ref[...] = mm(models_ref[...], diag_ref[...])


def local_kernel(
    leaf_ref,
    slot_ref,
    next_ref,
    five_ref,
    six_ref,
    two_ref,
    dense_ref,
    couple,
    leaf_down,
    leaf_out,
    base_ref,
    weight_ref,
):
    leaf = leaf_ref[0]
    couple_ref = couple()
    near = mm(next_ref[...], couple_ref[slot_ref[leaf ^ 1]])
    for step, pair_ref in ((5, five_ref), (6, six_ref), (2, two_ref)):
        for k in range(2):
            near = near + mm(pair_ref[k], couple_ref[slot_ref[leaf ^ step ^ k]])
    out = leaf_out()[...]
    base_ref[...] = dense_ref[...] + mm(near.astype(BF), out)
    weight_ref[...] = mm(leaf_down()[...], out).astype(BF)


def last_kernel(far_ref, base_ref, weight_ref, response_ref):
    m, r = far_ref.shape[0] * far_ref.shape[1], far_ref.shape[2]
    response_ref[...] = base_ref[...] + mm(far_ref[...].reshape(m, r), weight_ref[...])


def shards(
    models,
    leaf_slot,
    diag_blocks,
    leaf_in,
    leaf_out,
    leaf_up,
    leaf_down,
    leaf_couple,
    upper_up,
    upper_down,
    upper_couple,
):
    inputs = models[0, 0]
    m, length = inputs.shape
    r = leaf_in.shape[-1]
    n_leaf = lax.axis_size("leaf")
    n_wide = lax.axis_size("wide")
    cut = m // n_leaf
    wide = lax.axis_index("wide").astype(jnp.int32).reshape(1)
    leaf = lax.axis_index("leaf").astype(jnp.int32).reshape(1)


    def partner(x, step):
        return lax.ppermute(x, "leaf", [(k, k ^ step) for k in range(n_leaf)])

    lifted, skeleton = call(
        first_kernel,
        [((n_leaf, cut, r), BF), ((m, r), BF)],
        [],
        [],
        [inputs, leaf_in[0, 0], leaf_up[0, 0]],
        flops=2 * m * length * r,
        grant=58,
        name="first",
    )
    lifted, upper_up = lax.optimization_barrier((lifted, upper_up))
    parts = lax.all_to_all(lifted, "leaf", 0, 0, tiled=True)
    (ups,) = call(hold_kernel, [(upper_up.shape[1:], BF)], [], [upper_up[0]], name="hold")
    ups, skeleton = lax.optimization_barrier((ups, skeleton))
    following = partner(skeleton, 1)
    parts, following = lax.optimization_barrier((parts, following))
    (sent,) = call(
        up_kernel, [((n_wide, cut, r), BF)], [wide], [parts, ups], name="up"
    )
    sent, skeleton = lax.optimization_barrier((sent, skeleton))
    heard = lax.all_to_all(sent, "wide", 0, 0, tiled=True)
    (pair,) = call(pair_kernel, [((2, m, r), BF)], [], [skeleton, following], name="pair")
    two, six, five = [partner(pair, step) for step in (2, 6, 5)]
    (far,) = call(
        down_kernel,
        [((n_leaf, cut, r), BF)],
        [wide],
        [heard, upper_couple[0]],
        [upper_down[0]],
        name="down",
    )
    far = lax.all_to_all(far, "leaf", 0, 0, tiled=True)
    (dense,) = call(
        dense_kernel,
        [((m, length), F32)],
        [],
        [inputs, diag_blocks[0, 0]],
        flops=2 * m * length * length,
        name="dense",
    )
    base, weight = call(
        local_kernel,
        [((m, length), F32), ((r, length), BF)],
        [leaf, leaf_slot[0]],
        [following, five, six, two, dense],
        [leaf_couple[0, 0], leaf_down[0, 0], leaf_out[0, 0]],
        flops=2 * m * length * r,
        name="local",
    )
    (response,) = call(
        last_kernel,
        [((m, length), F32)],
        [],
        [far, base, weight],
        flops=2 * m * length * r,
        name="last",
    )
    return response[None, None]


def solution(mesh):
    placed = (
        P("wide", "leaf", None, None),
        P("wide", None),
        P("wide", "leaf", None, None),
        P("wide", "leaf", None, None),
        P("wide", "leaf", None, None),
        P("wide", "leaf", None, None),
        P("wide", "leaf", None, None),
        P("wide", "leaf", None, None, None),
        P("wide", None, None, None),
        P("wide", None, None, None),
        P("wide", None, None, None, None),
    )
    return jax.shard_map(
        shards, mesh=mesh, in_specs=placed, out_specs=P("wide", "leaf", None, None), check_vma=False
    )
```

time: 191 us -> 69.1 us (0.36)
  the two profiles are of different devices: /device:TPU:28 before, /device:TPU:16 now
where the time goes in v1:
time: 69.1 us; the launch traced here: 68.4 us
  starting transfers between devices  42.6 us (62%)
  waiting for transfers between devices  12.8 us (19%)
  Pallas kernels  8.06 us (12%)
  local copies, waits for them, and re-layouts  4.8 us (7%)
    ppermute x4, starting transfers between devices, partner(): return lax.ppermute(x, 'leaf', [(k, k ^ step) for k in range(n_leaf)])  15.6 us
    all_to_all x1, starting transfers between devices, shards(): heard = lax.all_to_all(sent, 'wide', 0, 0, tiled=True)  10.5 us
    all_to_all x1, starting transfers between devices, shards(): parts = lax.all_to_all(lifted, 'leaf', 0, 0, tiled=True)  10.3 us
    pallas_call x8, Pallas kernels, call(): pl.pallas_call(kernel, out_shape=[jax.ShapeDtypeStruct(s, t) for s, t in...  8.06 us
    all_to_all x1, starting transfers between devices, shards(): far = lax.all_to_all(far, 'leaf', 0, 0, tiled=True)  6.21 us
    all_to_all x1, waiting for transfers between devices, shards(): far = lax.all_to_all(far, 'leaf', 0, 0, tiled=True)  5.38 us
    unnamed x30, local copies, waits for them, and re-layouts  4.8 us
    all_to_all x1, waiting for transfers between devices, shards(): heard = lax.all_to_all(sent, 'wide', 0, 0, tiled=True)  3.82 us
  transfers between devices with their start and end apart: 7, of which 4 were waited for; matrix products, arithmetic and copies ran while one was open for 0% of the time, Pallas kernels for 6%

profile of v1, /device:TPU:16, one launch (start us, length us, event | category | flops | bytes accessed | tf_op | source)
XLA Modules:
  0.0 68.4 jit_solution(17332670028774872766)
XLA Ops:
  0.0 2.4 %first.1 = (bf16[8,32,128]{2,1,0:T(8,128)(2,1)}, bf16[256,128]{1,0:T(8,128)(2,1)}) custom-call(bf16[256,1024]{1,0:T(8,128)(2,1)} %bitcast.15, bf16[1024,128]{1,0:T(8,128)(2,1)} %bitcast.24, bf16[128,128]{1,0:T(8,128)(2,1)} %bitcast.25), custom_call_target="tpu_custom_call" | custom-call | flops 67108864 | bytes 819200 | tf_op jit(solution)/shard_map/first/pallas_call | solution.py:39
  2.4 10.3 %all-to-all-start = ((bf16[8,32,128]{2,1,0:T(8,128)(2,1)}), bf16[8,32,128]{2,1,0:T(8,128)(2,1)S(1)}, u32[]{:S(2)}, u32[]{:S(2)}) async-start(bf16[8,32,128]{2,1,0:T(8,128)(2,1)} %get-tuple-element.18), calls=%async_computation | async-start | bytes 131072 | tf_op jit(solution)/shard_map/all_to_all | solution.py:187
  12.7 0.8 %copy-done.10 = bf16[1,2,128,128]{3,2,1,0:T(8,128)(2,1)S(1)} copy-done((bf16[1,2,128,128]{3,2,1,0:T(8,128)(2,1)S(1)}, bf16[1,2,128,128]{3,2,1,0:T(8,128)(2,1)}, u32[]{:S(2)}) %copy-start.10) | copy-done | bytes 65560
  13.6 3.9 %collective-permute-start = (bf16[256,128]{1,0:T(8,128)(2,1)}, bf16[256,128]{1,0:T(8,128)(2,1)S(1)}, u32[]{:S(2)}, u32[]{:S(2)}) collective-permute-start(bf16[256,128]{1,0:T(8,128)(2,1)} %get-tuple-element.26.refs_0_), channel_id=1, source_target_pairs={{0,64},{64,0},{128,192},{192,128},{256,320},{320,256},{384,448},{4... | collective-permute-start | bytes 196616 | tf_op jit(solution)/shard_map/ppermute | solution.py:174
  17.5 2.4 %collective-permute-done.refs_1_.refs_2_ = bf16[256,128]{1,0:T(8,128)(2,1)S(1)} collective-permute-done((bf16[256,128]{1,0:T(8,128)(2,1)}, bf16[256,128]{1,0:T(8,128)(2,1)S(1)}, u32[]{:S(2)}, u32[]{:S(2)}) %collective-permute-start) | collective-permute-done | bytes 65568 | tf_op jit(solution)/shard_map/ppermute | solution.py:174
  20.0 1.1 %all-to-all-done.refs_1_ = bf16[8,32,128]{2,1,0:T(8,128)(2,1)S(1)} async-done(((bf16[8,32,128]{2,1,0:T(8,128)(2,1)}), bf16[8,32,128]{2,1,0:T(8,128)(2,1)S(1)}, u32[]{:S(2)}, u32[]{:S(2)}) %all-to-all-start) | async-done | bytes 65568 | tf_op jit(solution)/shard_map/all_to_all | solution.py:187
  21.1 0.3 up.1
  21.4 0.8 %copy-done.2 = bf16[64,32,128]{2,1,0:T(8,128)(2,1)} copy-done((bf16[64,32,128]{2,1,0:T(8,128)(2,1)}, bf16[64,32,128]{2,1,0:T(8,128)(2,1)S(1)}, u32[]{:S(2)}) %copy-start.2) | copy-done | bytes 524312
  22.2 10.5 %all-to-all-start.1 = ((bf16[64,32,128]{2,1,0:T(8,128)(2,1)}), bf16[64,32,128]{2,1,0:T(8,128)(2,1)S(1)}, u32[]{:S(2)}, u32[]{:S(2)}) async-start(bf16[64,32,128]{2,1,0:T(8,128)(2,1)} %copy-done.2), calls=%async_computation.1 | async-start | bytes 1048576 | tf_op jit(solution)/shard_map/all_to_all | solution.py:196
  32.7 0.8 %copy-done.7 = bf16[256,128]{1,0:T(8,128)(2,1)S(1)} copy-done((bf16[256,128]{1,0:T(8,128)(2,1)S(1)}, bf16[256,128]{1,0:T(8,128)(2,1)}, u32[]{:S(2)}) %copy-start.7) | copy-done | bytes 65560
  33.5 0.8 %copy-done.11 = bf16[256,128]{1,0:T(8,128)(2,1)S(1)} copy-done((bf16[256,128]{1,0:T(8,128)(2,1)S(1)}, bf16[256,128]{1,0:T(8,128)(2,1)}, u32[]{:S(2)}) %copy-start.11) | copy-done | bytes 65560
  34.4 0.7 pair.1
  35.0 3.7 %collective-permute-start.3 = (bf16[2,256,128]{2,1,0:T(8,128)(2,1)}, bf16[2,256,128]{2,1,0:T(8,128)(2,1)}, u32[]{:S(2)}, u32[]{:S(2)}) collective-permute-start(bf16[2,256,128]{2,1,0:T(8,128)(2,1)} %pair.1), channel_id=1, source_target_pairs={{0,128},{64,192},{128,0},{192,64},{256,384},{320,448},{384,256},{4... | collective-permute-start | bytes 393224 | tf_op jit(solution)/shard_map/ppermute | solution.py:174
  38.7 5.5 %collective-permute-start.2 = (bf16[2,256,128]{2,1,0:T(8,128)(2,1)}, bf16[2,256,128]{2,1,0:T(8,128)(2,1)}, u32[]{:S(2)}, u32[]{:S(2)}) collective-permute-start(bf16[2,256,128]{2,1,0:T(8,128)(2,1)} %pair.1), channel_id=1, source_target_pairs={{0,384},{64,448},{128,256},{192,320},{256,128},{320,192},{384,0},{... | collective-permute-start | bytes 393224 | tf_op jit(solution)/shard_map/ppermute | solution.py:174
  44.2 2.5 %collective-permute-start.1 = (bf16[2,256,128]{2,1,0:T(8,128)(2,1)}, bf16[2,256,128]{2,1,0:T(8,128)(2,1)}, u32[]{:S(2)}, u32[]{:S(2)}) collective-permute-start(bf16[2,256,128]{2,1,0:T(8,128)(2,1)} %pair.1), channel_id=1, source_target_pairs={{0,320},{64,256},{128,448},{192,384},{256,64},{320,0},{384,192},{4... | collective-permute-start | bytes 393224 | tf_op jit(solution)/shard_map/ppermute | solution.py:174
  46.7 3.8 %all-to-all-done.1.refs_1_ = bf16[64,32,128]{2,1,0:T(8,128)(2,1)S(1)} async-done(((bf16[64,32,128]{2,1,0:T(8,128)(2,1)}), bf16[64,32,128]{2,1,0:T(8,128)(2,1)S(1)}, u32[]{:S(2)}, u32[]{:S(2)}) %all-to-all-start.1) | async-done | bytes 524320 | tf_op jit(solution)/shard_map/all_to_all | solution.py:196
  50.5 0.8 %copy-done.12 = bf16[1,2,128,128]{3,2,1,0:T(8,128)(2,1)S(1)} copy-done((bf16[1,2,128,128]{3,2,1,0:T(8,128)(2,1)S(1)}, bf16[1,2,128,128]{3,2,1,0:T(8,128)(2,1)}, u32[]{:S(2)}) %copy-start.12) | copy-done | bytes 65560
  51.4 0.5 down.1
  51.9 0.6 copy-done.9
  52.6 6.2 %all-to-all-start.2 = ((bf16[8,32,128]{2,1,0:T(8,128)(2,1)}), bf16[8,32,128]{2,1,0:T(8,128)(2,1)S(1)}, u32[]{:S(2)}, u32[]{:S(2)}) async-start(bf16[8,32,128]{2,1,0:T(8,128)(2,1)} %copy-done.9), calls=%async_computation.2 | async-start | bytes 131072 | tf_op jit(solution)/shard_map/all_to_all | solution.py:207
  58.8 0.7 %dense.1.refs_6_ = f32[256,1024]{1,0:T(8,128)S(1)} custom-call(bf16[256,1024]{1,0:T(8,128)(2,1)S(1)} %bitcast.16, bf16[1024,1024]{1,0:T(8,128)(2,1)S(1)} %bitcast.14), custom_call_target="tpu_custom_call" | custom-call | flops 536870912 | bytes 2621440 | tf_op jit(solution)/shard_map/dense/pallas_call | solution.py:39
  59.6 2.2 %local.1 = (f32[256,1024]{1,0:T(8,128)S(1)}, bf16[128,1024]{1,0:T(8,128)(2,1)S(1)}) custom-call(s32[1]{0:T(128)} %bitcast.7.refs_0_, s32[8]{0:T(128)S(1)} %bitcast.23, bf16[256,128]{1,0:T(8,128)(2,1)S(1)} %copy-done.8, bf16[2,256,128]{2,1,0:T(8,128)(2,1)} %collective-permute-done.1.refs_3_, bf16[2,256,128]{2,1,0:T(8,128)(2,1)} %collective-permute-done.2.refs_4_, ...), custom_call_target="tpu_custom_call" | custom-call | flops 67108864 | bytes 2064384 | tf_op jit(solution)/shard_map/local/pallas_call | solution.py:39
  61.8 5.4 %all-to-all-done.2.refs_0_ = bf16[8,32,128]{2,1,0:T(8,128)(2,1)S(1)} async-done(((bf16[8,32,128]{2,1,0:T(8,128)(2,1)}), bf16[8,32,128]{2,1,0:T(8,128)(2,1)S(1)}, u32[]{:S(2)}, u32[]{:S(2)}) %all-to-all-start.2) | async-done | bytes 65568 | tf_op jit(solution)/shard_map/all_to_all | solution.py:207
  67.2 1.3 %last.1 = f32[256,1024]{1,0:T(8,128)} custom-call(bf16[8,32,128]{2,1,0:T(8,128)(2,1)S(1)} %all-to-all-done.2.refs_0_, f32[256,1024]{1,0:T(8,128)S(1)} %get-tuple-element.27.refs_1_, bf16[128,1024]{1,0:T(8,128)(2,1)S(1)} %get-tuple-element.28.refs_2_), custom_call_target="tpu_custom_call" | custom-call | flops 67108864 | bytes 1376256 | tf_op jit(solution)/shard_map/last/pallas_call | solution.py:39
  (28 shorter events, 0.1 us)
Async XLA Ops:
  0.0 50.5 %copy-start.3 = (bf16[1,3,4,128,128]{4,3,2,1,0:T(8,128)(2,1)S(1)}, bf16[1,3,4,128,128]{4,3,2,1,0:T(8,128)(2,1)}, u32[]{:S(2)}) copy-start(bf16[1,3,4,128,128]{4,3,2,1,0:T(8,128)(2,1)} %param.21) | copy-start | bytes 1179652
  0.0 58.8 %copy-start = (bf16[1,1,1024,1024]{3,2,1,0:T(8,128)(2,1)S(1)}, bf16[1,1,1024,1024]{3,2,1,0:T(8,128)(2,1)}, u32[]{:S(2)}) copy-start(bf16[1,1,1024,1024]{3,2,1,0:T(8,128)(2,1)} %param.13) | copy-start | bytes 6291460
  0.0 58.8 %copy-start.1 = (bf16[1,1,256,1024]{3,2,1,0:T(8,128)(2,1)S(1)}, bf16[1,1,256,1024]{3,2,1,0:T(8,128)(2,1)}, u32[]{:S(2)}) copy-start(bf16[1,1,256,1024]{3,2,1,0:T(8,128)(2,1)} %param.11) | copy-start | bytes 1572868
  2.4 18.7 %all-to-all-start = ((bf16[8,32,128]{2,1,0:T(8,128)(2,1)}), bf16[8,32,128]{2,1,0:T(8,128)(2,1)S(1)}, u32[]{:S(2)}, u32[]{:S(2)}) async-start(bf16[8,32,128]{2,1,0:T(8,128)(2,1)} %get-tuple-element.18), calls=%async_computation | async-start | bytes 131072 | tf_op jit(solution)/shard_map/all_to_all | solution.py:187
  12.7 0.8 %copy-start.10 = (bf16[1,2,128,128]{3,2,1,0:T(8,128)(2,1)S(1)}, bf16[1,2,128,128]{3,2,1,0:T(8,128)(2,1)}, u32[]{:S(2)}) copy-start(bf16[1,2,128,128]{3,2,1,0:T(8,128)(2,1)} %param.19) | copy-start | bytes 196612
  13.6 6.4 %collective-permute-start = (bf16[256,128]{1,0:T(8,128)(2,1)}, bf16[256,128]{1,0:T(8,128)(2,1)S(1)}, u32[]{:S(2)}, u32[]{:S(2)}) collective-permute-start(bf16[256,128]{1,0:T(8,128)(2,1)} %get-tuple-element.26.refs_0_), channel_id=1, source_target_pairs={{0,64},{64,0},{128,192},{192,128},{256,320},{320,256},{384,448},{4... | collective-permute-start | bytes 196616 | tf_op jit(solution)/shard_map/ppermute | solution.py:174
  20.0 2.3 %copy-start.6 = (bf16[256,128]{1,0:T(8,128)(2,1)}, bf16[256,128]{1,0:T(8,128)(2,1)S(1)}, u32[]{:S(2)}) copy-start(bf16[256,128]{1,0:T(8,128)(2,1)S(1)} %collective-permute-done.refs_1_.refs_2_) | copy-start | bytes 196612
  21.4 0.8 %copy-start.2 = (bf16[64,32,128]{2,1,0:T(8,128)(2,1)}, bf16[64,32,128]{2,1,0:T(8,128)(2,1)S(1)}, u32[]{:S(2)}) copy-start(bf16[64,32,128]{2,1,0:T(8,128)(2,1)S(1)} %up.1) | copy-start | bytes 1572868
  22.2 28.3 %all-to-all-start.1 = ((bf16[64,32,128]{2,1,0:T(8,128)(2,1)}), bf16[64,32,128]{2,1,0:T(8,128)(2,1)S(1)}, u32[]{:S(2)}, u32[]{:S(2)}) async-start(bf16[64,32,128]{2,1,0:T(8,128)(2,1)} %copy-done.2), calls=%async_computation.1 | async-start | bytes 1048576 | tf_op jit(solution)/shard_map/all_to_all | solution.py:196
  32.7 0.8 %copy-start.7 = (bf16[256,128]{1,0:T(8,128)(2,1)S(1)}, bf16[256,128]{1,0:T(8,128)(2,1)}, u32[]{:S(2)}) copy-start(bf16[256,128]{1,0:T(8,128)(2,1)} %copy-done.6) | copy-start | bytes 196612
  33.5 0.8 %copy-start.11 = (bf16[256,128]{1,0:T(8,128)(2,1)S(1)}, bf16[256,128]{1,0:T(8,128)(2,1)}, u32[]{:S(2)}) copy-start(bf16[256,128]{1,0:T(8,128)(2,1)} %get-tuple-element.26.refs_0_) | copy-start | bytes 196612
  35.0 24.5 %collective-permute-start.3 = (bf16[2,256,128]{2,1,0:T(8,128)(2,1)}, bf16[2,256,128]{2,1,0:T(8,128)(2,1)}, u32[]{:S(2)}, u32[]{:S(2)}) collective-permute-start(bf16[2,256,128]{2,1,0:T(8,128)(2,1)} %pair.1), channel_id=1, source_target_pairs={{0,128},{64,192},{128,0},{192,64},{256,384},{320,448},{384,256},{4... | collective-permute-start | bytes 393224 | tf_op jit(solution)/shard_map/ppermute | solution.py:174
  38.7 20.8 %collective-permute-start.2 = (bf16[2,256,128]{2,1,0:T(8,128)(2,1)}, bf16[2,256,128]{2,1,0:T(8,128)(2,1)}, u32[]{:S(2)}, u32[]{:S(2)}) collective-permute-start(bf16[2,256,128]{2,1,0:T(8,128)(2,1)} %pair.1), channel_id=1, source_target_pairs={{0,384},{64,448},{128,256},{192,320},{256,128},{320,192},{384,0},{... | collective-permute-start | bytes 393224 | tf_op jit(solution)/shard_map/ppermute | solution.py:174
  44.2 15.3 %collective-permute-start.1 = (bf16[2,256,128]{2,1,0:T(8,128)(2,1)}, bf16[2,256,128]{2,1,0:T(8,128)(2,1)}, u32[]{:S(2)}, u32[]{:S(2)}) collective-permute-start(bf16[2,256,128]{2,1,0:T(8,128)(2,1)} %pair.1), channel_id=1, source_target_pairs={{0,320},{64,256},{128,448},{192,384},{256,64},{320,0},{384,192},{4... | collective-permute-start | bytes 393224 | tf_op jit(solution)/shard_map/ppermute | solution.py:174
  50.5 0.8 %copy-start.12 = (bf16[1,2,128,128]{3,2,1,0:T(8,128)(2,1)S(1)}, bf16[1,2,128,128]{3,2,1,0:T(8,128)(2,1)}, u32[]{:S(2)}) copy-start(bf16[1,2,128,128]{3,2,1,0:T(8,128)(2,1)} %param.20) | copy-start | bytes 196612
  51.9 0.6 copy-start.9
  52.6 7.0 %copy-start.4 = (bf16[1,1,8,128,128]{4,3,2,1,0:T(8,128)(2,1)S(1)}, bf16[1,1,8,128,128]{4,3,2,1,0:T(8,128)(2,1)}, u32[]{:S(2)}) copy-start(bf16[1,1,8,128,128]{4,3,2,1,0:T(8,128)(2,1)} %param.18) | copy-start | bytes 786436
  52.6 7.0 %copy-start.5 = (bf16[1,1,128,1024]{3,2,1,0:T(8,128)(2,1)S(1)}, bf16[1,1,128,1024]{3,2,1,0:T(8,128)(2,1)}, u32[]{:S(2)}) copy-start(bf16[1,1,128,1024]{3,2,1,0:T(8,128)(2,1)} %param.15) | copy-start | bytes 786436
  52.6 7.0 %copy-start.8 = (bf16[256,128]{1,0:T(8,128)(2,1)S(1)}, bf16[256,128]{1,0:T(8,128)(2,1)}, u32[]{:S(2)}) copy-start(bf16[256,128]{1,0:T(8,128)(2,1)} %copy-done.6) | copy-start | bytes 196612
  52.6 7.0 %copy-start.13 = (bf16[1,1,128,128]{3,2,1,0:T(8,128)(2,1)S(1)}, bf16[1,1,128,128]{3,2,1,0:T(8,128)(2,1)}, u32[]{:S(2)}) copy-start(bf16[1,1,128,128]{3,2,1,0:T(8,128)(2,1)} %param.17) | copy-start | bytes 98308
  52.6 7.0 %copy-start.14 = (s32[1,8]{1,0:T(1,128)S(1)}, s32[1,8]{1,0:T(1,128)}, u32[]{:S(2)}) copy-start(s32[1,8]{1,0:T(1,128)} %param.12) | copy-start | bytes 100
  52.6 14.6 %all-to-all-start.2 = ((bf16[8,32,128]{2,1,0:T(8,128)(2,1)}), bf16[8,32,128]{2,1,0:T(8,128)(2,1)S(1)}, u32[]{:S(2)}, u32[]{:S(2)}) async-start(bf16[8,32,128]{2,1,0:T(8,128)(2,1)} %copy-done.9), calls=%async_computation.2 | async-start | bytes 131072 | tf_op jit(solution)/shard_map/all_to_all | solution.py:207

commit v2 on v1

--- a/solution.py
+++ b/solution.py
@@ -81,36 +81,30 @@
         sent_ref[wide // 4 * 4 + k] = own
 
 
-def down_kernel(wide_ref, heard_ref, couple_ref, upper_down, far_ref):
+def fold_kernel(couple_ref, upper_down, folded_ref):
+    down_ref = upper_down()
+    r = down_ref.shape[-1]
+    flat = (4 * r, r)
+    folded_ref[0] = couple_ref[0]
+    top = mm(couple_ref[2].reshape(flat), down_ref[1]).astype(BF)
+    folded_ref[2] = mm(top, down_ref[0]).astype(BF).reshape(4, r, r)
+    folded_ref[1] = mm(couple_ref[1].reshape(flat), down_ref[0]).astype(BF).reshape(4, r, r)
+
+
+def down_kernel(wide_ref, heard_ref, folded_ref, far_ref):
     wide = wide_ref[0]
-    sums = []
-    for level in range(3):
+    field = None
+    for level in (2, 1, 0):
         step = 4**level
         first = wide // (4 * step) * 4
         for s in range(4):
             block = total_of(heard_ref, (first + s) * step, step)
             block = jnp.where(first + s == wide // step, jnp.zeros_like(block), block)
-            sums.append(block.astype(BF))
-    down_ref = upper_down()
-
-    def near(level):
-        field = None
-        for s in range(4):
-            term = mm(sums[4 * level + s], couple_ref[level, s])
+            term = mm(block.astype(BF), folded_ref[level, s])
             field = term if field is None else field + term
-        return field
-
-    field = near(2)
-    for level in (1, 0):
-        field = near(level) + mm(field.astype(BF), down_ref[level])
     rounded = field.astype(BF)
     for k in range(far_ref.shape[0]):
         far_ref[k] = rounded
-
-
-def pair_kernel(own_ref, next_ref, pair_ref):
-    pair_ref[0] = own_ref[...]
-    pair_ref[1] = next_ref[...]
 
 
 def dense_kernel(models_ref, diag_ref, dense_ref):
@@ -142,9 +136,36 @@
     weight_ref[...] = mm(leaf_down()[...], out).astype(BF)
 
 
-def last_kernel(far_ref, base_ref, weight_ref, response_ref):
+def last_kernel(far_ref, base_ref, weight_ref, response_ref, held_ref, sems):
     m, r = far_ref.shape[0] * far_ref.shape[1], far_ref.shape[2]
-    response_ref[...] = base_ref[...] + mm(far_ref[...].reshape(m, r), weight_ref[...])
+    far = far_ref[...].reshape(m, r)
+    pieces = sems.shape[0]
+    size = m // pieces
+    copies = []
+    for k in range(pieces):
+        rows = slice(k * size, (k + 1) * size)
+        held_ref[rows] = base_ref[rows] + mm(far[rows], weight_ref[...])
+        copy = pltpu.make_async_copy(held_ref.at[rows], response_ref.at[rows], sems.at[k])
+        copy.start()
+        copies.append(copy)
+    for copy in copies:
+        copy.wait()
+
+
+def last_call(far, base, weight):
+    m, length = base.shape
+    return pl.pallas_call(
+        last_kernel,
+        out_shape=jax.ShapeDtypeStruct(base.shape, F32),
+        in_specs=[pl.BlockSpec(memory_space=pltpu.VMEM)] * 3,
+        out_specs=pl.BlockSpec(memory_space=pl.ANY),
+        scratch_shapes=[pltpu.VMEM(base.shape, F32), pltpu.SemaphoreType.DMA((4,))],
+        compiler_params=pltpu.CompilerParams(vmem_limit_bytes=32 * 2**20),
+        cost_estimate=pl.CostEstimate(
+            flops=2 * m * length * weight.shape[0], bytes_accessed=8 * m * length, transcendentals=0
+        ),
+        name="last",
+    )(far, base, weight)
 
 
 def shards(
@@ -192,17 +213,21 @@
     (sent,) = call(
         up_kernel, [((n_wide, cut, r), BF)], [wide], [parts, ups], name="up"
     )
-    sent, skeleton = lax.optimization_barrier((sent, skeleton))
+    sent, skeleton, upper_down = lax.optimization_barrier((sent, skeleton, upper_down))
     heard = lax.all_to_all(sent, "wide", 0, 0, tiled=True)
-    (pair,) = call(pair_kernel, [((2, m, r), BF)], [], [skeleton, following], name="pair")
+    pair = jnp.stack([skeleton, following])
     two, six, five = [partner(pair, step) for step in (2, 6, 5)]
+    (folded,) = call(
+        fold_kernel,
+        [(upper_couple.shape[1:], BF)],
+        [],
+        [upper_couple[0]],
+        [upper_down[0]],
+        flops=24 * r * r * r,
+        name="fold",
+    )
     (far,) = call(
-        down_kernel,
-        [((n_leaf, cut, r), BF)],
-        [wide],
-        [heard, upper_couple[0]],
-        [upper_down[0]],
-        name="down",
+        down_kernel, [((n_leaf, cut, r), BF)], [wide], [heard, folded], name="down"
     )
     far = lax.all_to_all(far, "leaf", 0, 0, tiled=True)
     (dense,) = call(
@@ -222,14 +247,7 @@
         flops=2 * m * length * r,
         name="local",
     )
-    (response,) = call(
-        last_kernel,
-        [((m, length), F32)],
-        [],
-        [far, base, weight],
-        flops=2 * m * length * r,
-        name="last",
-    )
+    response = last_call(far, base, weight)
     return response[None, None]
 
 

time: 69.1 us -> 67.9 us (0.983)
  other arithmetic: 0 us -> 1.49 us
  waiting for transfers between devices: 12.8 us -> 11.4 us
  Pallas kernels: 8.06 us -> 7.27 us
    pallas_call x8 -> x7, Pallas kernels: 8.06 us -> 6.09 us  [call(): pl.pallas_call(kernel, out_shape=[jax.ShapeDtypeStruct(s, t) for s, t in...]
    another operation x0 -> x1, other arithmetic: none -> 1.49 us  [shards(): pair = jnp.stack([skeleton, following])]
    all_to_all x1, waiting for transfers between devices: 3.82 us -> 2.43 us  [shards(): heard = lax.all_to_all(sent, 'wide', 0, 0, tiled=True)]
    pallas_call x0 -> x1, Pallas kernels: none -> 1.18 us  [last_call(): pl.pallas_call(last_kernel, out_shape=jax.ShapeDtypeStruct(base.shape, F3...]
    unnamed x30 -> x26, local copies, waits for them, and re-layouts: 4.8 us -> 4.12 us
  transfers between devices with their start and end apart: 7 -> 7, of which waited for: 4 -> 4; matrix products, arithmetic and copies ran while one was open for 0% -> 2% of each run, Pallas kernels for 6% -> 5%
where the time goes in v2:
time: 67.9 us; the launch traced here: 67.2 us
  starting transfers between devices  42.7 us (63%)
  waiting for transfers between devices  11.4 us (17%)
  Pallas kernels  7.27 us (11%)
  local copies, waits for them, and re-layouts  4.12 us (6%)
  other arithmetic  1.49 us (2%)
    ppermute x4, starting transfers between devices, partner(): return lax.ppermute(x, 'leaf', [(k, k ^ step) for k in range(n_leaf)])  15.6 us
    all_to_all x1, starting transfers between devices, shards(): parts = lax.all_to_all(lifted, 'leaf', 0, 0, tiled=True)  10.5 us
    all_to_all x1, starting transfers between devices, shards(): heard = lax.all_to_all(sent, 'wide', 0, 0, tiled=True)  10.5 us
    all_to_all x1, starting transfers between devices, shards(): far = lax.all_to_all(far, 'leaf', 0, 0, tiled=True)  6.2 us
    pallas_call x7, Pallas kernels, call(): pl.pallas_call(kernel, out_shape=[jax.ShapeDtypeStruct(s, t) for s, t in...  6.09 us
    all_to_all x1, waiting for transfers between devices, shards(): far = lax.all_to_all(far, 'leaf', 0, 0, tiled=True)  5.38 us
    unnamed x26, local copies, waits for them, and re-layouts  4.12 us
    ppermute x4, waiting for transfers between devices, partner(): return lax.ppermute(x, 'leaf', [(k, k ^ step) for k in range(n_leaf)])  2.44 us
  transfers between devices with their start and end apart: 7, of which 4 were waited for; matrix products, arithmetic and copies ran while one was open for 2% of the time, Pallas kernels for 5%

profile of v2, /device:TPU:16, one launch (start us, length us, event | category | flops | bytes accessed | tf_op | source)
XLA Modules:
  0.0 67.2 jit_solution(5632857480105428512)
XLA Ops:
  0.0 2.2 %first.1 = (bf16[8,32,128]{2,1,0:T(8,128)(2,1)}, bf16[256,128]{1,0:T(8,128)(2,1)}) custom-call(bf16[256,1024]{1,0:T(8,128)(2,1)} %bitcast.17, bf16[1024,128]{1,0:T(8,128)(2,1)} %bitcast.27, bf16[128,128]{1,0:T(8,128)(2,1)} %bitcast.29), custom_call_target="tpu_custom_call" | custom-call | flops 67108864 | bytes 819200 | tf_op jit(solution)/shard_map/first/pallas_call | solution.py:39
  2.3 10.5 %all-to-all-start = ((bf16[8,32,128]{2,1,0:T(8,128)(2,1)}), bf16[8,32,128]{2,1,0:T(8,128)(2,1)S(1)}, u32[]{:S(2)}, u32[]{:S(2)}) async-start(bf16[8,32,128]{2,1,0:T(8,128)(2,1)} %get-tuple-element.19), calls=%async_computation | async-start | bytes 131072 | tf_op jit(solution)/shard_map/all_to_all | solution.py:208
  12.7 0.8 %copy-done.9 = bf16[1,2,128,128]{3,2,1,0:T(8,128)(2,1)S(1)} copy-done((bf16[1,2,128,128]{3,2,1,0:T(8,128)(2,1)S(1)}, bf16[1,2,128,128]{3,2,1,0:T(8,128)(2,1)}, u32[]{:S(2)}) %copy-start.9) | copy-done | bytes 65560
  13.6 3.9 %collective-permute-start = (bf16[256,128]{1,0:T(8,128)(2,1)}, bf16[256,128]{1,0:T(8,128)(2,1)S(1)}, u32[]{:S(2)}, u32[]{:S(2)}) collective-permute-start(bf16[256,128]{1,0:T(8,128)(2,1)} %get-tuple-element.28), channel_id=1, source_target_pairs={{0,64},{64,0},{128,192},{192,128},{256,320},{320,256},{384,448},{4... | collective-permute-start | bytes 196616 | tf_op jit(solution)/shard_map/ppermute | solution.py:195
  17.5 2.4 %collective-permute-done.refs_2_ = bf16[256,128]{1,0:T(8,128)(2,1)S(1)} collective-permute-done((bf16[256,128]{1,0:T(8,128)(2,1)}, bf16[256,128]{1,0:T(8,128)(2,1)S(1)}, u32[]{:S(2)}, u32[]{:S(2)}) %collective-permute-start) | collective-permute-done | bytes 65568 | tf_op jit(solution)/shard_map/ppermute | solution.py:195
  20.0 1.1 %all-to-all-done.refs_1_ = bf16[8,32,128]{2,1,0:T(8,128)(2,1)S(1)} async-done(((bf16[8,32,128]{2,1,0:T(8,128)(2,1)}), bf16[8,32,128]{2,1,0:T(8,128)(2,1)S(1)}, u32[]{:S(2)}, u32[]{:S(2)}) %all-to-all-start) | async-done | bytes 65568 | tf_op jit(solution)/shard_map/all_to_all | solution.py:208
  21.1 0.3 up.1
  21.4 0.8 %copy-done.2 = bf16[64,32,128]{2,1,0:T(8,128)(2,1)} copy-done((bf16[64,32,128]{2,1,0:T(8,128)(2,1)}, bf16[64,32,128]{2,1,0:T(8,128)(2,1)S(1)}, u32[]{:S(2)}) %copy-start.2) | copy-done | bytes 524312
  22.2 10.5 %all-to-all-start.1 = ((bf16[64,32,128]{2,1,0:T(8,128)(2,1)}), bf16[64,32,128]{2,1,0:T(8,128)(2,1)S(1)}, u32[]{:S(2)}, u32[]{:S(2)}) async-start(bf16[64,32,128]{2,1,0:T(8,128)(2,1)} %copy-done.2), calls=%async_computation.1 | async-start | bytes 1048576 | tf_op jit(solution)/shard_map/all_to_all | solution.py:217
  32.7 1.5 %pad_maximum_fusion = bf16[2,256,128]{2,1,0:T(8,128)(2,1)} fusion(bf16[1,256,128]{2,1,0:T(8,128)(2,1)S(1)} %bitcast.22, bf16[1,256,128]{2,1,0:T(8,128)(2,1)} %bitcast.28), kind=kLoop, calls=%fused_computation | loop fusion | flops 65536 | bytes 262144 | tf_op jit(solution)/shard_map/stack | solution.py:218
  34.2 3.7 %collective-permute-start.3 = (bf16[2,256,128]{2,1,0:T(8,128)(2,1)}, bf16[2,256,128]{2,1,0:T(8,128)(2,1)}, u32[]{:S(2)}, u32[]{:S(2)}) collective-permute-start(bf16[2,256,128]{2,1,0:T(8,128)(2,1)} %pad_maximum_fusion), channel_id=1, source_target_pairs={{0,128},{64,192},{128,0},{192,64},{256,384},{320,448},{384,256},{4... | collective-permute-start | bytes 393224 | tf_op jit(solution)/shard_map/ppermute | solution.py:195
  37.9 5.5 %collective-permute-start.2 = (bf16[2,256,128]{2,1,0:T(8,128)(2,1)}, bf16[2,256,128]{2,1,0:T(8,128)(2,1)}, u32[]{:S(2)}, u32[]{:S(2)}) collective-permute-start(bf16[2,256,128]{2,1,0:T(8,128)(2,1)} %pad_maximum_fusion), channel_id=1, source_target_pairs={{0,384},{64,448},{128,256},{192,320},{256,128},{320,192},{384,0},{... | collective-permute-start | bytes 393224 | tf_op jit(solution)/shard_map/ppermute | solution.py:195
  43.3 2.5 %collective-permute-start.1 = (bf16[2,256,128]{2,1,0:T(8,128)(2,1)}, bf16[2,256,128]{2,1,0:T(8,128)(2,1)}, u32[]{:S(2)}, u32[]{:S(2)}) collective-permute-start(bf16[2,256,128]{2,1,0:T(8,128)(2,1)} %pad_maximum_fusion), channel_id=1, source_target_pairs={{0,320},{64,256},{128,448},{192,384},{256,64},{320,0},{384,192},{4... | collective-permute-start | bytes 393224 | tf_op jit(solution)/shard_map/ppermute | solution.py:195
  45.9 1.0 %copy-done.3 = bf16[1,3,4,128,128]{4,3,2,1,0:T(8,128)(2,1)S(1)} copy-done((bf16[1,3,4,128,128]{4,3,2,1,0:T(8,128)(2,1)S(1)}, bf16[1,3,4,128,128]{4,3,2,1,0:T(8,128)(2,1)}, u32[]{:S(2)}) %copy-start.3) | copy-done | bytes 393240
  46.8 0.8 %copy-done.10 = bf16[1,2,128,128]{3,2,1,0:T(8,128)(2,1)S(1)} copy-done((bf16[1,2,128,128]{3,2,1,0:T(8,128)(2,1)S(1)}, bf16[1,2,128,128]{3,2,1,0:T(8,128)(2,1)}, u32[]{:S(2)}) %copy-start.10) | copy-done | bytes 65560
  47.7 0.4 fold.1.refs_2_
  48.1 2.4 %all-to-all-done.1.refs_1_ = bf16[64,32,128]{2,1,0:T(8,128)(2,1)S(1)} async-done(((bf16[64,32,128]{2,1,0:T(8,128)(2,1)}), bf16[64,32,128]{2,1,0:T(8,128)(2,1)S(1)}, u32[]{:S(2)}, u32[]{:S(2)}) %all-to-all-start.1) | async-done | bytes 524320 | tf_op jit(solution)/shard_map/all_to_all | solution.py:217
  50.5 0.3 down.1
  50.8 0.6 copy-done.6
  51.4 6.2 %all-to-all-start.2 = ((bf16[8,32,128]{2,1,0:T(8,128)(2,1)}), bf16[8,32,128]{2,1,0:T(8,128)(2,1)S(1)}, u32[]{:S(2)}, u32[]{:S(2)}) async-start(bf16[8,32,128]{2,1,0:T(8,128)(2,1)} %copy-done.6), calls=%async_computation.2 | async-start | bytes 131072 | tf_op jit(solution)/shard_map/all_to_all | solution.py:232
  57.7 0.7 %dense.1.refs_6_ = f32[256,1024]{1,0:T(8,128)S(1)} custom-call(bf16[256,1024]{1,0:T(8,128)(2,1)S(1)} %bitcast.18, bf16[1024,1024]{1,0:T(8,128)(2,1)S(1)} %bitcast.16), custom_call_target="tpu_custom_call" | custom-call | flops 536870912 | bytes 2621440 | tf_op jit(solution)/shard_map/dense/pallas_call | solution.py:39
  58.5 2.2 %local.1 = (f32[256,1024]{1,0:T(8,128)S(1)}, bf16[128,1024]{1,0:T(8,128)(2,1)S(1)}) custom-call(s32[1]{0:T(128)} %bitcast.7.refs_0_, s32[8]{0:T(128)S(1)} %bitcast.26, bf16[256,128]{1,0:T(8,128)(2,1)S(1)} %copy-done.8, bf16[2,256,128]{2,1,0:T(8,128)(2,1)} %collective-permute-done.1.refs_3_, bf16[2,256,128]{2,1,0:T(8,128)(2,1)} %collective-permute-done.2.refs_4_, ...), custom_call_target="tpu_custom_call" | custom-call | flops 67108864 | bytes 2064384 | tf_op jit(solution)/shard_map/local/pallas_call | solution.py:39
  60.6 5.4 %all-to-all-done.2.far_ref = bf16[8,32,128]{2,1,0:T(8,128)(2,1)S(1)} async-done(((bf16[8,32,128]{2,1,0:T(8,128)(2,1)}), bf16[8,32,128]{2,1,0:T(8,128)(2,1)S(1)}, u32[]{:S(2)}, u32[]{:S(2)}) %all-to-all-start.2) | async-done | bytes 65568 | tf_op jit(solution)/shard_map/all_to_all | solution.py:232
  66.0 1.2 %last.1 = f32[256,1024]{1,0:T(8,128)} custom-call(bf16[8,32,128]{2,1,0:T(8,128)(2,1)S(1)} %all-to-all-done.2.far_ref, f32[256,1024]{1,0:T(8,128)S(1)} %get-tuple-element.29.base_ref, bf16[128,1024]{1,0:T(8,128)(2,1)S(1)} %get-tuple-element.30.weight_ref), custom_call_target="tpu_custom_call" | custom-call | flops 67108864 | bytes 2097152 | tf_op jit(solution)/shard_map/last/pallas_call | solution.py:157
  (25 shorter events, 0.1 us)
Async XLA Ops:
  2.2 55.4 %copy-start = (bf16[1,1,1024,1024]{3,2,1,0:T(8,128)(2,1)S(1)}, bf16[1,1,1024,1024]{3,2,1,0:T(8,128)(2,1)}, u32[]{:S(2)}) copy-start(bf16[1,1,1024,1024]{3,2,1,0:T(8,128)(2,1)} %param.13) | copy-start | bytes 6291460
  2.3 55.4 %copy-start.1 = (bf16[1,1,256,1024]{3,2,1,0:T(8,128)(2,1)S(1)}, bf16[1,1,256,1024]{3,2,1,0:T(8,128)(2,1)}, u32[]{:S(2)}) copy-start(bf16[1,1,256,1024]{3,2,1,0:T(8,128)(2,1)} %param.11) | copy-start | bytes 1572868
  2.3 18.8 %all-to-all-start = ((bf16[8,32,128]{2,1,0:T(8,128)(2,1)}), bf16[8,32,128]{2,1,0:T(8,128)(2,1)S(1)}, u32[]{:S(2)}, u32[]{:S(2)}) async-start(bf16[8,32,128]{2,1,0:T(8,128)(2,1)} %get-tuple-element.19), calls=%async_computation | async-start | bytes 131072 | tf_op jit(solution)/shard_map/all_to_all | solution.py:208
  12.7 0.8 %copy-start.9 = (bf16[1,2,128,128]{3,2,1,0:T(8,128)(2,1)S(1)}, bf16[1,2,128,128]{3,2,1,0:T(8,128)(2,1)}, u32[]{:S(2)}) copy-start(bf16[1,2,128,128]{3,2,1,0:T(8,128)(2,1)} %param.19) | copy-start | bytes 196612
  13.6 6.4 %collective-permute-start = (bf16[256,128]{1,0:T(8,128)(2,1)}, bf16[256,128]{1,0:T(8,128)(2,1)S(1)}, u32[]{:S(2)}, u32[]{:S(2)}) collective-permute-start(bf16[256,128]{1,0:T(8,128)(2,1)} %get-tuple-element.28), channel_id=1, source_target_pairs={{0,64},{64,0},{128,192},{192,128},{256,320},{320,256},{384,448},{4... | collective-permute-start | bytes 196616 | tf_op jit(solution)/shard_map/ppermute | solution.py:195
  20.0 25.9 %copy-start.7 = (bf16[256,128]{1,0:T(8,128)(2,1)}, bf16[256,128]{1,0:T(8,128)(2,1)S(1)}, u32[]{:S(2)}) copy-start(bf16[256,128]{1,0:T(8,128)(2,1)S(1)} %collective-permute-done.refs_2_) | copy-start | bytes 196612
  21.4 0.8 %copy-start.2 = (bf16[64,32,128]{2,1,0:T(8,128)(2,1)}, bf16[64,32,128]{2,1,0:T(8,128)(2,1)S(1)}, u32[]{:S(2)}) copy-start(bf16[64,32,128]{2,1,0:T(8,128)(2,1)S(1)} %up.1) | copy-start | bytes 1572868
  22.2 28.3 %all-to-all-start.1 = ((bf16[64,32,128]{2,1,0:T(8,128)(2,1)}), bf16[64,32,128]{2,1,0:T(8,128)(2,1)S(1)}, u32[]{:S(2)}, u32[]{:S(2)}) async-start(bf16[64,32,128]{2,1,0:T(8,128)(2,1)} %copy-done.2), calls=%async_computation.1 | async-start | bytes 1048576 | tf_op jit(solution)/shard_map/all_to_all | solution.py:217
  34.2 24.2 %collective-permute-start.3 = (bf16[2,256,128]{2,1,0:T(8,128)(2,1)}, bf16[2,256,128]{2,1,0:T(8,128)(2,1)}, u32[]{:S(2)}, u32[]{:S(2)}) collective-permute-start(bf16[2,256,128]{2,1,0:T(8,128)(2,1)} %pad_maximum_fusion), channel_id=1, source_target_pairs={{0,128},{64,192},{128,0},{192,64},{256,384},{320,448},{384,256},{4... | collective-permute-start | bytes 393224 | tf_op jit(solution)/shard_map/ppermute | solution.py:195
  37.9 20.5 %collective-permute-start.2 = (bf16[2,256,128]{2,1,0:T(8,128)(2,1)}, bf16[2,256,128]{2,1,0:T(8,128)(2,1)}, u32[]{:S(2)}, u32[]{:S(2)}) collective-permute-start(bf16[2,256,128]{2,1,0:T(8,128)(2,1)} %pad_maximum_fusion), channel_id=1, source_target_pairs={{0,384},{64,448},{128,256},{192,320},{256,128},{320,192},{384,0},{... | collective-permute-start | bytes 393224 | tf_op jit(solution)/shard_map/ppermute | solution.py:195
  43.3 15.1 %collective-permute-start.1 = (bf16[2,256,128]{2,1,0:T(8,128)(2,1)}, bf16[2,256,128]{2,1,0:T(8,128)(2,1)}, u32[]{:S(2)}, u32[]{:S(2)}) collective-permute-start(bf16[2,256,128]{2,1,0:T(8,128)(2,1)} %pad_maximum_fusion), channel_id=1, source_target_pairs={{0,320},{64,256},{128,448},{192,384},{256,64},{320,0},{384,192},{4... | collective-permute-start | bytes 393224 | tf_op jit(solution)/shard_map/ppermute | solution.py:195
  45.8 1.0 %copy-start.3 = (bf16[1,3,4,128,128]{4,3,2,1,0:T(8,128)(2,1)S(1)}, bf16[1,3,4,128,128]{4,3,2,1,0:T(8,128)(2,1)}, u32[]{:S(2)}) copy-start(bf16[1,3,4,128,128]{4,3,2,1,0:T(8,128)(2,1)} %param.21) | copy-start | bytes 1179652
  46.8 0.8 %copy-start.10 = (bf16[1,2,128,128]{3,2,1,0:T(8,128)(2,1)S(1)}, bf16[1,2,128,128]{3,2,1,0:T(8,128)(2,1)}, u32[]{:S(2)}) copy-start(bf16[1,2,128,128]{3,2,1,0:T(8,128)(2,1)} %param.20) | copy-start | bytes 196612
  50.8 0.6 copy-start.6
  51.4 7.0 %copy-start.4 = (bf16[1,1,8,128,128]{4,3,2,1,0:T(8,128)(2,1)S(1)}, bf16[1,1,8,128,128]{4,3,2,1,0:T(8,128)(2,1)}, u32[]{:S(2)}) copy-start(bf16[1,1,8,128,128]{4,3,2,1,0:T(8,128)(2,1)} %param.18) | copy-start | bytes 786436
  51.4 7.0 %copy-start.5 = (bf16[1,1,128,1024]{3,2,1,0:T(8,128)(2,1)S(1)}, bf16[1,1,128,1024]{3,2,1,0:T(8,128)(2,1)}, u32[]{:S(2)}) copy-start(bf16[1,1,128,1024]{3,2,1,0:T(8,128)(2,1)} %param.15) | copy-start | bytes 786436
  51.4 7.0 %copy-start.8 = (bf16[256,128]{1,0:T(8,128)(2,1)S(1)}, bf16[256,128]{1,0:T(8,128)(2,1)}, u32[]{:S(2)}) copy-start(bf16[256,128]{1,0:T(8,128)(2,1)} %copy-done.7) | copy-start | bytes 196612
  51.4 7.0 %copy-start.11 = (bf16[1,1,128,128]{3,2,1,0:T(8,128)(2,1)S(1)}, bf16[1,1,128,128]{3,2,1,0:T(8,128)(2,1)}, u32[]{:S(2)}) copy-start(bf16[1,1,128,128]{3,2,1,0:T(8,128)(2,1)} %param.17) | copy-start | bytes 98308
  51.4 7.0 %copy-start.12 = (s32[1,8]{1,0:T(1,128)S(1)}, s32[1,8]{1,0:T(1,128)}, u32[]{:S(2)}) copy-start(s32[1,8]{1,0:T(1,128)} %param.12) | copy-start | bytes 100
  51.4 14.6 %all-to-all-start.2 = ((bf16[8,32,128]{2,1,0:T(8,128)(2,1)}), bf16[8,32,128]{2,1,0:T(8,128)(2,1)S(1)}, u32[]{:S(2)}, u32[]{:S(2)}) async-start(bf16[8,32,128]{2,1,0:T(8,128)(2,1)} %copy-done.6), calls=%async_computation.2 | async-start | bytes 131072 | tf_op jit(solution)/shard_map/all_to_all | solution.py:232

commit v3 on v2

--- a/solution.py
+++ b/solution.py
@@ -204,19 +204,9 @@
         grant=58,
         name="first",
     )
-    lifted, upper_up = lax.optimization_barrier((lifted, upper_up))
+    lifted, upper_up, upper_down = lax.optimization_barrier((lifted, upper_up, upper_down))
     parts = lax.all_to_all(lifted, "leaf", 0, 0, tiled=True)
     (ups,) = call(hold_kernel, [(upper_up.shape[1:], BF)], [], [upper_up[0]], name="hold")
-    ups, skeleton = lax.optimization_barrier((ups, skeleton))
-    following = partner(skeleton, 1)
-    parts, following = lax.optimization_barrier((parts, following))
-    (sent,) = call(
-        up_kernel, [((n_wide, cut, r), BF)], [wide], [parts, ups], name="up"
-    )
-    sent, skeleton, upper_down = lax.optimization_barrier((sent, skeleton, upper_down))
-    heard = lax.all_to_all(sent, "wide", 0, 0, tiled=True)
-    pair = jnp.stack([skeleton, following])
-    two, six, five = [partner(pair, step) for step in (2, 6, 5)]
     (folded,) = call(
         fold_kernel,
         [(upper_couple.shape[1:], BF)],
@@ -226,6 +216,15 @@
         flops=24 * r * r * r,
         name="fold",
     )
+    ups, folded, skeleton = lax.optimization_barrier((ups, folded, skeleton))
+    following = partner(skeleton, 1)
+    (sent,) = call(
+        up_kernel, [((n_wide, cut, r), BF)], [wide], [parts, ups], name="up"
+    )
+    sent, skeleton = lax.optimization_barrier((sent, skeleton))
+    heard = lax.all_to_all(sent, "wide", 0, 0, tiled=True)
+    pair = jnp.stack([skeleton, following])
+    two, six, five = [partner(pair, step) for step in (2, 6, 5)]
     (far,) = call(
         down_kernel, [((n_leaf, cut, r), BF)], [wide], [heard, folded], name="down"
     )

time: 67.9 us -> 66.7 us (0.982)
  the two profiles are of different devices: /device:TPU:16 before, /device:TPU:2 now
where the time goes in v3:
time: 66.7 us; the launch traced here: 66 us
  starting transfers between devices  38.4 us (58%)
  waiting for transfers between devices  14.5 us (22%)
  Pallas kernels  7.28 us (11%)
  local copies, waits for them, and re-layouts  4.12 us (6%)
  other arithmetic  1.52 us (2%)
    ppermute x4, starting transfers between devices, partner(): return lax.ppermute(x, 'leaf', [(k, k ^ step) for k in range(n_leaf)])  13.8 us
    all_to_all x1, starting transfers between devices, shards(): heard = lax.all_to_all(sent, 'wide', 0, 0, tiled=True)  10.7 us
    all_to_all x1, starting transfers between devices, shards(): parts = lax.all_to_all(lifted, 'leaf', 0, 0, tiled=True)  10.5 us
    pallas_call x7, Pallas kernels, call(): pl.pallas_call(kernel, out_shape=[jax.ShapeDtypeStruct(s, t) for s, t in...  6.1 us
    all_to_all x1, waiting for transfers between devices, shards(): parts = lax.all_to_all(lifted, 'leaf', 0, 0, tiled=True)  5.27 us
    all_to_all x1, waiting for transfers between devices, shards(): far = lax.all_to_all(far, 'leaf', 0, 0, tiled=True)  4.96 us
    ppermute x4, waiting for transfers between devices, partner(): return lax.ppermute(x, 'leaf', [(k, k ^ step) for k in range(n_leaf)])  4.24 us
    unnamed x26, local copies, waits for them, and re-layouts  4.12 us
  transfers between devices with their start and end apart: 7, of which 4 were waited for; matrix products, arithmetic and copies ran while one was open for 2% of the time, Pallas kernels for 5%

profile of v3, /device:TPU:2, one launch (start us, length us, event | category | flops | bytes accessed | tf_op | source)
XLA Modules:
  0.0 66.0 jit_solution(8542177954045680688)
XLA Ops:
  0.0 2.2 %first.1 = (bf16[8,32,128]{2,1,0:T(8,128)(2,1)}, bf16[256,128]{1,0:T(8,128)(2,1)}) custom-call(bf16[256,1024]{1,0:T(8,128)(2,1)} %bitcast.17, bf16[1024,128]{1,0:T(8,128)(2,1)} %bitcast.27, bf16[128,128]{1,0:T(8,128)(2,1)} %bitcast.29), custom_call_target="tpu_custom_call" | custom-call | flops 67108864 | bytes 819200 | tf_op jit(solution)/shard_map/first/pallas_call | solution.py:39
  2.3 10.5 %all-to-all-start = ((bf16[8,32,128]{2,1,0:T(8,128)(2,1)}), bf16[8,32,128]{2,1,0:T(8,128)(2,1)S(1)}, u32[]{:S(2)}, u32[]{:S(2)}) async-start(bf16[8,32,128]{2,1,0:T(8,128)(2,1)} %get-tuple-element.18), calls=%async_computation | async-start | bytes 131072 | tf_op jit(solution)/shard_map/all_to_all | solution.py:208
  12.7 0.8 %copy-done.9 = bf16[1,2,128,128]{3,2,1,0:T(8,128)(2,1)S(1)} copy-done((bf16[1,2,128,128]{3,2,1,0:T(8,128)(2,1)S(1)}, bf16[1,2,128,128]{3,2,1,0:T(8,128)(2,1)}, u32[]{:S(2)}) %copy-start.9) | copy-done | bytes 65560
  13.6 1.0 %copy-done.3 = bf16[1,3,4,128,128]{4,3,2,1,0:T(8,128)(2,1)S(1)} copy-done((bf16[1,3,4,128,128]{4,3,2,1,0:T(8,128)(2,1)S(1)}, bf16[1,3,4,128,128]{4,3,2,1,0:T(8,128)(2,1)}, u32[]{:S(2)}) %copy-start.3) | copy-done | bytes 393240
  14.6 0.8 %copy-done.10 = bf16[1,2,128,128]{3,2,1,0:T(8,128)(2,1)S(1)} copy-done((bf16[1,2,128,128]{3,2,1,0:T(8,128)(2,1)S(1)}, bf16[1,2,128,128]{3,2,1,0:T(8,128)(2,1)}, u32[]{:S(2)}) %copy-start.10) | copy-done | bytes 65560
  15.4 0.4 fold.1.refs_2_
  15.8 5.3 %all-to-all-done.refs_1_ = bf16[8,32,128]{2,1,0:T(8,128)(2,1)S(1)} async-done(((bf16[8,32,128]{2,1,0:T(8,128)(2,1)}), bf16[8,32,128]{2,1,0:T(8,128)(2,1)S(1)}, u32[]{:S(2)}, u32[]{:S(2)}) %all-to-all-start) | async-done | bytes 65568 | tf_op jit(solution)/shard_map/all_to_all | solution.py:208
  21.1 0.3 up.1
  21.4 0.8 %copy-done.2 = bf16[64,32,128]{2,1,0:T(8,128)(2,1)} copy-done((bf16[64,32,128]{2,1,0:T(8,128)(2,1)}, bf16[64,32,128]{2,1,0:T(8,128)(2,1)S(1)}, u32[]{:S(2)}) %copy-start.2) | copy-done | bytes 524312
  22.2 10.7 %all-to-all-start.1 = ((bf16[64,32,128]{2,1,0:T(8,128)(2,1)}), bf16[64,32,128]{2,1,0:T(8,128)(2,1)S(1)}, u32[]{:S(2)}, u32[]{:S(2)}) async-start(bf16[64,32,128]{2,1,0:T(8,128)(2,1)} %copy-done.2), calls=%async_computation.1 | async-start | bytes 1048576 | tf_op jit(solution)/shard_map/all_to_all | solution.py:225
  32.9 2.5 %collective-permute-start = (bf16[256,128]{1,0:T(8,128)(2,1)}, bf16[256,128]{1,0:T(8,128)(2,1)S(1)}, u32[]{:S(2)}, u32[]{:S(2)}) collective-permute-start(bf16[256,128]{1,0:T(8,128)(2,1)} %get-tuple-element.26), channel_id=1, source_target_pairs={{0,64},{64,0},{128,192},{192,128},{256,320},{320,256},{384,448},{4... | collective-permute-start | bytes 196616 | tf_op jit(solution)/shard_map/ppermute | solution.py:195
  35.4 3.9 %collective-permute-done.refs_2_ = bf16[256,128]{1,0:T(8,128)(2,1)S(1)} collective-permute-done((bf16[256,128]{1,0:T(8,128)(2,1)}, bf16[256,128]{1,0:T(8,128)(2,1)S(1)}, u32[]{:S(2)}, u32[]{:S(2)}) %collective-permute-start) | collective-permute-done | bytes 65568 | tf_op jit(solution)/shard_map/ppermute | solution.py:195
  39.2 1.5 %pad_maximum_fusion = bf16[2,256,128]{2,1,0:T(8,128)(2,1)} fusion(bf16[1,256,128]{2,1,0:T(8,128)(2,1)S(1)} %bitcast.22, bf16[1,256,128]{2,1,0:T(8,128)(2,1)} %bitcast.28), kind=kLoop, calls=%fused_computation | loop fusion | flops 65536 | bytes 262144 | tf_op jit(solution)/shard_map/stack | solution.py:226
  40.8 2.4 %collective-permute-start.3 = (bf16[2,256,128]{2,1,0:T(8,128)(2,1)}, bf16[2,256,128]{2,1,0:T(8,128)(2,1)}, u32[]{:S(2)}, u32[]{:S(2)}) collective-permute-start(bf16[2,256,128]{2,1,0:T(8,128)(2,1)} %pad_maximum_fusion), channel_id=1, source_target_pairs={{0,128},{64,192},{128,0},{192,64},{256,384},{320,448},{384,256},{4... | collective-permute-start | bytes 393224 | tf_op jit(solution)/shard_map/ppermute | solution.py:195
  43.1 2.7 %collective-permute-start.2 = (bf16[2,256,128]{2,1,0:T(8,128)(2,1)}, bf16[2,256,128]{2,1,0:T(8,128)(2,1)}, u32[]{:S(2)}, u32[]{:S(2)}) collective-permute-start(bf16[2,256,128]{2,1,0:T(8,128)(2,1)} %pad_maximum_fusion), channel_id=1, source_target_pairs={{0,384},{64,448},{128,256},{192,320},{256,128},{320,192},{384,0},{... | collective-permute-start | bytes 393224 | tf_op jit(solution)/shard_map/ppermute | solution.py:195
  45.8 6.3 %collective-permute-start.1 = (bf16[2,256,128]{2,1,0:T(8,128)(2,1)}, bf16[2,256,128]{2,1,0:T(8,128)(2,1)}, u32[]{:S(2)}, u32[]{:S(2)}) collective-permute-start(bf16[2,256,128]{2,1,0:T(8,128)(2,1)} %pad_maximum_fusion), channel_id=1, source_target_pairs={{0,320},{64,256},{128,448},{192,384},{256,64},{320,0},{384,192},{4... | collective-permute-start | bytes 393224 | tf_op jit(solution)/shard_map/ppermute | solution.py:195
  52.1 0.3 down.1
  52.4 0.6 copy-done.6
  53.0 3.5 %all-to-all-start.2 = ((bf16[8,32,128]{2,1,0:T(8,128)(2,1)}), bf16[8,32,128]{2,1,0:T(8,128)(2,1)S(1)}, u32[]{:S(2)}, u32[]{:S(2)}) async-start(bf16[8,32,128]{2,1,0:T(8,128)(2,1)} %copy-done.6), calls=%async_computation.2 | async-start | bytes 131072 | tf_op jit(solution)/shard_map/all_to_all | solution.py:231
  56.6 0.7 %dense.1.refs_6_ = f32[256,1024]{1,0:T(8,128)S(1)} custom-call(bf16[256,1024]{1,0:T(8,128)(2,1)S(1)} %bitcast.18, bf16[1024,1024]{1,0:T(8,128)(2,1)S(1)} %bitcast.16), custom_call_target="tpu_custom_call" | custom-call | flops 536870912 | bytes 2621440 | tf_op jit(solution)/shard_map/dense/pallas_call | solution.py:39
  57.3 0.3 collective-permute-done.1.refs_3_
  57.7 2.2 %local.1 = (f32[256,1024]{1,0:T(8,128)S(1)}, bf16[128,1024]{1,0:T(8,128)(2,1)S(1)}) custom-call(s32[1]{0:T(128)} %bitcast.7.refs_0_, s32[8]{0:T(128)S(1)} %bitcast.26, bf16[256,128]{1,0:T(8,128)(2,1)S(1)} %copy-done.8, bf16[2,256,128]{2,1,0:T(8,128)(2,1)} %collective-permute-done.1.refs_3_, bf16[2,256,128]{2,1,0:T(8,128)(2,1)} %collective-permute-done.2.refs_4_, ...), custom_call_target="tpu_custom_call" | custom-call | flops 67108864 | bytes 2064384 | tf_op jit(solution)/shard_map/local/pallas_call | solution.py:39
  59.9 5.0 %all-to-all-done.2.far_ref = bf16[8,32,128]{2,1,0:T(8,128)(2,1)S(1)} async-done(((bf16[8,32,128]{2,1,0:T(8,128)(2,1)}), bf16[8,32,128]{2,1,0:T(8,128)(2,1)S(1)}, u32[]{:S(2)}, u32[]{:S(2)}) %all-to-all-start.2) | async-done | bytes 65568 | tf_op jit(solution)/shard_map/all_to_all | solution.py:231
  64.8 1.2 %last.1 = f32[256,1024]{1,0:T(8,128)} custom-call(bf16[8,32,128]{2,1,0:T(8,128)(2,1)S(1)} %all-to-all-done.2.far_ref, f32[256,1024]{1,0:T(8,128)S(1)} %get-tuple-element.27.base_ref, bf16[128,1024]{1,0:T(8,128)(2,1)S(1)} %get-tuple-element.28.weight_ref), custom_call_target="tpu_custom_call" | custom-call | flops 67108864 | bytes 2097152 | tf_op jit(solution)/shard_map/last/pallas_call | solution.py:157
  (25 shorter events, 0.1 us)
Async XLA Ops:
  2.2 54.3 %copy-start = (bf16[1,1,1024,1024]{3,2,1,0:T(8,128)(2,1)S(1)}, bf16[1,1,1024,1024]{3,2,1,0:T(8,128)(2,1)}, u32[]{:S(2)}) copy-start(bf16[1,1,1024,1024]{3,2,1,0:T(8,128)(2,1)} %param.13) | copy-start | bytes 6291460
  2.3 54.3 %copy-start.1 = (bf16[1,1,256,1024]{3,2,1,0:T(8,128)(2,1)S(1)}, bf16[1,1,256,1024]{3,2,1,0:T(8,128)(2,1)}, u32[]{:S(2)}) copy-start(bf16[1,1,256,1024]{3,2,1,0:T(8,128)(2,1)} %param.11) | copy-start | bytes 1572868
  2.3 18.8 %all-to-all-start = ((bf16[8,32,128]{2,1,0:T(8,128)(2,1)}), bf16[8,32,128]{2,1,0:T(8,128)(2,1)S(1)}, u32[]{:S(2)}, u32[]{:S(2)}) async-start(bf16[8,32,128]{2,1,0:T(8,128)(2,1)} %get-tuple-element.18), calls=%async_computation | async-start | bytes 131072 | tf_op jit(solution)/shard_map/all_to_all | solution.py:208
  12.7 0.8 %copy-start.9 = (bf16[1,2,128,128]{3,2,1,0:T(8,128)(2,1)S(1)}, bf16[1,2,128,128]{3,2,1,0:T(8,128)(2,1)}, u32[]{:S(2)}) copy-start(bf16[1,2,128,128]{3,2,1,0:T(8,128)(2,1)} %param.19) | copy-start | bytes 196612
  13.6 1.0 %copy-start.3 = (bf16[1,3,4,128,128]{4,3,2,1,0:T(8,128)(2,1)S(1)}, bf16[1,3,4,128,128]{4,3,2,1,0:T(8,128)(2,1)}, u32[]{:S(2)}) copy-start(bf16[1,3,4,128,128]{4,3,2,1,0:T(8,128)(2,1)} %param.21) | copy-start | bytes 1179652
  14.6 0.8 %copy-start.10 = (bf16[1,2,128,128]{3,2,1,0:T(8,128)(2,1)S(1)}, bf16[1,2,128,128]{3,2,1,0:T(8,128)(2,1)}, u32[]{:S(2)}) copy-start(bf16[1,2,128,128]{3,2,1,0:T(8,128)(2,1)} %param.20) | copy-start | bytes 196612
  21.4 0.8 %copy-start.2 = (bf16[64,32,128]{2,1,0:T(8,128)(2,1)}, bf16[64,32,128]{2,1,0:T(8,128)(2,1)S(1)}, u32[]{:S(2)}) copy-start(bf16[64,32,128]{2,1,0:T(8,128)(2,1)S(1)} %up.1) | copy-start | bytes 1572868
  22.2 29.9 %all-to-all-start.1 = ((bf16[64,32,128]{2,1,0:T(8,128)(2,1)}), bf16[64,32,128]{2,1,0:T(8,128)(2,1)S(1)}, u32[]{:S(2)}, u32[]{:S(2)}) async-start(bf16[64,32,128]{2,1,0:T(8,128)(2,1)} %copy-done.2), calls=%async_computation.1 | async-start | bytes 1048576 | tf_op jit(solution)/shard_map/all_to_all | solution.py:225
  32.9 6.4 %collective-permute-start = (bf16[256,128]{1,0:T(8,128)(2,1)}, bf16[256,128]{1,0:T(8,128)(2,1)S(1)}, u32[]{:S(2)}, u32[]{:S(2)}) collective-permute-start(bf16[256,128]{1,0:T(8,128)(2,1)} %get-tuple-element.26), channel_id=1, source_target_pairs={{0,64},{64,0},{128,192},{192,128},{256,320},{320,256},{384,448},{4... | collective-permute-start | bytes 196616 | tf_op jit(solution)/shard_map/ppermute | solution.py:195
  39.2 6.6 %copy-start.7 = (bf16[256,128]{1,0:T(8,128)(2,1)}, bf16[256,128]{1,0:T(8,128)(2,1)S(1)}, u32[]{:S(2)}) copy-start(bf16[256,128]{1,0:T(8,128)(2,1)S(1)} %collective-permute-done.refs_2_) | copy-start | bytes 196612
  40.8 16.5 %collective-permute-start.3 = (bf16[2,256,128]{2,1,0:T(8,128)(2,1)}, bf16[2,256,128]{2,1,0:T(8,128)(2,1)}, u32[]{:S(2)}, u32[]{:S(2)}) collective-permute-start(bf16[2,256,128]{2,1,0:T(8,128)(2,1)} %pad_maximum_fusion), channel_id=1, source_target_pairs={{0,128},{64,192},{128,0},{192,64},{256,384},{320,448},{384,256},{4... | collective-permute-start | bytes 393224 | tf_op jit(solution)/shard_map/ppermute | solution.py:195
  43.1 14.2 %collective-permute-start.2 = (bf16[2,256,128]{2,1,0:T(8,128)(2,1)}, bf16[2,256,128]{2,1,0:T(8,128)(2,1)}, u32[]{:S(2)}, u32[]{:S(2)}) collective-permute-start(bf16[2,256,128]{2,1,0:T(8,128)(2,1)} %pad_maximum_fusion), channel_id=1, source_target_pairs={{0,384},{64,448},{128,256},{192,320},{256,128},{320,192},{384,0},{... | collective-permute-start | bytes 393224 | tf_op jit(solution)/shard_map/ppermute | solution.py:195
  45.8 11.8 %collective-permute-start.1 = (bf16[2,256,128]{2,1,0:T(8,128)(2,1)}, bf16[2,256,128]{2,1,0:T(8,128)(2,1)}, u32[]{:S(2)}, u32[]{:S(2)}) collective-permute-start(bf16[2,256,128]{2,1,0:T(8,128)(2,1)} %pad_maximum_fusion), channel_id=1, source_target_pairs={{0,320},{64,256},{128,448},{192,384},{256,64},{320,0},{384,192},{4... | collective-permute-start | bytes 393224 | tf_op jit(solution)/shard_map/ppermute | solution.py:195
  52.4 0.6 copy-start.6
  53.0 4.7 %copy-start.4 = (bf16[1,1,8,128,128]{4,3,2,1,0:T(8,128)(2,1)S(1)}, bf16[1,1,8,128,128]{4,3,2,1,0:T(8,128)(2,1)}, u32[]{:S(2)}) copy-start(bf16[1,1,8,128,128]{4,3,2,1,0:T(8,128)(2,1)} %param.18) | copy-start | bytes 786436
  53.0 4.7 %copy-start.5 = (bf16[1,1,128,1024]{3,2,1,0:T(8,128)(2,1)S(1)}, bf16[1,1,128,1024]{3,2,1,0:T(8,128)(2,1)}, u32[]{:S(2)}) copy-start(bf16[1,1,128,1024]{3,2,1,0:T(8,128)(2,1)} %param.15) | copy-start | bytes 786436
  53.0 4.7 %copy-start.8 = (bf16[256,128]{1,0:T(8,128)(2,1)S(1)}, bf16[256,128]{1,0:T(8,128)(2,1)}, u32[]{:S(2)}) copy-start(bf16[256,128]{1,0:T(8,128)(2,1)} %copy-done.7) | copy-start | bytes 196612
  53.0 4.7 %copy-start.11 = (bf16[1,1,128,128]{3,2,1,0:T(8,128)(2,1)S(1)}, bf16[1,1,128,128]{3,2,1,0:T(8,128)(2,1)}, u32[]{:S(2)}) copy-start(bf16[1,1,128,128]{3,2,1,0:T(8,128)(2,1)} %param.17) | copy-start | bytes 98308
  53.0 4.7 %copy-start.12 = (s32[1,8]{1,0:T(1,128)S(1)}, s32[1,8]{1,0:T(1,128)}, u32[]{:S(2)}) copy-start(s32[1,8]{1,0:T(1,128)} %param.12) | copy-start | bytes 100
  53.0 11.8 %all-to-all-start.2 = ((bf16[8,32,128]{2,1,0:T(8,128)(2,1)}), bf16[8,32,128]{2,1,0:T(8,128)(2,1)S(1)}, u32[]{:S(2)}, u32[]{:S(2)}) async-start(bf16[8,32,128]{2,1,0:T(8,128)(2,1)} %copy-done.6), calls=%async_computation.2 | async-start | bytes 131072 | tf_op jit(solution)/shard_map/all_to_all | solution.py:231

commit v4 on v2

--- a/solution.py
+++ b/solution.py
@@ -58,10 +58,64 @@
     return total
 
 
-def first_kernel(models, leaf_in, leaf_up, lifted_ref, skeleton_ref):
-    skeleton = mm(models()[...], leaf_in()[...]).astype(BF)
+def first_kernel(models_ref, in_ref, up_ref, lifted_ref, skeleton_ref, models, leaf_in, up, sems):
+    half = models.shape[1] // 2
+    copies = []
+    for k in range(2):
+        cut = pl.ds(k * half, half)
+        copies.append(
+            pltpu.make_async_copy(models_ref.at[:, cut], models.at[:, cut], sems.at[2 * k])
+        )
+        copies.append(pltpu.make_async_copy(in_ref.at[cut], leaf_in.at[cut], sems.at[2 * k + 1]))
+    copies.append(pltpu.make_async_copy(up_ref, up, sems.at[4]))
+    for copy in copies:
+        copy.start()
+    coeff = None
+    for k in range(2):
+        cut = pl.ds(k * half, half)
+        copies[2 * k].wait()
+        copies[2 * k + 1].wait()
+        term = mm(models[:, cut], leaf_in[cut])
+        coeff = term if coeff is None else coeff + term
+    skeleton = coeff.astype(BF)
     skeleton_ref[...] = skeleton
-    lifted_ref[...] = mm(skeleton, leaf_up()[...]).astype(BF).reshape(lifted_ref.shape)
+    copies[4].wait()
+    lifted_ref[...] = mm(skeleton, up[...]).astype(BF).reshape(lifted_ref.shape)
+
+
+def first_call(models, leaf_in, leaf_up, n_leaf):
+    m, length = models.shape
+    r = leaf_in.shape[1]
+    return pl.pallas_call(
+        first_kernel,
+        out_shape=[
+            jax.ShapeDtypeStruct((n_leaf, m // n_leaf, r), BF),
+            jax.ShapeDtypeStruct((m, r), BF),
+        ],
+        in_specs=[pl.BlockSpec(memory_space=pl.ANY)] * 3,
+        out_specs=[pl.BlockSpec(memory_space=pltpu.VMEM)] * 2,
+        scratch_shapes=[pltpu.VMEM(a.shape, BF) for a in (models, leaf_in, leaf_up)]
+        + [pltpu.SemaphoreType.DMA((5,))],
+        compiler_params=pltpu.CompilerParams(vmem_limit_bytes=58 * 2**20),
+        cost_estimate=pl.CostEstimate(
+            flops=2 * m * length * r, bytes_accessed=2 * m * length, transcendentals=0
+        ),
+        name="first",
+    )(models, leaf_in, leaf_up)
+
+
+def step_kernel(leaf_ref, same_ref):
+    same_ref[0] = leaf_ref[0]
+
+
+def step_call(leaf):
+    return pl.pallas_call(
+        step_kernel,
+        out_shape=jax.ShapeDtypeStruct(leaf.shape, leaf.dtype),
+        in_specs=[pl.BlockSpec(memory_space=pltpu.SMEM)],
+        out_specs=pl.BlockSpec(memory_space=pltpu.SMEM),
+        name="step",
+    )(leaf)
 
 
 def hold_kernel(upper_up_ref, held_ref):
@@ -194,26 +248,18 @@
     def partner(x, step):
         return lax.ppermute(x, "leaf", [(k, k ^ step) for k in range(n_leaf)])
 
-    lifted, skeleton = call(
-        first_kernel,
-        [((n_leaf, cut, r), BF), ((m, r), BF)],
-        [],
-        [],
-        [inputs, leaf_in[0, 0], leaf_up[0, 0]],
-        flops=2 * m * length * r,
-        grant=58,
-        name="first",
-    )
-    lifted, upper_up = lax.optimization_barrier((lifted, upper_up))
+    lifted, skeleton = first_call(inputs, leaf_in[0, 0], leaf_up[0, 0], n_leaf)
+    lifted, upper_up, leaf = lax.optimization_barrier((lifted, upper_up, leaf))
     parts = lax.all_to_all(lifted, "leaf", 0, 0, tiled=True)
+    leaf, skeleton = lax.optimization_barrier((step_call(leaf), skeleton))
+    following = partner(skeleton, 1)
     (ups,) = call(hold_kernel, [(upper_up.shape[1:], BF)], [], [upper_up[0]], name="hold")
-    ups, skeleton = lax.optimization_barrier((ups, skeleton))
-    following = partner(skeleton, 1)
-    parts, following = lax.optimization_barrier((parts, following))
     (sent,) = call(
         up_kernel, [((n_wide, cut, r), BF)], [wide], [parts, ups], name="up"
     )
-    sent, skeleton, upper_down = lax.optimization_barrier((sent, skeleton, upper_down))
+    sent, skeleton, following, upper_down = lax.optimization_barrier(
+        (sent, skeleton, following, upper_down)
+    )
     heard = lax.all_to_all(sent, "wide", 0, 0, tiled=True)
     pair = jnp.stack([skeleton, following])
     two, six, five = [partner(pair, step) for step in (2, 6, 5)]

time: 67.9 us -> 66.5 us (0.979)
  starting transfers between devices: 42.7 us -> 40.9 us
  Pallas kernels: 7.27 us -> 8.37 us
  waiting for transfers between devices: 11.4 us -> 10.6 us
    pallas_call x0 -> x2, Pallas kernels: none -> 2.78 us  [the longest x1 2.27 us: first_call(): pl.pallas_call(first_kernel, out_shape=[jax.ShapeDtypeStruct((n_leaf, m /...]
    ppermute x4, waiting for transfers between devices: 2.44 us -> 0.01 us  [partner(): return lax.ppermute(x, 'leaf', [(k, k ^ step) for k in range(n_leaf)])]
    all_to_all x1, waiting for transfers between devices: 1.14 us -> 3.05 us  [shards(): parts = lax.all_to_all(lifted, 'leaf', 0, 0, tiled=True)]
    pallas_call x7 -> x6, Pallas kernels: 6.09 us -> 4.4 us  [call(): pl.pallas_call(kernel, out_shape=[jax.ShapeDtypeStruct(s, t) for s, t in...]
    all_to_all x1, starting transfers between devices: 6.2 us -> 4.76 us  [shards(): far = lax.all_to_all(far, 'leaf', 0, 0, tiled=True)]
  transfers between devices with their start and end apart: 7 -> 7, of which waited for: 4 -> 3; matrix products, arithmetic and copies ran while one was open for 2% -> 2% of each run, Pallas kernels for 5% -> 7%
where the time goes in v4:
time: 66.5 us; the launch traced here: 65.8 us
  starting transfers between devices  40.9 us (62%)
  waiting for transfers between devices  10.6 us (16%)
  Pallas kernels  8.37 us (13%)
  local copies, waits for them, and re-layouts  4.11 us (6%)
  other arithmetic  1.52 us (2%)
    ppermute x4, starting transfers between devices, partner(): return lax.ppermute(x, 'leaf', [(k, k ^ step) for k in range(n_leaf)])  15.2 us
    all_to_all x1, starting transfers between devices, shards(): parts = lax.all_to_all(lifted, 'leaf', 0, 0, tiled=True)  10.5 us
    all_to_all x1, starting transfers between devices, shards(): heard = lax.all_to_all(sent, 'wide', 0, 0, tiled=True)  10.5 us
    all_to_all x1, waiting for transfers between devices, shards(): far = lax.all_to_all(far, 'leaf', 0, 0, tiled=True)  4.83 us
    all_to_all x1, starting transfers between devices, shards(): far = lax.all_to_all(far, 'leaf', 0, 0, tiled=True)  4.76 us
    pallas_call x6, Pallas kernels, call(): pl.pallas_call(kernel, out_shape=[jax.ShapeDtypeStruct(s, t) for s, t in...  4.4 us
    unnamed x26, local copies, waits for them, and re-layouts  4.11 us
    all_to_all x1, waiting for transfers between devices, shards(): parts = lax.all_to_all(lifted, 'leaf', 0, 0, tiled=True)  3.05 us
  transfers between devices with their start and end apart: 7, of which 3 were waited for; matrix products, arithmetic and copies ran while one was open for 2% of the time, Pallas kernels for 7%

profile of v4, /device:TPU:16, one launch (start us, length us, event | category | flops | bytes accessed | tf_op | source)
XLA Modules:
  0.0 65.8 jit_solution(4978640021770959653)
XLA Ops:
  0.0 2.3 %first.1 = (bf16[8,32,128]{2,1,0:T(8,128)(2,1)}, bf16[256,128]{1,0:T(8,128)(2,1)}) custom-call(bf16[256,1024]{1,0:T(8,128)(2,1)} %bitcast.17, bf16[1024,128]{1,0:T(8,128)(2,1)} %bitcast.27, bf16[128,128]{1,0:T(8,128)(2,1)} %bitcast.29), custom_call_target="tpu_custom_call" | custom-call | flops 67108864 | bytes 524288 | tf_op jit(solution)/shard_map/first/pallas_call | solution.py:89
  2.3 10.5 %all-to-all-start = ((bf16[8,32,128]{2,1,0:T(8,128)(2,1)}), bf16[8,32,128]{2,1,0:T(8,128)(2,1)S(1)}, u32[]{:S(2)}, u32[]{:S(2)}) async-start(bf16[8,32,128]{2,1,0:T(8,128)(2,1)} %get-tuple-element.19), calls=%async_computation | async-start | bytes 131072 | tf_op jit(solution)/shard_map/all_to_all | solution.py:253
  12.8 0.5 step.1.refs_0_
  13.3 3.9 %collective-permute-start = (bf16[256,128]{1,0:T(8,128)(2,1)}, bf16[256,128]{1,0:T(8,128)(2,1)S(1)}, u32[]{:S(2)}, u32[]{:S(2)}) collective-permute-start(bf16[256,128]{1,0:T(8,128)(2,1)} %get-tuple-element.28), channel_id=1, source_target_pairs={{0,64},{64,0},{128,192},{192,128},{256,320},{320,256},{384,448},{4... | collective-permute-start | bytes 196616 | tf_op jit(solution)/shard_map/ppermute | solution.py:249
  17.2 0.8 %copy-done.9 = bf16[1,2,128,128]{3,2,1,0:T(8,128)(2,1)S(1)} copy-done((bf16[1,2,128,128]{3,2,1,0:T(8,128)(2,1)S(1)}, bf16[1,2,128,128]{3,2,1,0:T(8,128)(2,1)}, u32[]{:S(2)}) %copy-start.9) | copy-done | bytes 65560
  18.1 3.1 %all-to-all-done.refs_1_ = bf16[8,32,128]{2,1,0:T(8,128)(2,1)S(1)} async-done(((bf16[8,32,128]{2,1,0:T(8,128)(2,1)}), bf16[8,32,128]{2,1,0:T(8,128)(2,1)S(1)}, u32[]{:S(2)}, u32[]{:S(2)}) %all-to-all-start) | async-done | bytes 65568 | tf_op jit(solution)/shard_map/all_to_all | solution.py:253
  21.1 0.3 up.1
  21.5 0.8 %copy-done.2 = bf16[64,32,128]{2,1,0:T(8,128)(2,1)} copy-done((bf16[64,32,128]{2,1,0:T(8,128)(2,1)}, bf16[64,32,128]{2,1,0:T(8,128)(2,1)S(1)}, u32[]{:S(2)}) %copy-start.2) | copy-done | bytes 524312
  22.3 10.5 %all-to-all-start.1 = ((bf16[64,32,128]{2,1,0:T(8,128)(2,1)}), bf16[64,32,128]{2,1,0:T(8,128)(2,1)S(1)}, u32[]{:S(2)}, u32[]{:S(2)}) async-start(bf16[64,32,128]{2,1,0:T(8,128)(2,1)} %copy-done.2), calls=%async_computation.1 | async-start | bytes 1048576 | tf_op jit(solution)/shard_map/all_to_all | solution.py:263
  32.7 1.5 %pad_maximum_fusion = bf16[2,256,128]{2,1,0:T(8,128)(2,1)} fusion(bf16[1,256,128]{2,1,0:T(8,128)(2,1)S(1)} %bitcast.22, bf16[1,256,128]{2,1,0:T(8,128)(2,1)} %bitcast.28), kind=kLoop, calls=%fused_computation | loop fusion | flops 65536 | bytes 262144 | tf_op jit(solution)/shard_map/stack | solution.py:264
  34.2 2.4 %collective-permute-start.3 = (bf16[2,256,128]{2,1,0:T(8,128)(2,1)}, bf16[2,256,128]{2,1,0:T(8,128)(2,1)}, u32[]{:S(2)}, u32[]{:S(2)}) collective-permute-start(bf16[2,256,128]{2,1,0:T(8,128)(2,1)} %pad_maximum_fusion), channel_id=1, source_target_pairs={{0,128},{64,192},{128,0},{192,64},{256,384},{320,448},{384,256},{4... | collective-permute-start | bytes 393224 | tf_op jit(solution)/shard_map/ppermute | solution.py:249
  36.6 5.3 %collective-permute-start.2 = (bf16[2,256,128]{2,1,0:T(8,128)(2,1)}, bf16[2,256,128]{2,1,0:T(8,128)(2,1)}, u32[]{:S(2)}, u32[]{:S(2)}) collective-permute-start(bf16[2,256,128]{2,1,0:T(8,128)(2,1)} %pad_maximum_fusion), channel_id=1, source_target_pairs={{0,384},{64,448},{128,256},{192,320},{256,128},{320,192},{384,0},{... | collective-permute-start | bytes 393224 | tf_op jit(solution)/shard_map/ppermute | solution.py:249
  42.0 3.6 %collective-permute-start.1 = (bf16[2,256,128]{2,1,0:T(8,128)(2,1)}, bf16[2,256,128]{2,1,0:T(8,128)(2,1)}, u32[]{:S(2)}, u32[]{:S(2)}) collective-permute-start(bf16[2,256,128]{2,1,0:T(8,128)(2,1)} %pad_maximum_fusion), channel_id=1, source_target_pairs={{0,320},{64,256},{128,448},{192,384},{256,64},{320,0},{384,192},{4... | collective-permute-start | bytes 393224 | tf_op jit(solution)/shard_map/ppermute | solution.py:249
  45.6 1.0 %copy-done.3 = bf16[1,3,4,128,128]{4,3,2,1,0:T(8,128)(2,1)S(1)} copy-done((bf16[1,3,4,128,128]{4,3,2,1,0:T(8,128)(2,1)S(1)}, bf16[1,3,4,128,128]{4,3,2,1,0:T(8,128)(2,1)}, u32[]{:S(2)}) %copy-start.3) | copy-done | bytes 393240
  46.6 0.8 %copy-done.10 = bf16[1,2,128,128]{3,2,1,0:T(8,128)(2,1)S(1)} copy-done((bf16[1,2,128,128]{3,2,1,0:T(8,128)(2,1)S(1)}, bf16[1,2,128,128]{3,2,1,0:T(8,128)(2,1)}, u32[]{:S(2)}) %copy-start.10) | copy-done | bytes 65560
  47.4 0.4 fold.1.refs_2_
  47.8 2.7 %all-to-all-done.1.refs_1_ = bf16[64,32,128]{2,1,0:T(8,128)(2,1)S(1)} async-done(((bf16[64,32,128]{2,1,0:T(8,128)(2,1)}), bf16[64,32,128]{2,1,0:T(8,128)(2,1)S(1)}, u32[]{:S(2)}, u32[]{:S(2)}) %all-to-all-start.1) | async-done | bytes 524320 | tf_op jit(solution)/shard_map/all_to_all | solution.py:263
  50.5 0.3 down.1
  50.8 0.6 copy-done.6
  51.5 4.8 %all-to-all-start.2 = ((bf16[8,32,128]{2,1,0:T(8,128)(2,1)}), bf16[8,32,128]{2,1,0:T(8,128)(2,1)S(1)}, u32[]{:S(2)}, u32[]{:S(2)}) async-start(bf16[8,32,128]{2,1,0:T(8,128)(2,1)} %copy-done.6), calls=%async_computation.2 | async-start | bytes 131072 | tf_op jit(solution)/shard_map/all_to_all | solution.py:278
  56.2 0.7 %dense.1.refs_6_ = f32[256,1024]{1,0:T(8,128)S(1)} custom-call(bf16[256,1024]{1,0:T(8,128)(2,1)S(1)} %bitcast.18, bf16[1024,1024]{1,0:T(8,128)(2,1)S(1)} %bitcast.16), custom_call_target="tpu_custom_call" | custom-call | flops 536870912 | bytes 2621440 | tf_op jit(solution)/shard_map/dense/pallas_call | solution.py:39
  57.1 2.7 %local.1 = (f32[256,1024]{1,0:T(8,128)S(1)}, bf16[128,1024]{1,0:T(8,128)(2,1)S(1)}) custom-call(s32[1]{0:T(128)} %step.1.refs_0_, s32[8]{0:T(128)S(1)} %bitcast.26, bf16[256,128]{1,0:T(8,128)(2,1)S(1)} %copy-done.8, bf16[2,256,128]{2,1,0:T(8,128)(2,1)} %collective-permute-done.1.refs_3_, bf16[2,256,128]{2,1,0:T(8,128)(2,1)} %collective-permute-done.2.refs_4_, ...), custom_call_target="tpu_custom_call" | custom-call | flops 67108864 | bytes 2064384 | tf_op jit(solution)/shard_map/local/pallas_call | solution.py:39
  59.8 4.8 %all-to-all-done.2.far_ref = bf16[8,32,128]{2,1,0:T(8,128)(2,1)S(1)} async-done(((bf16[8,32,128]{2,1,0:T(8,128)(2,1)}), bf16[8,32,128]{2,1,0:T(8,128)(2,1)S(1)}, u32[]{:S(2)}, u32[]{:S(2)}) %all-to-all-start.2) | async-done | bytes 65568 | tf_op jit(solution)/shard_map/all_to_all | solution.py:278
  64.6 1.2 %last.1 = f32[256,1024]{1,0:T(8,128)} custom-call(bf16[8,32,128]{2,1,0:T(8,128)(2,1)S(1)} %all-to-all-done.2.far_ref, f32[256,1024]{1,0:T(8,128)S(1)} %get-tuple-element.29.base_ref, bf16[128,1024]{1,0:T(8,128)(2,1)S(1)} %get-tuple-element.30.weight_ref), custom_call_target="tpu_custom_call" | custom-call | flops 67108864 | bytes 2097152 | tf_op jit(solution)/shard_map/last/pallas_call | solution.py:211
  (26 shorter events, 0.1 us)
Async XLA Ops:
  2.3 54.0 %copy-start = (bf16[1,1,1024,1024]{3,2,1,0:T(8,128)(2,1)S(1)}, bf16[1,1,1024,1024]{3,2,1,0:T(8,128)(2,1)}, u32[]{:S(2)}) copy-start(bf16[1,1,1024,1024]{3,2,1,0:T(8,128)(2,1)} %param.13) | copy-start | bytes 6291460
  2.3 53.9 %copy-start.1 = (bf16[1,1,256,1024]{3,2,1,0:T(8,128)(2,1)S(1)}, bf16[1,1,256,1024]{3,2,1,0:T(8,128)(2,1)}, u32[]{:S(2)}) copy-start(bf16[1,1,256,1024]{3,2,1,0:T(8,128)(2,1)} %param.11) | copy-start | bytes 1572868
  2.3 18.8 %all-to-all-start = ((bf16[8,32,128]{2,1,0:T(8,128)(2,1)}), bf16[8,32,128]{2,1,0:T(8,128)(2,1)S(1)}, u32[]{:S(2)}, u32[]{:S(2)}) async-start(bf16[8,32,128]{2,1,0:T(8,128)(2,1)} %get-tuple-element.19), calls=%async_computation | async-start | bytes 131072 | tf_op jit(solution)/shard_map/all_to_all | solution.py:253
  13.3 9.0 %collective-permute-start = (bf16[256,128]{1,0:T(8,128)(2,1)}, bf16[256,128]{1,0:T(8,128)(2,1)S(1)}, u32[]{:S(2)}, u32[]{:S(2)}) collective-permute-start(bf16[256,128]{1,0:T(8,128)(2,1)} %get-tuple-element.28), channel_id=1, source_target_pairs={{0,64},{64,0},{128,192},{192,128},{256,320},{320,256},{384,448},{4... | collective-permute-start | bytes 196616 | tf_op jit(solution)/shard_map/ppermute | solution.py:249
  17.2 0.8 %copy-start.9 = (bf16[1,2,128,128]{3,2,1,0:T(8,128)(2,1)S(1)}, bf16[1,2,128,128]{3,2,1,0:T(8,128)(2,1)}, u32[]{:S(2)}) copy-start(bf16[1,2,128,128]{3,2,1,0:T(8,128)(2,1)} %param.19) | copy-start | bytes 196612
  21.4 0.8 %copy-start.2 = (bf16[64,32,128]{2,1,0:T(8,128)(2,1)}, bf16[64,32,128]{2,1,0:T(8,128)(2,1)S(1)}, u32[]{:S(2)}) copy-start(bf16[64,32,128]{2,1,0:T(8,128)(2,1)S(1)} %up.1) | copy-start | bytes 1572868
  22.2 23.3 %copy-start.7 = (bf16[256,128]{1,0:T(8,128)(2,1)}, bf16[256,128]{1,0:T(8,128)(2,1)S(1)}, u32[]{:S(2)}) copy-start(bf16[256,128]{1,0:T(8,128)(2,1)S(1)} %collective-permute-done.refs_2_) | copy-start | bytes 196612
  22.3 28.3 %all-to-all-start.1 = ((bf16[64,32,128]{2,1,0:T(8,128)(2,1)}), bf16[64,32,128]{2,1,0:T(8,128)(2,1)S(1)}, u32[]{:S(2)}, u32[]{:S(2)}) async-start(bf16[64,32,128]{2,1,0:T(8,128)(2,1)} %copy-done.2), calls=%async_computation.1 | async-start | bytes 1048576 | tf_op jit(solution)/shard_map/all_to_all | solution.py:263
  34.2 22.7 %collective-permute-start.3 = (bf16[2,256,128]{2,1,0:T(8,128)(2,1)}, bf16[2,256,128]{2,1,0:T(8,128)(2,1)}, u32[]{:S(2)}, u32[]{:S(2)}) collective-permute-start(bf16[2,256,128]{2,1,0:T(8,128)(2,1)} %pad_maximum_fusion), channel_id=1, source_target_pairs={{0,128},{64,192},{128,0},{192,64},{256,384},{320,448},{384,256},{4... | collective-permute-start | bytes 393224 | tf_op jit(solution)/shard_map/ppermute | solution.py:249
  36.6 20.4 %collective-permute-start.2 = (bf16[2,256,128]{2,1,0:T(8,128)(2,1)}, bf16[2,256,128]{2,1,0:T(8,128)(2,1)}, u32[]{:S(2)}, u32[]{:S(2)}) collective-permute-start(bf16[2,256,128]{2,1,0:T(8,128)(2,1)} %pad_maximum_fusion), channel_id=1, source_target_pairs={{0,384},{64,448},{128,256},{192,320},{256,128},{320,192},{384,0},{... | collective-permute-start | bytes 393224 | tf_op jit(solution)/shard_map/ppermute | solution.py:249
  42.0 15.0 %collective-permute-start.1 = (bf16[2,256,128]{2,1,0:T(8,128)(2,1)}, bf16[2,256,128]{2,1,0:T(8,128)(2,1)}, u32[]{:S(2)}, u32[]{:S(2)}) collective-permute-start(bf16[2,256,128]{2,1,0:T(8,128)(2,1)} %pad_maximum_fusion), channel_id=1, source_target_pairs={{0,320},{64,256},{128,448},{192,384},{256,64},{320,0},{384,192},{4... | collective-permute-start | bytes 393224 | tf_op jit(solution)/shard_map/ppermute | solution.py:249
  45.6 1.0 %copy-start.3 = (bf16[1,3,4,128,128]{4,3,2,1,0:T(8,128)(2,1)S(1)}, bf16[1,3,4,128,128]{4,3,2,1,0:T(8,128)(2,1)}, u32[]{:S(2)}) copy-start(bf16[1,3,4,128,128]{4,3,2,1,0:T(8,128)(2,1)} %param.21) | copy-start | bytes 1179652
  46.6 0.8 %copy-start.10 = (bf16[1,2,128,128]{3,2,1,0:T(8,128)(2,1)S(1)}, bf16[1,2,128,128]{3,2,1,0:T(8,128)(2,1)}, u32[]{:S(2)}) copy-start(bf16[1,2,128,128]{3,2,1,0:T(8,128)(2,1)} %param.20) | copy-start | bytes 196612
  50.8 0.6 copy-start.6
  51.4 5.6 %copy-start.4 = (bf16[1,1,8,128,128]{4,3,2,1,0:T(8,128)(2,1)S(1)}, bf16[1,1,8,128,128]{4,3,2,1,0:T(8,128)(2,1)}, u32[]{:S(2)}) copy-start(bf16[1,1,8,128,128]{4,3,2,1,0:T(8,128)(2,1)} %param.18) | copy-start | bytes 786436
  51.4 5.6 %copy-start.5 = (bf16[1,1,128,1024]{3,2,1,0:T(8,128)(2,1)S(1)}, bf16[1,1,128,1024]{3,2,1,0:T(8,128)(2,1)}, u32[]{:S(2)}) copy-start(bf16[1,1,128,1024]{3,2,1,0:T(8,128)(2,1)} %param.15) | copy-start | bytes 786436
  51.5 5.6 %copy-start.8 = (bf16[256,128]{1,0:T(8,128)(2,1)S(1)}, bf16[256,128]{1,0:T(8,128)(2,1)}, u32[]{:S(2)}) copy-start(bf16[256,128]{1,0:T(8,128)(2,1)} %copy-done.7) | copy-start | bytes 196612
  51.5 5.6 %copy-start.11 = (bf16[1,1,128,128]{3,2,1,0:T(8,128)(2,1)S(1)}, bf16[1,1,128,128]{3,2,1,0:T(8,128)(2,1)}, u32[]{:S(2)}) copy-start(bf16[1,1,128,128]{3,2,1,0:T(8,128)(2,1)} %param.17) | copy-start | bytes 98308
  51.5 5.6 %copy-start.12 = (s32[1,8]{1,0:T(1,128)S(1)}, s32[1,8]{1,0:T(1,128)}, u32[]{:S(2)}) copy-start(s32[1,8]{1,0:T(1,128)} %param.12) | copy-start | bytes 100
  51.5 13.1 %all-to-all-start.2 = ((bf16[8,32,128]{2,1,0:T(8,128)(2,1)}), bf16[8,32,128]{2,1,0:T(8,128)(2,1)S(1)}, u32[]{:S(2)}, u32[]{:S(2)}) async-start(bf16[8,32,128]{2,1,0:T(8,128)(2,1)} %copy-done.6), calls=%async_computation.2 | async-start | bytes 131072 | tf_op jit(solution)/shard_map/all_to_all | solution.py:278

commit v5 on v4

--- a/solution.py
+++ b/solution.py
@@ -58,7 +58,9 @@
     return total
 
 
-def first_kernel(models_ref, in_ref, up_ref, lifted_ref, skeleton_ref, models, leaf_in, up, sems):
+def first_kernel(
+    models_ref, in_ref, up_ref, lifted_ref, skeleton_ref, pair_ref, models, leaf_in, up, sems
+):
     half = models.shape[1] // 2
     copies = []
     for k in range(2):
@@ -79,6 +81,8 @@
         coeff = term if coeff is None else coeff + term
     skeleton = coeff.astype(BF)
     skeleton_ref[...] = skeleton
+    pair_ref[0] = skeleton
+    pair_ref[1] = skeleton
     copies[4].wait()
     lifted_ref[...] = mm(skeleton, up[...]).astype(BF).reshape(lifted_ref.shape)
 
@@ -91,9 +95,10 @@
         out_shape=[
             jax.ShapeDtypeStruct((n_leaf, m // n_leaf, r), BF),
             jax.ShapeDtypeStruct((m, r), BF),
+            jax.ShapeDtypeStruct((2, m, r), BF),
         ],
         in_specs=[pl.BlockSpec(memory_space=pl.ANY)] * 3,
-        out_specs=[pl.BlockSpec(memory_space=pltpu.VMEM)] * 2,
+        out_specs=[pl.BlockSpec(memory_space=pltpu.VMEM)] * 3,
         scratch_shapes=[pltpu.VMEM(a.shape, BF) for a in (models, leaf_in, leaf_up)]
         + [pltpu.SemaphoreType.DMA((5,))],
         compiler_params=pltpu.CompilerParams(vmem_limit_bytes=58 * 2**20),
@@ -118,8 +123,8 @@
     )(leaf)
 
 
-def hold_kernel(upper_up_ref, held_ref):
-    held_ref[...] = upper_up_ref[...]
+def hold_kernel(weight_ref, held_ref):
+    held_ref[...] = weight_ref[...]
 
 
 def up_kernel(wide_ref, parts_ref, up_ref, sent_ref):
@@ -135,26 +140,18 @@
         sent_ref[wide // 4 * 4 + k] = own
 
 
-def fold_kernel(couple_ref, upper_down, folded_ref):
-    down_ref = upper_down()
-    r = down_ref.shape[-1]
-    flat = (4 * r, r)
-    folded_ref[0] = couple_ref[0]
-    top = mm(couple_ref[2].reshape(flat), down_ref[1]).astype(BF)
-    folded_ref[2] = mm(top, down_ref[0]).astype(BF).reshape(4, r, r)
-    folded_ref[1] = mm(couple_ref[1].reshape(flat), down_ref[0]).astype(BF).reshape(4, r, r)
-
-
-def down_kernel(wide_ref, heard_ref, folded_ref, far_ref):
+def down_kernel(wide_ref, heard_ref, couple_ref, down_ref, far_ref):
     wide = wide_ref[0]
     field = None
     for level in (2, 1, 0):
+        if field is not None:
+            field = mm(field.astype(BF), down_ref[level])
         step = 4**level
         first = wide // (4 * step) * 4
         for s in range(4):
             block = total_of(heard_ref, (first + s) * step, step)
             block = jnp.where(first + s == wide // step, jnp.zeros_like(block), block)
-            term = mm(block.astype(BF), folded_ref[level, s])
+            term = mm(block.astype(BF), couple_ref[level, s])
             field = term if field is None else field + term
     rounded = field.astype(BF)
     for k in range(far_ref.shape[0]):
@@ -248,7 +245,7 @@
     def partner(x, step):
         return lax.ppermute(x, "leaf", [(k, k ^ step) for k in range(n_leaf)])
 
-    lifted, skeleton = first_call(inputs, leaf_in[0, 0], leaf_up[0, 0], n_leaf)
+    lifted, skeleton, pair = first_call(inputs, leaf_in[0, 0], leaf_up[0, 0], n_leaf)
     lifted, upper_up, leaf = lax.optimization_barrier((lifted, upper_up, leaf))
     parts = lax.all_to_all(lifted, "leaf", 0, 0, tiled=True)
     leaf, skeleton = lax.optimization_barrier((step_call(leaf), skeleton))
@@ -257,23 +254,17 @@
     (sent,) = call(
         up_kernel, [((n_wide, cut, r), BF)], [wide], [parts, ups], name="up"
     )
-    sent, skeleton, following, upper_down = lax.optimization_barrier(
-        (sent, skeleton, following, upper_down)
-    )
+    sent, following, upper_down = lax.optimization_barrier((sent, following, upper_down))
     heard = lax.all_to_all(sent, "wide", 0, 0, tiled=True)
-    pair = jnp.stack([skeleton, following])
+    pair = lax.dynamic_update_slice(pair, following[None], (1, 0, 0))
     two, six, five = [partner(pair, step) for step in (2, 6, 5)]
-    (folded,) = call(
-        fold_kernel,
-        [(upper_couple.shape[1:], BF)],
-        [],
-        [upper_couple[0]],
-        [upper_down[0]],
-        flops=24 * r * r * r,
-        name="fold",
-    )
+    (downs,) = call(hold_kernel, [(upper_down.shape[1:], BF)], [], [upper_down[0]], name="hold_down")
     (far,) = call(
-        down_kernel, [((n_leaf, cut, r), BF)], [wide], [heard, folded], name="down"
+        down_kernel,
+        [((n_leaf, cut, r), BF)],
+        [wide],
+        [heard, upper_couple[0], downs],
+        name="down",
     )
     far = lax.all_to_all(far, "leaf", 0, 0, tiled=True)
     (dense,) = call(

time: 66.5 us -> 68.2 us (1.026)
  local copies, waits for them, and re-layouts: 4.11 us -> 5.87 us
  other arithmetic: 1.52 us -> 0 us
  Pallas kernels: 8.37 us -> 9.3 us
  waiting for transfers between devices: 10.6 us -> 11.4 us
    another operation x1 -> x0, other arithmetic: 1.52 us -> none  [shards(): pair = jnp.stack([skeleton, following])]
    dynamic_update_slice x0 -> x1, local copies, waits for them, and re-layouts: none -> 1.47 us  [shards(): pair = lax.dynamic_update_slice(pair, following[None], (1, 0, 0))]
    all_to_all x1, waiting for transfers between devices: 2.72 us -> 3.55 us  [shards(): heard = lax.all_to_all(sent, 'wide', 0, 0, tiled=True)]
    pallas_call x6, Pallas kernels: 4.4 us -> 5.18 us  [call(): pl.pallas_call(kernel, out_shape=[jax.ShapeDtypeStruct(s, t) for s, t in...]
    unnamed x26 -> x28, local copies, waits for them, and re-layouts: 4.11 us -> 4.4 us
  transfers between devices with their start and end apart: 7 -> 7, of which waited for: 3 -> 3; matrix products, arithmetic and copies ran while one was open for 2% -> 2% of each run, Pallas kernels for 7% -> 8%
where the time goes in v5:
time: 68.2 us; the launch traced here: 67.6 us
  starting transfers between devices  40.8 us (60%)
  waiting for transfers between devices  11.4 us (17%)
  Pallas kernels  9.3 us (14%)
  local copies, waits for them, and re-layouts  5.87 us (9%)
    ppermute x4, starting transfers between devices, partner(): return lax.ppermute(x, 'leaf', [(k, k ^ step) for k in range(n_leaf)])  15.2 us
    all_to_all x1, starting transfers between devices, shards(): heard = lax.all_to_all(sent, 'wide', 0, 0, tiled=True)  10.5 us
    all_to_all x1, starting transfers between devices, shards(): parts = lax.all_to_all(lifted, 'leaf', 0, 0, tiled=True)  10.3 us
    pallas_call x6, Pallas kernels, call(): pl.pallas_call(kernel, out_shape=[jax.ShapeDtypeStruct(s, t) for s, t in...  5.18 us
    all_to_all x1, starting transfers between devices, shards(): far = lax.all_to_all(far, 'leaf', 0, 0, tiled=True)  4.75 us
    all_to_all x1, waiting for transfers between devices, shards(): far = lax.all_to_all(far, 'leaf', 0, 0, tiled=True)  4.75 us
    unnamed x28, local copies, waits for them, and re-layouts  4.4 us
    all_to_all x1, waiting for transfers between devices, shards(): heard = lax.all_to_all(sent, 'wide', 0, 0, tiled=True)  3.55 us
  transfers between devices with their start and end apart: 7, of which 3 were waited for; matrix products, arithmetic and copies ran while one was open for 2% of the time, Pallas kernels for 8%

profile of v5, /device:TPU:16, one launch (start us, length us, event | category | flops | bytes accessed | tf_op | source)
XLA Modules:
  0.0 67.6 jit_solution(1166523319041844428)
XLA Ops:
  0.0 2.4 %first.1 = (bf16[8,32,128]{2,1,0:T(8,128)(2,1)}, bf16[256,128]{1,0:T(8,128)(2,1)}, bf16[2,256,128]{2,1,0:T(8,128)(2,1)}) custom-call(bf16[256,1024]{1,0:T(8,128)(2,1)} %bitcast.17, bf16[1024,128]{1,0:T(8,128)(2,1)} %bitcast.26, bf16[128,128]{1,0:T(8,128)(2,1)} %bitcast.27), custom_call_target="tpu_custom_call" | custom-call | flops 67108864 | bytes 524288 | tf_op jit(solution)/shard_map/first/pallas_call | solution.py:93
  2.4 10.3 %all-to-all-start = ((bf16[8,32,128]{2,1,0:T(8,128)(2,1)}), bf16[8,32,128]{2,1,0:T(8,128)(2,1)S(1)}, u32[]{:S(2)}, u32[]{:S(2)}) async-start(bf16[8,32,128]{2,1,0:T(8,128)(2,1)} %get-tuple-element.19), calls=%async_computation | async-start | bytes 131072 | tf_op jit(solution)/shard_map/all_to_all | solution.py:250
  12.8 0.5 step.1.refs_0_
  13.3 3.9 %collective-permute-start = (bf16[256,128]{1,0:T(8,128)(2,1)}, bf16[256,128]{1,0:T(8,128)(2,1)S(1)}, u32[]{:S(2)}, u32[]{:S(2)}) collective-permute-start(bf16[256,128]{1,0:T(8,128)(2,1)} %get-tuple-element.23), channel_id=1, source_target_pairs={{0,64},{64,0},{128,192},{192,128},{256,320},{320,256},{384,448},{4... | collective-permute-start | bytes 196616 | tf_op jit(solution)/shard_map/ppermute | solution.py:246
  17.2 0.8 %copy-done.10 = bf16[1,2,128,128]{3,2,1,0:T(8,128)(2,1)S(1)} copy-done((bf16[1,2,128,128]{3,2,1,0:T(8,128)(2,1)S(1)}, bf16[1,2,128,128]{3,2,1,0:T(8,128)(2,1)}, u32[]{:S(2)}) %copy-start.10) | copy-done | bytes 65560
  18.1 3.1 %all-to-all-done.refs_1_ = bf16[8,32,128]{2,1,0:T(8,128)(2,1)S(1)} async-done(((bf16[8,32,128]{2,1,0:T(8,128)(2,1)}), bf16[8,32,128]{2,1,0:T(8,128)(2,1)S(1)}, u32[]{:S(2)}, u32[]{:S(2)}) %all-to-all-start) | async-done | bytes 65568 | tf_op jit(solution)/shard_map/all_to_all | solution.py:250
  21.1 1.1 %up.1 = bf16[64,32,128]{2,1,0:T(8,128)(2,1)} custom-call(s32[1]{0:T(128)} %bitcast.refs_0_, bf16[8,32,128]{2,1,0:T(8,128)(2,1)S(1)} %all-to-all-done.refs_1_, bf16[2,128,128]{2,1,0:T(8,128)(2,1)S(1)} %hold.1.refs_2_), custom_call_target="tpu_custom_call" | custom-call | flops 1000000 | bytes 131072 | tf_op jit(solution)/shard_map/up/pallas_call | solution.py:39
  22.3 0.6 copy-done.5
  22.9 10.5 %all-to-all-start.1 = ((bf16[64,32,128]{2,1,0:T(8,128)(2,1)}), bf16[64,32,128]{2,1,0:T(8,128)(2,1)S(1)}, u32[]{:S(2)}, u32[]{:S(2)}) async-start(bf16[64,32,128]{2,1,0:T(8,128)(2,1)} %up.1), calls=%async_computation.1 | async-start | bytes 1048576 | tf_op jit(solution)/shard_map/all_to_all | solution.py:258
  33.4 1.5 %bitcast_dynamic-update-slice_fusion = bf16[2,256,128]{2,1,0:T(8,128)(2,1)} fusion(bf16[2,256,128]{2,1,0:T(8,128)(2,1)} %get-tuple-element.28, bf16[256,128]{1,0:T(8,128)(2,1)} %copy-done.5), kind=kLoop, calls=%fused_computation | loop fusion | bytes 131072 | tf_op jit(solution)/shard_map/dynamic_update_slice | solution.py:259
  34.8 2.4 %collective-permute-start.3 = (bf16[2,256,128]{2,1,0:T(8,128)(2,1)}, bf16[2,256,128]{2,1,0:T(8,128)(2,1)}, u32[]{:S(2)}, u32[]{:S(2)}) collective-permute-start(bf16[2,256,128]{2,1,0:T(8,128)(2,1)} %bitcast_dynamic-update-slice_fusion), channel_id=1, source_target_pairs={{0,128},{64,192},{128,0},{192,64},{256,384},{320,448},{384,256},{4... | collective-permute-start | bytes 393224 | tf_op jit(solution)/shard_map/ppermute | solution.py:246
  37.2 5.3 %collective-permute-start.2 = (bf16[2,256,128]{2,1,0:T(8,128)(2,1)}, bf16[2,256,128]{2,1,0:T(8,128)(2,1)}, u32[]{:S(2)}, u32[]{:S(2)}) collective-permute-start(bf16[2,256,128]{2,1,0:T(8,128)(2,1)} %bitcast_dynamic-update-slice_fusion), channel_id=1, source_target_pairs={{0,384},{64,448},{128,256},{192,320},{256,128},{320,192},{384,0},{... | collective-permute-start | bytes 393224 | tf_op jit(solution)/shard_map/ppermute | solution.py:246
  42.5 3.6 %collective-permute-start.1 = (bf16[2,256,128]{2,1,0:T(8,128)(2,1)}, bf16[2,256,128]{2,1,0:T(8,128)(2,1)}, u32[]{:S(2)}, u32[]{:S(2)}) collective-permute-start(bf16[2,256,128]{2,1,0:T(8,128)(2,1)} %bitcast_dynamic-update-slice_fusion), channel_id=1, source_target_pairs={{0,320},{64,256},{128,448},{192,384},{256,64},{320,0},{384,192},{4... | collective-permute-start | bytes 393224 | tf_op jit(solution)/shard_map/ppermute | solution.py:246
  46.2 0.8 %copy-done.11 = bf16[1,2,128,128]{3,2,1,0:T(8,128)(2,1)S(1)} copy-done((bf16[1,2,128,128]{3,2,1,0:T(8,128)(2,1)S(1)}, bf16[1,2,128,128]{3,2,1,0:T(8,128)(2,1)}, u32[]{:S(2)}) %copy-start.11) | copy-done | bytes 65560
  47.0 0.6 copy-done.8
  47.6 3.5 %all-to-all-done.1.refs_1_ = bf16[64,32,128]{2,1,0:T(8,128)(2,1)S(1)} async-done(((bf16[64,32,128]{2,1,0:T(8,128)(2,1)}), bf16[64,32,128]{2,1,0:T(8,128)(2,1)S(1)}, u32[]{:S(2)}, u32[]{:S(2)}) %all-to-all-start.1) | async-done | bytes 524320 | tf_op jit(solution)/shard_map/all_to_all | solution.py:258
  51.2 0.8 %copy-done.9 = bf16[2,128,128]{2,1,0:T(8,128)(2,1)S(1)} copy-done((bf16[2,128,128]{2,1,0:T(8,128)(2,1)S(1)}, bf16[2,128,128]{2,1,0:T(8,128)(2,1)}, u32[]{:S(2)}) %copy-start.9) | copy-done | bytes 65560
  52.0 0.5 down.1
  52.6 0.6 copy-done.7
  53.2 4.8 %all-to-all-start.2 = ((bf16[8,32,128]{2,1,0:T(8,128)(2,1)}), bf16[8,32,128]{2,1,0:T(8,128)(2,1)S(1)}, u32[]{:S(2)}, u32[]{:S(2)}) async-start(bf16[8,32,128]{2,1,0:T(8,128)(2,1)} %copy-done.7), calls=%async_computation.2 | async-start | bytes 131072 | tf_op jit(solution)/shard_map/all_to_all | solution.py:269
  58.0 0.7 %dense.1.refs_6_ = f32[256,1024]{1,0:T(8,128)S(1)} custom-call(bf16[256,1024]{1,0:T(8,128)(2,1)S(1)} %bitcast.18, bf16[1024,1024]{1,0:T(8,128)(2,1)S(1)} %bitcast.16), custom_call_target="tpu_custom_call" | custom-call | flops 536870912 | bytes 2621440 | tf_op jit(solution)/shard_map/dense/pallas_call | solution.py:39
  58.8 2.8 %local.1 = (f32[256,1024]{1,0:T(8,128)S(1)}, bf16[128,1024]{1,0:T(8,128)(2,1)S(1)}) custom-call(s32[1]{0:T(128)} %step.1.refs_0_, s32[8]{0:T(128)S(1)} %bitcast.25, bf16[256,128]{1,0:T(8,128)(2,1)S(1)} %copy-done.6, bf16[2,256,128]{2,1,0:T(8,128)(2,1)} %collective-permute-done.1.refs_3_, bf16[2,256,128]{2,1,0:T(8,128)(2,1)} %collective-permute-done.2.refs_4_, ...), custom_call_target="tpu_custom_call" | custom-call | flops 67108864 | bytes 2064384 | tf_op jit(solution)/shard_map/local/pallas_call | solution.py:39
  61.6 4.7 %all-to-all-done.2.far_ref = bf16[8,32,128]{2,1,0:T(8,128)(2,1)S(1)} async-done(((bf16[8,32,128]{2,1,0:T(8,128)(2,1)}), bf16[8,32,128]{2,1,0:T(8,128)(2,1)S(1)}, u32[]{:S(2)}, u32[]{:S(2)}) %all-to-all-start.2) | async-done | bytes 65568 | tf_op jit(solution)/shard_map/all_to_all | solution.py:269
  66.4 1.2 %last.1 = f32[256,1024]{1,0:T(8,128)} custom-call(bf16[8,32,128]{2,1,0:T(8,128)(2,1)S(1)} %all-to-all-done.2.far_ref, f32[256,1024]{1,0:T(8,128)S(1)} %get-tuple-element.29.base_ref, bf16[128,1024]{1,0:T(8,128)(2,1)S(1)} %get-tuple-element.30.weight_ref), custom_call_target="tpu_custom_call" | custom-call | flops 67108864 | bytes 2097152 | tf_op jit(solution)/shard_map/last/pallas_call | solution.py:208
  (28 shorter events, 0.1 us)
Async XLA Ops:
  0.0 51.2 %copy-start.2 = (bf16[1,3,4,128,128]{4,3,2,1,0:T(8,128)(2,1)S(1)}, bf16[1,3,4,128,128]{4,3,2,1,0:T(8,128)(2,1)}, u32[]{:S(2)}) copy-start(bf16[1,3,4,128,128]{4,3,2,1,0:T(8,128)(2,1)} %param.21) | copy-start | bytes 1179652
  0.0 58.0 %copy-start = (bf16[1,1,1024,1024]{3,2,1,0:T(8,128)(2,1)S(1)}, bf16[1,1,1024,1024]{3,2,1,0:T(8,128)(2,1)}, u32[]{:S(2)}) copy-start(bf16[1,1,1024,1024]{3,2,1,0:T(8,128)(2,1)} %param.13) | copy-start | bytes 6291460
  0.0 58.0 %copy-start.1 = (bf16[1,1,256,1024]{3,2,1,0:T(8,128)(2,1)S(1)}, bf16[1,1,256,1024]{3,2,1,0:T(8,128)(2,1)}, u32[]{:S(2)}) copy-start(bf16[1,1,256,1024]{3,2,1,0:T(8,128)(2,1)} %param.11) | copy-start | bytes 1572868
  2.4 18.7 %all-to-all-start = ((bf16[8,32,128]{2,1,0:T(8,128)(2,1)}), bf16[8,32,128]{2,1,0:T(8,128)(2,1)S(1)}, u32[]{:S(2)}, u32[]{:S(2)}) async-start(bf16[8,32,128]{2,1,0:T(8,128)(2,1)} %get-tuple-element.19), calls=%async_computation | async-start | bytes 131072 | tf_op jit(solution)/shard_map/all_to_all | solution.py:250
  13.3 9.0 %collective-permute-start = (bf16[256,128]{1,0:T(8,128)(2,1)}, bf16[256,128]{1,0:T(8,128)(2,1)S(1)}, u32[]{:S(2)}, u32[]{:S(2)}) collective-permute-start(bf16[256,128]{1,0:T(8,128)(2,1)} %get-tuple-element.23), channel_id=1, source_target_pairs={{0,64},{64,0},{128,192},{192,128},{256,320},{320,256},{384,448},{4... | collective-permute-start | bytes 196616 | tf_op jit(solution)/shard_map/ppermute | solution.py:246
  17.2 0.8 %copy-start.10 = (bf16[1,2,128,128]{3,2,1,0:T(8,128)(2,1)S(1)}, bf16[1,2,128,128]{3,2,1,0:T(8,128)(2,1)}, u32[]{:S(2)}) copy-start(bf16[1,2,128,128]{3,2,1,0:T(8,128)(2,1)} %param.19) | copy-start | bytes 196612
  22.3 0.6 copy-start.5
  22.9 28.3 %all-to-all-start.1 = ((bf16[64,32,128]{2,1,0:T(8,128)(2,1)}), bf16[64,32,128]{2,1,0:T(8,128)(2,1)S(1)}, u32[]{:S(2)}, u32[]{:S(2)}) async-start(bf16[64,32,128]{2,1,0:T(8,128)(2,1)} %up.1), calls=%async_computation.1 | async-start | bytes 1048576 | tf_op jit(solution)/shard_map/all_to_all | solution.py:258
  34.8 23.9 %collective-permute-start.3 = (bf16[2,256,128]{2,1,0:T(8,128)(2,1)}, bf16[2,256,128]{2,1,0:T(8,128)(2,1)}, u32[]{:S(2)}, u32[]{:S(2)}) collective-permute-start(bf16[2,256,128]{2,1,0:T(8,128)(2,1)} %bitcast_dynamic-update-slice_fusion), channel_id=1, source_target_pairs={{0,128},{64,192},{128,0},{192,64},{256,384},{320,448},{384,256},{4... | collective-permute-start | bytes 393224 | tf_op jit(solution)/shard_map/ppermute | solution.py:246
  37.2 21.5 %collective-permute-start.2 = (bf16[2,256,128]{2,1,0:T(8,128)(2,1)}, bf16[2,256,128]{2,1,0:T(8,128)(2,1)}, u32[]{:S(2)}, u32[]{:S(2)}) collective-permute-start(bf16[2,256,128]{2,1,0:T(8,128)(2,1)} %bitcast_dynamic-update-slice_fusion), channel_id=1, source_target_pairs={{0,384},{64,448},{128,256},{192,320},{256,128},{320,192},{384,0},{... | collective-permute-start | bytes 393224 | tf_op jit(solution)/shard_map/ppermute | solution.py:246
  42.5 16.2 %collective-permute-start.1 = (bf16[2,256,128]{2,1,0:T(8,128)(2,1)}, bf16[2,256,128]{2,1,0:T(8,128)(2,1)}, u32[]{:S(2)}, u32[]{:S(2)}) collective-permute-start(bf16[2,256,128]{2,1,0:T(8,128)(2,1)} %bitcast_dynamic-update-slice_fusion), channel_id=1, source_target_pairs={{0,320},{64,256},{128,448},{192,384},{256,64},{320,0},{384,192},{4... | collective-permute-start | bytes 393224 | tf_op jit(solution)/shard_map/ppermute | solution.py:246
  46.2 0.8 %copy-start.11 = (bf16[1,2,128,128]{3,2,1,0:T(8,128)(2,1)S(1)}, bf16[1,2,128,128]{3,2,1,0:T(8,128)(2,1)}, u32[]{:S(2)}) copy-start(bf16[1,2,128,128]{3,2,1,0:T(8,128)(2,1)} %param.20) | copy-start | bytes 196612
  47.0 0.6 copy-start.8
  51.2 0.8 %copy-start.9 = (bf16[2,128,128]{2,1,0:T(8,128)(2,1)S(1)}, bf16[2,128,128]{2,1,0:T(8,128)(2,1)}, u32[]{:S(2)}) copy-start(bf16[2,128,128]{2,1,0:T(8,128)(2,1)} %copy-done.8) | copy-start | bytes 196612
  52.6 0.6 copy-start.7
  53.2 5.6 %copy-start.3 = (bf16[1,1,8,128,128]{4,3,2,1,0:T(8,128)(2,1)S(1)}, bf16[1,1,8,128,128]{4,3,2,1,0:T(8,128)(2,1)}, u32[]{:S(2)}) copy-start(bf16[1,1,8,128,128]{4,3,2,1,0:T(8,128)(2,1)} %param.18) | copy-start | bytes 786436
  53.2 5.6 %copy-start.4 = (bf16[1,1,128,1024]{3,2,1,0:T(8,128)(2,1)S(1)}, bf16[1,1,128,1024]{3,2,1,0:T(8,128)(2,1)}, u32[]{:S(2)}) copy-start(bf16[1,1,128,1024]{3,2,1,0:T(8,128)(2,1)} %param.15) | copy-start | bytes 786436
  53.2 5.6 %copy-start.6 = (bf16[256,128]{1,0:T(8,128)(2,1)S(1)}, bf16[256,128]{1,0:T(8,128)(2,1)}, u32[]{:S(2)}) copy-start(bf16[256,128]{1,0:T(8,128)(2,1)} %copy-done.5) | copy-start | bytes 196612
  53.2 5.6 %copy-start.12 = (bf16[1,1,128,128]{3,2,1,0:T(8,128)(2,1)S(1)}, bf16[1,1,128,128]{3,2,1,0:T(8,128)(2,1)}, u32[]{:S(2)}) copy-start(bf16[1,1,128,128]{3,2,1,0:T(8,128)(2,1)} %param.17) | copy-start | bytes 98308
  53.2 5.6 %copy-start.13 = (s32[1,8]{1,0:T(1,128)S(1)}, s32[1,8]{1,0:T(1,128)}, u32[]{:S(2)}) copy-start(s32[1,8]{1,0:T(1,128)} %param.12) | copy-start | bytes 100
  53.2 13.1 %all-to-all-start.2 = ((bf16[8,32,128]{2,1,0:T(8,128)(2,1)}), bf16[8,32,128]{2,1,0:T(8,128)(2,1)S(1)}, u32[]{:S(2)}, u32[]{:S(2)}) async-start(bf16[8,32,128]{2,1,0:T(8,128)(2,1)} %copy-done.7), calls=%async_computation.2 | async-start | bytes 131072 | tf_op jit(solution)/shard_map/all_to_all | solution.py:269

commit v6 on v5

--- a/solution.py
+++ b/solution.py
@@ -58,9 +58,7 @@
     return total
 
 
-def first_kernel(
-    models_ref, in_ref, up_ref, lifted_ref, skeleton_ref, pair_ref, models, leaf_in, up, sems
-):
+def first_kernel(models_ref, in_ref, up_ref, lifted_ref, skeleton_ref, models, leaf_in, up, sems):
     half = models.shape[1] // 2
     copies = []
     for k in range(2):
@@ -81,8 +79,6 @@
         coeff = term if coeff is None else coeff + term
     skeleton = coeff.astype(BF)
     skeleton_ref[...] = skeleton
-    pair_ref[0] = skeleton
-    pair_ref[1] = skeleton
     copies[4].wait()
     lifted_ref[...] = mm(skeleton, up[...]).astype(BF).reshape(lifted_ref.shape)
 
@@ -95,10 +91,9 @@
         out_shape=[
             jax.ShapeDtypeStruct((n_leaf, m // n_leaf, r), BF),
             jax.ShapeDtypeStruct((m, r), BF),
-            jax.ShapeDtypeStruct((2, m, r), BF),
         ],
         in_specs=[pl.BlockSpec(memory_space=pl.ANY)] * 3,
-        out_specs=[pl.BlockSpec(memory_space=pltpu.VMEM)] * 3,
+        out_specs=[pl.BlockSpec(memory_space=pltpu.VMEM)] * 2,
         scratch_shapes=[pltpu.VMEM(a.shape, BF) for a in (models, leaf_in, leaf_up)]
         + [pltpu.SemaphoreType.DMA((5,))],
         compiler_params=pltpu.CompilerParams(vmem_limit_bytes=58 * 2**20),
@@ -123,8 +118,8 @@
     )(leaf)
 
 
-def hold_kernel(weight_ref, held_ref):
-    held_ref[...] = weight_ref[...]
+def hold_kernel(upper_up_ref, held_ref):
+    held_ref[...] = upper_up_ref[...]
 
 
 def up_kernel(wide_ref, parts_ref, up_ref, sent_ref):
@@ -140,19 +135,23 @@
         sent_ref[wide // 4 * 4 + k] = own
 
 
-def down_kernel(wide_ref, heard_ref, couple_ref, down_ref, far_ref):
+def down_kernel(wide_ref, heard_ref, couple_ref, upper_down, far_ref):
     wide = wide_ref[0]
-    field = None
-    for level in (2, 1, 0):
-        if field is not None:
-            field = mm(field.astype(BF), down_ref[level])
+    nears = []
+    for level in range(3):
         step = 4**level
         first = wide // (4 * step) * 4
+        near = None
         for s in range(4):
             block = total_of(heard_ref, (first + s) * step, step)
             block = jnp.where(first + s == wide // step, jnp.zeros_like(block), block)
             term = mm(block.astype(BF), couple_ref[level, s])
-            field = term if field is None else field + term
+            near = term if near is None else near + term
+        nears.append(near)
+    down_ref = upper_down()
+    field = nears[2]
+    for level in (1, 0):
+        field = nears[level] + mm(field.astype(BF), down_ref[level])
     rounded = field.astype(BF)
     for k in range(far_ref.shape[0]):
         far_ref[k] = rounded
@@ -245,7 +244,7 @@
     def partner(x, step):
         return lax.ppermute(x, "leaf", [(k, k ^ step) for k in range(n_leaf)])
 
-    lifted, skeleton, pair = first_call(inputs, leaf_in[0, 0], leaf_up[0, 0], n_leaf)
+    lifted, skeleton = first_call(inputs, leaf_in[0, 0], leaf_up[0, 0], n_leaf)
     lifted, upper_up, leaf = lax.optimization_barrier((lifted, upper_up, leaf))
     parts = lax.all_to_all(lifted, "leaf", 0, 0, tiled=True)
     leaf, skeleton = lax.optimization_barrier((step_call(leaf), skeleton))
@@ -254,16 +253,16 @@
     (sent,) = call(
         up_kernel, [((n_wide, cut, r), BF)], [wide], [parts, ups], name="up"
     )
-    sent, following, upper_down = lax.optimization_barrier((sent, following, upper_down))
+    sent, skeleton, following = lax.optimization_barrier((sent, skeleton, following))
     heard = lax.all_to_all(sent, "wide", 0, 0, tiled=True)
-    pair = lax.dynamic_update_slice(pair, following[None], (1, 0, 0))
+    pair = jnp.stack([skeleton, following])
     two, six, five = [partner(pair, step) for step in (2, 6, 5)]
-    (downs,) = call(hold_kernel, [(upper_down.shape[1:], BF)], [], [upper_down[0]], name="hold_down")
     (far,) = call(
         down_kernel,
         [((n_leaf, cut, r), BF)],
         [wide],
-        [heard, upper_couple[0], downs],
+        [heard, upper_couple[0]],
+        [upper_down[0]],
         name="down",
     )
     far = lax.all_to_all(far, "leaf", 0, 0, tiled=True)

time: 68.2 us -> 68.1 us (level)
  local copies, waits for them, and re-layouts: 5.87 us -> 3.75 us
  other arithmetic: 0 us -> 1.55 us
  waiting for transfers between devices: 11.4 us -> 12.8 us
  Pallas kernels: 9.3 us -> 8.39 us
    another operation x0 -> x1, other arithmetic: none -> 1.55 us  [shards(): pair = jnp.stack([skeleton, following])]
    dynamic_update_slice x1 -> x0, local copies, waits for them, and re-layouts: 1.47 us -> none  [shards(): pair = lax.dynamic_update_slice(pair, following[None], (1, 0, 0))]
    all_to_all x1, waiting for transfers between devices: 3.55 us -> 4.94 us  [shards(): heard = lax.all_to_all(sent, 'wide', 0, 0, tiled=True)]
    pallas_call x6 -> x5, Pallas kernels: 5.18 us -> 4.28 us  [call(): pl.pallas_call(kernel, out_shape=[jax.ShapeDtypeStruct(s, t) for s, t in...]
    unnamed x28 -> x26, local copies, waits for them, and re-layouts: 4.4 us -> 3.75 us
  transfers between devices with their start and end apart: 7 -> 7, of which waited for: 3 -> 3; matrix products, arithmetic and copies ran while one was open for 2% -> 2% of each run, Pallas kernels for 8% -> 7%
where the time goes in v6:
time: 68.1 us; the launch traced here: 67.5 us
  starting transfers between devices  40.8 us (60%)
  waiting for transfers between devices  12.8 us (19%)
  Pallas kernels  8.39 us (12%)
  local copies, waits for them, and re-layouts  3.75 us (6%)
  other arithmetic  1.55 us (2%)
    ppermute x4, starting transfers between devices, partner(): return lax.ppermute(x, 'leaf', [(k, k ^ step) for k in range(n_leaf)])  15.2 us
    all_to_all x1, starting transfers between devices, shards(): heard = lax.all_to_all(sent, 'wide', 0, 0, tiled=True)  10.5 us
    all_to_all x1, starting transfers between devices, shards(): parts = lax.all_to_all(lifted, 'leaf', 0, 0, tiled=True)  10.3 us
    all_to_all x1, waiting for transfers between devices, shards(): heard = lax.all_to_all(sent, 'wide', 0, 0, tiled=True)  4.94 us
    all_to_all x1, waiting for transfers between devices, shards(): far = lax.all_to_all(far, 'leaf', 0, 0, tiled=True)  4.83 us
    all_to_all x1, starting transfers between devices, shards(): far = lax.all_to_all(far, 'leaf', 0, 0, tiled=True)  4.76 us
    pallas_call x5, Pallas kernels, call(): pl.pallas_call(kernel, out_shape=[jax.ShapeDtypeStruct(s, t) for s, t in...  4.28 us
    unnamed x26, local copies, waits for them, and re-layouts  3.75 us
  transfers between devices with their start and end apart: 7, of which 3 were waited for; matrix products, arithmetic and copies ran while one was open for 2% of the time, Pallas kernels for 7%

profile of v6, /device:TPU:16, one launch (start us, length us, event | category | flops | bytes accessed | tf_op | source)
XLA Modules:
  0.0 67.5 jit_solution(14879382199484802546)
XLA Ops:
  0.0 2.4 %first.1 = (bf16[8,32,128]{2,1,0:T(8,128)(2,1)}, bf16[256,128]{1,0:T(8,128)(2,1)}) custom-call(bf16[256,1024]{1,0:T(8,128)(2,1)} %bitcast.17, bf16[1024,128]{1,0:T(8,128)(2,1)} %bitcast.27, bf16[128,128]{1,0:T(8,128)(2,1)} %bitcast.29), custom_call_target="tpu_custom_call" | custom-call | flops 67108864 | bytes 524288 | tf_op jit(solution)/shard_map/first/pallas_call | solution.py:89
  2.4 10.3 %all-to-all-start = ((bf16[8,32,128]{2,1,0:T(8,128)(2,1)}), bf16[8,32,128]{2,1,0:T(8,128)(2,1)S(1)}, u32[]{:S(2)}, u32[]{:S(2)}) async-start(bf16[8,32,128]{2,1,0:T(8,128)(2,1)} %get-tuple-element.18), calls=%async_computation | async-start | bytes 131072 | tf_op jit(solution)/shard_map/all_to_all | solution.py:249
  12.8 0.5 step.1.refs_0_
  13.3 3.9 %collective-permute-start = (bf16[256,128]{1,0:T(8,128)(2,1)}, bf16[256,128]{1,0:T(8,128)(2,1)S(1)}, u32[]{:S(2)}, u32[]{:S(2)}) collective-permute-start(bf16[256,128]{1,0:T(8,128)(2,1)} %get-tuple-element.26), channel_id=1, source_target_pairs={{0,64},{64,0},{128,192},{192,128},{256,320},{320,256},{384,448},{4... | collective-permute-start | bytes 196616 | tf_op jit(solution)/shard_map/ppermute | solution.py:245
  17.2 0.0 copy-start.9
  17.2 0.8 %copy-done.9 = bf16[1,2,128,128]{3,2,1,0:T(8,128)(2,1)S(1)} copy-done((bf16[1,2,128,128]{3,2,1,0:T(8,128)(2,1)S(1)}, bf16[1,2,128,128]{3,2,1,0:T(8,128)(2,1)}, u32[]{:S(2)}) %copy-start.9) | copy-done | bytes 65560
  18.1 3.1 %all-to-all-done.refs_1_ = bf16[8,32,128]{2,1,0:T(8,128)(2,1)S(1)} async-done(((bf16[8,32,128]{2,1,0:T(8,128)(2,1)}), bf16[8,32,128]{2,1,0:T(8,128)(2,1)S(1)}, u32[]{:S(2)}, u32[]{:S(2)}) %all-to-all-start) | async-done | bytes 65568 | tf_op jit(solution)/shard_map/all_to_all | solution.py:249
  21.1 0.3 up.1
  21.5 0.8 %copy-done.2 = bf16[64,32,128]{2,1,0:T(8,128)(2,1)} copy-done((bf16[64,32,128]{2,1,0:T(8,128)(2,1)}, bf16[64,32,128]{2,1,0:T(8,128)(2,1)S(1)}, u32[]{:S(2)}) %copy-start.2) | copy-done | bytes 524312
  22.3 0.6 copy-done.6
  22.9 10.5 %all-to-all-start.1 = ((bf16[64,32,128]{2,1,0:T(8,128)(2,1)}), bf16[64,32,128]{2,1,0:T(8,128)(2,1)S(1)}, u32[]{:S(2)}, u32[]{:S(2)}) async-start(bf16[64,32,128]{2,1,0:T(8,128)(2,1)} %copy-done.2), calls=%async_computation.1 | async-start | bytes 1048576 | tf_op jit(solution)/shard_map/all_to_all | solution.py:257
  33.4 1.6 %pad_maximum_fusion = bf16[2,256,128]{2,1,0:T(8,128)(2,1)} fusion(bf16[1,256,128]{2,1,0:T(8,128)(2,1)} %bitcast.22, bf16[1,256,128]{2,1,0:T(8,128)(2,1)} %bitcast.28), kind=kLoop, calls=%fused_computation | loop fusion | flops 65536 | bytes 262144 | tf_op jit(solution)/shard_map/stack | solution.py:258
  34.9 2.4 %collective-permute-start.3 = (bf16[2,256,128]{2,1,0:T(8,128)(2,1)}, bf16[2,256,128]{2,1,0:T(8,128)(2,1)}, u32[]{:S(2)}, u32[]{:S(2)}) collective-permute-start(bf16[2,256,128]{2,1,0:T(8,128)(2,1)} %pad_maximum_fusion), channel_id=1, source_target_pairs={{0,128},{64,192},{128,0},{192,64},{256,384},{320,448},{384,256},{4... | collective-permute-start | bytes 393224 | tf_op jit(solution)/shard_map/ppermute | solution.py:245
  37.3 5.3 %collective-permute-start.2 = (bf16[2,256,128]{2,1,0:T(8,128)(2,1)}, bf16[2,256,128]{2,1,0:T(8,128)(2,1)}, u32[]{:S(2)}, u32[]{:S(2)}) collective-permute-start(bf16[2,256,128]{2,1,0:T(8,128)(2,1)} %pad_maximum_fusion), channel_id=1, source_target_pairs={{0,384},{64,448},{128,256},{192,320},{256,128},{320,192},{384,0},{... | collective-permute-start | bytes 393224 | tf_op jit(solution)/shard_map/ppermute | solution.py:245
  42.6 3.6 %collective-permute-start.1 = (bf16[2,256,128]{2,1,0:T(8,128)(2,1)}, bf16[2,256,128]{2,1,0:T(8,128)(2,1)}, u32[]{:S(2)}, u32[]{:S(2)}) collective-permute-start(bf16[2,256,128]{2,1,0:T(8,128)(2,1)} %pad_maximum_fusion), channel_id=1, source_target_pairs={{0,320},{64,256},{128,448},{192,384},{256,64},{320,0},{384,192},{4... | collective-permute-start | bytes 393224 | tf_op jit(solution)/shard_map/ppermute | solution.py:245
  46.2 4.9 %all-to-all-done.1.refs_1_ = bf16[64,32,128]{2,1,0:T(8,128)(2,1)S(1)} async-done(((bf16[64,32,128]{2,1,0:T(8,128)(2,1)}), bf16[64,32,128]{2,1,0:T(8,128)(2,1)S(1)}, u32[]{:S(2)}, u32[]{:S(2)}) %all-to-all-start.1) | async-done | bytes 524320 | tf_op jit(solution)/shard_map/all_to_all | solution.py:257
  51.2 0.8 %copy-done.10 = bf16[1,2,128,128]{3,2,1,0:T(8,128)(2,1)S(1)} copy-done((bf16[1,2,128,128]{3,2,1,0:T(8,128)(2,1)S(1)}, bf16[1,2,128,128]{3,2,1,0:T(8,128)(2,1)}, u32[]{:S(2)}) %copy-start.10) | copy-done | bytes 65560
  52.0 0.5 down.1
  52.6 0.6 copy-done.8
  53.2 4.8 %all-to-all-start.2 = ((bf16[8,32,128]{2,1,0:T(8,128)(2,1)}), bf16[8,32,128]{2,1,0:T(8,128)(2,1)S(1)}, u32[]{:S(2)}, u32[]{:S(2)}) async-start(bf16[8,32,128]{2,1,0:T(8,128)(2,1)} %copy-done.8), calls=%async_computation.2 | async-start | bytes 131072 | tf_op jit(solution)/shard_map/all_to_all | solution.py:268
  58.0 0.7 %dense.1.refs_6_ = f32[256,1024]{1,0:T(8,128)S(1)} custom-call(bf16[256,1024]{1,0:T(8,128)(2,1)S(1)} %bitcast.18, bf16[1024,1024]{1,0:T(8,128)(2,1)S(1)} %bitcast.16), custom_call_target="tpu_custom_call" | custom-call | flops 536870912 | bytes 2621440 | tf_op jit(solution)/shard_map/dense/pallas_call | solution.py:39
  58.8 2.7 %local.1 = (f32[256,1024]{1,0:T(8,128)S(1)}, bf16[128,1024]{1,0:T(8,128)(2,1)S(1)}) custom-call(s32[1]{0:T(128)} %step.1.refs_0_, s32[8]{0:T(128)S(1)} %bitcast.26, bf16[256,128]{1,0:T(8,128)(2,1)S(1)} %copy-done.7, bf16[2,256,128]{2,1,0:T(8,128)(2,1)} %collective-permute-done.1.refs_3_, bf16[2,256,128]{2,1,0:T(8,128)(2,1)} %collective-permute-done.2.refs_4_, ...), custom_call_target="tpu_custom_call" | custom-call | flops 67108864 | bytes 2064384 | tf_op jit(solution)/shard_map/local/pallas_call | solution.py:39
  61.5 4.8 %all-to-all-done.2.far_ref = bf16[8,32,128]{2,1,0:T(8,128)(2,1)S(1)} async-done(((bf16[8,32,128]{2,1,0:T(8,128)(2,1)}), bf16[8,32,128]{2,1,0:T(8,128)(2,1)S(1)}, u32[]{:S(2)}, u32[]{:S(2)}) %all-to-all-start.2) | async-done | bytes 65568 | tf_op jit(solution)/shard_map/all_to_all | solution.py:268
  66.4 1.2 %last.1 = f32[256,1024]{1,0:T(8,128)} custom-call(bf16[8,32,128]{2,1,0:T(8,128)(2,1)S(1)} %all-to-all-done.2.far_ref, f32[256,1024]{1,0:T(8,128)S(1)} %get-tuple-element.27.base_ref, bf16[128,1024]{1,0:T(8,128)(2,1)S(1)} %get-tuple-element.28.weight_ref), custom_call_target="tpu_custom_call" | custom-call | flops 67108864 | bytes 2097152 | tf_op jit(solution)/shard_map/last/pallas_call | solution.py:207
  (25 shorter events, 0.1 us)
Async XLA Ops:
  0.0 51.2 %copy-start.3 = (bf16[1,3,4,128,128]{4,3,2,1,0:T(8,128)(2,1)S(1)}, bf16[1,3,4,128,128]{4,3,2,1,0:T(8,128)(2,1)}, u32[]{:S(2)}) copy-start(bf16[1,3,4,128,128]{4,3,2,1,0:T(8,128)(2,1)} %param.21) | copy-start | bytes 1179652
  0.0 58.0 %copy-start = (bf16[1,1,1024,1024]{3,2,1,0:T(8,128)(2,1)S(1)}, bf16[1,1,1024,1024]{3,2,1,0:T(8,128)(2,1)}, u32[]{:S(2)}) copy-start(bf16[1,1,1024,1024]{3,2,1,0:T(8,128)(2,1)} %param.13) | copy-start | bytes 6291460
  0.0 58.0 %copy-start.1 = (bf16[1,1,256,1024]{3,2,1,0:T(8,128)(2,1)S(1)}, bf16[1,1,256,1024]{3,2,1,0:T(8,128)(2,1)}, u32[]{:S(2)}) copy-start(bf16[1,1,256,1024]{3,2,1,0:T(8,128)(2,1)} %param.11) | copy-start | bytes 1572868
  2.4 18.7 %all-to-all-start = ((bf16[8,32,128]{2,1,0:T(8,128)(2,1)}), bf16[8,32,128]{2,1,0:T(8,128)(2,1)S(1)}, u32[]{:S(2)}, u32[]{:S(2)}) async-start(bf16[8,32,128]{2,1,0:T(8,128)(2,1)} %get-tuple-element.18), calls=%async_computation | async-start | bytes 131072 | tf_op jit(solution)/shard_map/all_to_all | solution.py:249
  13.3 9.0 %collective-permute-start = (bf16[256,128]{1,0:T(8,128)(2,1)}, bf16[256,128]{1,0:T(8,128)(2,1)S(1)}, u32[]{:S(2)}, u32[]{:S(2)}) collective-permute-start(bf16[256,128]{1,0:T(8,128)(2,1)} %get-tuple-element.26), channel_id=1, source_target_pairs={{0,64},{64,0},{128,192},{192,128},{256,320},{320,256},{384,448},{4... | collective-permute-start | bytes 196616 | tf_op jit(solution)/shard_map/ppermute | solution.py:245
  17.2 0.8 %copy-start.9 = (bf16[1,2,128,128]{3,2,1,0:T(8,128)(2,1)S(1)}, bf16[1,2,128,128]{3,2,1,0:T(8,128)(2,1)}, u32[]{:S(2)}) copy-start(bf16[1,2,128,128]{3,2,1,0:T(8,128)(2,1)} %param.19) | copy-start | bytes 196612
  21.5 0.8 %copy-start.2 = (bf16[64,32,128]{2,1,0:T(8,128)(2,1)}, bf16[64,32,128]{2,1,0:T(8,128)(2,1)S(1)}, u32[]{:S(2)}) copy-start(bf16[64,32,128]{2,1,0:T(8,128)(2,1)S(1)} %up.1) | copy-start | bytes 1572868
  22.3 0.6 copy-start.6
  22.9 28.3 %all-to-all-start.1 = ((bf16[64,32,128]{2,1,0:T(8,128)(2,1)}), bf16[64,32,128]{2,1,0:T(8,128)(2,1)S(1)}, u32[]{:S(2)}, u32[]{:S(2)}) async-start(bf16[64,32,128]{2,1,0:T(8,128)(2,1)} %copy-done.2), calls=%async_computation.1 | async-start | bytes 1048576 | tf_op jit(solution)/shard_map/all_to_all | solution.py:257
  34.9 23.8 %collective-permute-start.3 = (bf16[2,256,128]{2,1,0:T(8,128)(2,1)}, bf16[2,256,128]{2,1,0:T(8,128)(2,1)}, u32[]{:S(2)}, u32[]{:S(2)}) collective-permute-start(bf16[2,256,128]{2,1,0:T(8,128)(2,1)} %pad_maximum_fusion), channel_id=1, source_target_pairs={{0,128},{64,192},{128,0},{192,64},{256,384},{320,448},{384,256},{4... | collective-permute-start | bytes 393224 | tf_op jit(solution)/shard_map/ppermute | solution.py:245
  37.3 21.4 %collective-permute-start.2 = (bf16[2,256,128]{2,1,0:T(8,128)(2,1)}, bf16[2,256,128]{2,1,0:T(8,128)(2,1)}, u32[]{:S(2)}, u32[]{:S(2)}) collective-permute-start(bf16[2,256,128]{2,1,0:T(8,128)(2,1)} %pad_maximum_fusion), channel_id=1, source_target_pairs={{0,384},{64,448},{128,256},{192,320},{256,128},{320,192},{384,0},{... | collective-permute-start | bytes 393224 | tf_op jit(solution)/shard_map/ppermute | solution.py:245
  42.6 16.1 %collective-permute-start.1 = (bf16[2,256,128]{2,1,0:T(8,128)(2,1)}, bf16[2,256,128]{2,1,0:T(8,128)(2,1)}, u32[]{:S(2)}, u32[]{:S(2)}) collective-permute-start(bf16[2,256,128]{2,1,0:T(8,128)(2,1)} %pad_maximum_fusion), channel_id=1, source_target_pairs={{0,320},{64,256},{128,448},{192,384},{256,64},{320,0},{384,192},{4... | collective-permute-start | bytes 393224 | tf_op jit(solution)/shard_map/ppermute | solution.py:245
  51.2 0.8 %copy-start.10 = (bf16[1,2,128,128]{3,2,1,0:T(8,128)(2,1)S(1)}, bf16[1,2,128,128]{3,2,1,0:T(8,128)(2,1)}, u32[]{:S(2)}) copy-start(bf16[1,2,128,128]{3,2,1,0:T(8,128)(2,1)} %param.20) | copy-start | bytes 196612
  52.6 0.6 copy-start.8
  53.2 5.6 %copy-start.4 = (bf16[1,1,8,128,128]{4,3,2,1,0:T(8,128)(2,1)S(1)}, bf16[1,1,8,128,128]{4,3,2,1,0:T(8,128)(2,1)}, u32[]{:S(2)}) copy-start(bf16[1,1,8,128,128]{4,3,2,1,0:T(8,128)(2,1)} %param.18) | copy-start | bytes 786436
  53.2 5.6 %copy-start.5 = (bf16[1,1,128,1024]{3,2,1,0:T(8,128)(2,1)S(1)}, bf16[1,1,128,1024]{3,2,1,0:T(8,128)(2,1)}, u32[]{:S(2)}) copy-start(bf16[1,1,128,1024]{3,2,1,0:T(8,128)(2,1)} %param.15) | copy-start | bytes 786436
  53.2 5.6 %copy-start.7 = (bf16[256,128]{1,0:T(8,128)(2,1)S(1)}, bf16[256,128]{1,0:T(8,128)(2,1)}, u32[]{:S(2)}) copy-start(bf16[256,128]{1,0:T(8,128)(2,1)} %copy-done.6) | copy-start | bytes 196612
  53.2 5.6 %copy-start.11 = (bf16[1,1,128,128]{3,2,1,0:T(8,128)(2,1)S(1)}, bf16[1,1,128,128]{3,2,1,0:T(8,128)(2,1)}, u32[]{:S(2)}) copy-start(bf16[1,1,128,128]{3,2,1,0:T(8,128)(2,1)} %param.17) | copy-start | bytes 98308
  53.2 5.6 %copy-start.12 = (s32[1,8]{1,0:T(1,128)S(1)}, s32[1,8]{1,0:T(1,128)}, u32[]{:S(2)}) copy-start(s32[1,8]{1,0:T(1,128)} %param.12) | copy-start | bytes 100
  53.2 13.1 %all-to-all-start.2 = ((bf16[8,32,128]{2,1,0:T(8,128)(2,1)}), bf16[8,32,128]{2,1,0:T(8,128)(2,1)S(1)}, u32[]{:S(2)}, u32[]{:S(2)}) async-start(bf16[8,32,128]{2,1,0:T(8,128)(2,1)} %copy-done.8), calls=%async_computation.2 | async-start | bytes 131072 | tf_op jit(solution)/shard_map/all_to_all | solution.py:268

commit v7 on v4

--- a/solution.py
+++ b/solution.py
@@ -104,20 +104,6 @@
     )(models, leaf_in, leaf_up)
 
 
-def step_kernel(leaf_ref, same_ref):
-    same_ref[0] = leaf_ref[0]
-
-
-def step_call(leaf):
-    return pl.pallas_call(
-        step_kernel,
-        out_shape=jax.ShapeDtypeStruct(leaf.shape, leaf.dtype),
-        in_specs=[pl.BlockSpec(memory_space=pltpu.SMEM)],
-        out_specs=pl.BlockSpec(memory_space=pltpu.SMEM),
-        name="step",
-    )(leaf)
-
-
 def hold_kernel(upper_up_ref, held_ref):
     held_ref[...] = upper_up_ref[...]
 
@@ -249,9 +235,8 @@
         return lax.ppermute(x, "leaf", [(k, k ^ step) for k in range(n_leaf)])
 
     lifted, skeleton = first_call(inputs, leaf_in[0, 0], leaf_up[0, 0], n_leaf)
-    lifted, upper_up, leaf = lax.optimization_barrier((lifted, upper_up, leaf))
+    lifted, upper_up = lax.optimization_barrier((lifted, upper_up))
     parts = lax.all_to_all(lifted, "leaf", 0, 0, tiled=True)
-    leaf, skeleton = lax.optimization_barrier((step_call(leaf), skeleton))
     following = partner(skeleton, 1)
     (ups,) = call(hold_kernel, [(upper_up.shape[1:], BF)], [], [upper_up[0]], name="hold")
     (sent,) = call(

time: 66.5 us -> 65.9 us (level)
  waiting for transfers between devices: 10.6 us -> 11.7 us
  Pallas kernels: 8.37 us -> 7.32 us
  transfers between devices with their start and end apart: 7 -> 7, of which waited for: 3 -> 3; matrix products, arithmetic and copies ran while one was open for 2% -> 2% of each run, Pallas kernels for 7% -> 6%
where the time goes in v7:
time: 65.9 us; the launch traced here: 65.3 us
  starting transfers between devices  40.4 us (61%)
  waiting for transfers between devices  11.7 us (18%)
  Pallas kernels  7.32 us (11%)
  local copies, waits for them, and re-layouts  4.11 us (6%)
  other arithmetic  1.49 us (2%)
    ppermute x4, starting transfers between devices, partner(): return lax.ppermute(x, 'leaf', [(k, k ^ step) for k in range(n_leaf)])  15.2 us
    all_to_all x1, starting transfers between devices, shards(): parts = lax.all_to_all(lifted, 'leaf', 0, 0, tiled=True)  10.5 us
    all_to_all x1, starting transfers between devices, shards(): heard = lax.all_to_all(sent, 'wide', 0, 0, tiled=True)  10.5 us
    all_to_all x1, waiting for transfers between devices, shards(): far = lax.all_to_all(far, 'leaf', 0, 0, tiled=True)  5.38 us
    all_to_all x1, starting transfers between devices, shards(): far = lax.all_to_all(far, 'leaf', 0, 0, tiled=True)  4.22 us
    unnamed x26, local copies, waits for them, and re-layouts  4.11 us
    pallas_call x6, Pallas kernels, call(): pl.pallas_call(kernel, out_shape=[jax.ShapeDtypeStruct(s, t) for s, t in...  3.86 us
    all_to_all x1, waiting for transfers between devices, shards(): parts = lax.all_to_all(lifted, 'leaf', 0, 0, tiled=True)  3.58 us
  transfers between devices with their start and end apart: 7, of which 3 were waited for; matrix products, arithmetic and copies ran while one was open for 2% of the time, Pallas kernels for 6%

profile of v7, /device:TPU:16, one launch (start us, length us, event | category | flops | bytes accessed | tf_op | source)
XLA Modules:
  0.0 65.3 jit_solution(12852988830522773480)
XLA Ops:
  0.0 2.3 %first.1 = (bf16[8,32,128]{2,1,0:T(8,128)(2,1)}, bf16[256,128]{1,0:T(8,128)(2,1)}) custom-call(bf16[256,1024]{1,0:T(8,128)(2,1)} %bitcast.17, bf16[1024,128]{1,0:T(8,128)(2,1)} %bitcast.27, bf16[128,128]{1,0:T(8,128)(2,1)} %bitcast.29), custom_call_target="tpu_custom_call" | custom-call | flops 67108864 | bytes 524288 | tf_op jit(solution)/shard_map/first/pallas_call | solution.py:89
  2.3 10.5 %all-to-all-start = ((bf16[8,32,128]{2,1,0:T(8,128)(2,1)}), bf16[8,32,128]{2,1,0:T(8,128)(2,1)S(1)}, u32[]{:S(2)}, u32[]{:S(2)}) async-start(bf16[8,32,128]{2,1,0:T(8,128)(2,1)} %get-tuple-element.16), calls=%async_computation | async-start | bytes 131072 | tf_op jit(solution)/shard_map/all_to_all | solution.py:239
  12.8 3.9 %collective-permute-start = (bf16[256,128]{1,0:T(8,128)(2,1)}, bf16[256,128]{1,0:T(8,128)(2,1)S(1)}, u32[]{:S(2)}, u32[]{:S(2)}) collective-permute-start(bf16[256,128]{1,0:T(8,128)(2,1)} %get-tuple-element.22), channel_id=1, source_target_pairs={{0,64},{64,0},{128,192},{192,128},{256,320},{320,256},{384,448},{4... | collective-permute-start | bytes 196616 | tf_op jit(solution)/shard_map/ppermute | solution.py:235
  16.7 0.0 copy-start.9
  16.7 0.8 %copy-done.9 = bf16[1,2,128,128]{3,2,1,0:T(8,128)(2,1)S(1)} copy-done((bf16[1,2,128,128]{3,2,1,0:T(8,128)(2,1)S(1)}, bf16[1,2,128,128]{3,2,1,0:T(8,128)(2,1)}, u32[]{:S(2)}) %copy-start.9) | copy-done | bytes 65560
  17.6 3.6 %all-to-all-done.refs_1_ = bf16[8,32,128]{2,1,0:T(8,128)(2,1)S(1)} async-done(((bf16[8,32,128]{2,1,0:T(8,128)(2,1)}), bf16[8,32,128]{2,1,0:T(8,128)(2,1)S(1)}, u32[]{:S(2)}, u32[]{:S(2)}) %all-to-all-start) | async-done | bytes 65568 | tf_op jit(solution)/shard_map/all_to_all | solution.py:239
  21.1 0.3 up.1
  21.5 0.8 %copy-done.2 = bf16[64,32,128]{2,1,0:T(8,128)(2,1)} copy-done((bf16[64,32,128]{2,1,0:T(8,128)(2,1)}, bf16[64,32,128]{2,1,0:T(8,128)(2,1)S(1)}, u32[]{:S(2)}) %copy-start.2) | copy-done | bytes 524312
  22.3 10.5 %all-to-all-start.1 = ((bf16[64,32,128]{2,1,0:T(8,128)(2,1)}), bf16[64,32,128]{2,1,0:T(8,128)(2,1)S(1)}, u32[]{:S(2)}, u32[]{:S(2)}) async-start(bf16[64,32,128]{2,1,0:T(8,128)(2,1)} %copy-done.2), calls=%async_computation.1 | async-start | bytes 1048576 | tf_op jit(solution)/shard_map/all_to_all | solution.py:248
  32.7 1.5 %pad_maximum_fusion = bf16[2,256,128]{2,1,0:T(8,128)(2,1)} fusion(bf16[1,256,128]{2,1,0:T(8,128)(2,1)S(1)} %bitcast.22, bf16[1,256,128]{2,1,0:T(8,128)(2,1)} %bitcast.28), kind=kLoop, calls=%fused_computation | loop fusion | flops 65536 | bytes 262144 | tf_op jit(solution)/shard_map/stack | solution.py:249
  34.2 2.4 %collective-permute-start.3 = (bf16[2,256,128]{2,1,0:T(8,128)(2,1)}, bf16[2,256,128]{2,1,0:T(8,128)(2,1)}, u32[]{:S(2)}, u32[]{:S(2)}) collective-permute-start(bf16[2,256,128]{2,1,0:T(8,128)(2,1)} %pad_maximum_fusion), channel_id=1, source_target_pairs={{0,128},{64,192},{128,0},{192,64},{256,384},{320,448},{384,256},{4... | collective-permute-start | bytes 393224 | tf_op jit(solution)/shard_map/ppermute | solution.py:235
  36.6 4.8 %collective-permute-start.2 = (bf16[2,256,128]{2,1,0:T(8,128)(2,1)}, bf16[2,256,128]{2,1,0:T(8,128)(2,1)}, u32[]{:S(2)}, u32[]{:S(2)}) collective-permute-start(bf16[2,256,128]{2,1,0:T(8,128)(2,1)} %pad_maximum_fusion), channel_id=1, source_target_pairs={{0,384},{64,448},{128,256},{192,320},{256,128},{320,192},{384,0},{... | collective-permute-start | bytes 393224 | tf_op jit(solution)/shard_map/ppermute | solution.py:235
  41.4 4.2 %collective-permute-start.1 = (bf16[2,256,128]{2,1,0:T(8,128)(2,1)}, bf16[2,256,128]{2,1,0:T(8,128)(2,1)}, u32[]{:S(2)}, u32[]{:S(2)}) collective-permute-start(bf16[2,256,128]{2,1,0:T(8,128)(2,1)} %pad_maximum_fusion), channel_id=1, source_target_pairs={{0,320},{64,256},{128,448},{192,384},{256,64},{320,0},{384,192},{4... | collective-permute-start | bytes 393224 | tf_op jit(solution)/shard_map/ppermute | solution.py:235
  45.6 1.0 %copy-done.3 = bf16[1,3,4,128,128]{4,3,2,1,0:T(8,128)(2,1)S(1)} copy-done((bf16[1,3,4,128,128]{4,3,2,1,0:T(8,128)(2,1)S(1)}, bf16[1,3,4,128,128]{4,3,2,1,0:T(8,128)(2,1)}, u32[]{:S(2)}) %copy-start.3) | copy-done | bytes 393240
  46.6 0.8 %copy-done.10 = bf16[1,2,128,128]{3,2,1,0:T(8,128)(2,1)S(1)} copy-done((bf16[1,2,128,128]{3,2,1,0:T(8,128)(2,1)S(1)}, bf16[1,2,128,128]{3,2,1,0:T(8,128)(2,1)}, u32[]{:S(2)}) %copy-start.10) | copy-done | bytes 65560
  47.4 0.4 fold.1.refs_2_
  47.8 2.7 %all-to-all-done.1.refs_1_ = bf16[64,32,128]{2,1,0:T(8,128)(2,1)S(1)} async-done(((bf16[64,32,128]{2,1,0:T(8,128)(2,1)}), bf16[64,32,128]{2,1,0:T(8,128)(2,1)S(1)}, u32[]{:S(2)}, u32[]{:S(2)}) %all-to-all-start.1) | async-done | bytes 524320 | tf_op jit(solution)/shard_map/all_to_all | solution.py:248
  50.5 0.3 down.1
  50.8 0.6 copy-done.6
  51.5 4.2 %all-to-all-start.2 = ((bf16[8,32,128]{2,1,0:T(8,128)(2,1)}), bf16[8,32,128]{2,1,0:T(8,128)(2,1)S(1)}, u32[]{:S(2)}, u32[]{:S(2)}) async-start(bf16[8,32,128]{2,1,0:T(8,128)(2,1)} %copy-done.6), calls=%async_computation.2 | async-start | bytes 131072 | tf_op jit(solution)/shard_map/all_to_all | solution.py:263
  55.7 0.7 %dense.1.refs_6_ = f32[256,1024]{1,0:T(8,128)S(1)} custom-call(bf16[256,1024]{1,0:T(8,128)(2,1)S(1)} %bitcast.18, bf16[1024,1024]{1,0:T(8,128)(2,1)S(1)} %bitcast.16), custom_call_target="tpu_custom_call" | custom-call | flops 536870912 | bytes 2621440 | tf_op jit(solution)/shard_map/dense/pallas_call | solution.py:39
  56.5 2.2 %local.1 = (f32[256,1024]{1,0:T(8,128)S(1)}, bf16[128,1024]{1,0:T(8,128)(2,1)S(1)}) custom-call(s32[1]{0:T(128)} %bitcast.7.refs_0_, s32[8]{0:T(128)S(1)} %bitcast.26, bf16[256,128]{1,0:T(8,128)(2,1)S(1)} %copy-done.8, bf16[2,256,128]{2,1,0:T(8,128)(2,1)} %collective-permute-done.1.refs_3_, bf16[2,256,128]{2,1,0:T(8,128)(2,1)} %collective-permute-done.2.refs_4_, ...), custom_call_target="tpu_custom_call" | custom-call | flops 67108864 | bytes 2064384 | tf_op jit(solution)/shard_map/local/pallas_call | solution.py:39
  58.7 5.4 %all-to-all-done.2.far_ref = bf16[8,32,128]{2,1,0:T(8,128)(2,1)S(1)} async-done(((bf16[8,32,128]{2,1,0:T(8,128)(2,1)}), bf16[8,32,128]{2,1,0:T(8,128)(2,1)S(1)}, u32[]{:S(2)}, u32[]{:S(2)}) %all-to-all-start.2) | async-done | bytes 65568 | tf_op jit(solution)/shard_map/all_to_all | solution.py:263
  64.1 1.2 %last.1 = f32[256,1024]{1,0:T(8,128)} custom-call(bf16[8,32,128]{2,1,0:T(8,128)(2,1)S(1)} %all-to-all-done.2.far_ref, f32[256,1024]{1,0:T(8,128)S(1)} %get-tuple-element.23.base_ref, bf16[128,1024]{1,0:T(8,128)(2,1)S(1)} %get-tuple-element.24.weight_ref), custom_call_target="tpu_custom_call" | custom-call | flops 67108864 | bytes 2097152 | tf_op jit(solution)/shard_map/last/pallas_call | solution.py:197
  (25 shorter events, 0.1 us)
Async XLA Ops:
  2.3 53.4 %copy-start = (bf16[1,1,1024,1024]{3,2,1,0:T(8,128)(2,1)S(1)}, bf16[1,1,1024,1024]{3,2,1,0:T(8,128)(2,1)}, u32[]{:S(2)}) copy-start(bf16[1,1,1024,1024]{3,2,1,0:T(8,128)(2,1)} %param.13) | copy-start | bytes 6291460
  2.3 53.4 %copy-start.1 = (bf16[1,1,256,1024]{3,2,1,0:T(8,128)(2,1)S(1)}, bf16[1,1,256,1024]{3,2,1,0:T(8,128)(2,1)}, u32[]{:S(2)}) copy-start(bf16[1,1,256,1024]{3,2,1,0:T(8,128)(2,1)} %param.11) | copy-start | bytes 1572868
  2.3 18.8 %all-to-all-start = ((bf16[8,32,128]{2,1,0:T(8,128)(2,1)}), bf16[8,32,128]{2,1,0:T(8,128)(2,1)S(1)}, u32[]{:S(2)}, u32[]{:S(2)}) async-start(bf16[8,32,128]{2,1,0:T(8,128)(2,1)} %get-tuple-element.16), calls=%async_computation | async-start | bytes 131072 | tf_op jit(solution)/shard_map/all_to_all | solution.py:239
  12.8 9.5 %collective-permute-start = (bf16[256,128]{1,0:T(8,128)(2,1)}, bf16[256,128]{1,0:T(8,128)(2,1)S(1)}, u32[]{:S(2)}, u32[]{:S(2)}) collective-permute-start(bf16[256,128]{1,0:T(8,128)(2,1)} %get-tuple-element.22), channel_id=1, source_target_pairs={{0,64},{64,0},{128,192},{192,128},{256,320},{320,256},{384,448},{4... | collective-permute-start | bytes 196616 | tf_op jit(solution)/shard_map/ppermute | solution.py:235
  16.7 0.8 %copy-start.9 = (bf16[1,2,128,128]{3,2,1,0:T(8,128)(2,1)S(1)}, bf16[1,2,128,128]{3,2,1,0:T(8,128)(2,1)}, u32[]{:S(2)}) copy-start(bf16[1,2,128,128]{3,2,1,0:T(8,128)(2,1)} %param.19) | copy-start | bytes 196612
  21.4 0.8 %copy-start.2 = (bf16[64,32,128]{2,1,0:T(8,128)(2,1)}, bf16[64,32,128]{2,1,0:T(8,128)(2,1)S(1)}, u32[]{:S(2)}) copy-start(bf16[64,32,128]{2,1,0:T(8,128)(2,1)S(1)} %up.1) | copy-start | bytes 1572868
  22.2 23.3 %copy-start.7 = (bf16[256,128]{1,0:T(8,128)(2,1)}, bf16[256,128]{1,0:T(8,128)(2,1)S(1)}, u32[]{:S(2)}) copy-start(bf16[256,128]{1,0:T(8,128)(2,1)S(1)} %collective-permute-done.refs_2_) | copy-start | bytes 196612
  22.3 28.3 %all-to-all-start.1 = ((bf16[64,32,128]{2,1,0:T(8,128)(2,1)}), bf16[64,32,128]{2,1,0:T(8,128)(2,1)S(1)}, u32[]{:S(2)}, u32[]{:S(2)}) async-start(bf16[64,32,128]{2,1,0:T(8,128)(2,1)} %copy-done.2), calls=%async_computation.1 | async-start | bytes 1048576 | tf_op jit(solution)/shard_map/all_to_all | solution.py:248
  34.2 22.2 %collective-permute-start.3 = (bf16[2,256,128]{2,1,0:T(8,128)(2,1)}, bf16[2,256,128]{2,1,0:T(8,128)(2,1)}, u32[]{:S(2)}, u32[]{:S(2)}) collective-permute-start(bf16[2,256,128]{2,1,0:T(8,128)(2,1)} %pad_maximum_fusion), channel_id=1, source_target_pairs={{0,128},{64,192},{128,0},{192,64},{256,384},{320,448},{384,256},{4... | collective-permute-start | bytes 393224 | tf_op jit(solution)/shard_map/ppermute | solution.py:235
  36.6 19.8 %collective-permute-start.2 = (bf16[2,256,128]{2,1,0:T(8,128)(2,1)}, bf16[2,256,128]{2,1,0:T(8,128)(2,1)}, u32[]{:S(2)}, u32[]{:S(2)}) collective-permute-start(bf16[2,256,128]{2,1,0:T(8,128)(2,1)} %pad_maximum_fusion), channel_id=1, source_target_pairs={{0,384},{64,448},{128,256},{192,320},{256,128},{320,192},{384,0},{... | collective-permute-start | bytes 393224 | tf_op jit(solution)/shard_map/ppermute | solution.py:235
  41.4 15.1 %collective-permute-start.1 = (bf16[2,256,128]{2,1,0:T(8,128)(2,1)}, bf16[2,256,128]{2,1,0:T(8,128)(2,1)}, u32[]{:S(2)}, u32[]{:S(2)}) collective-permute-start(bf16[2,256,128]{2,1,0:T(8,128)(2,1)} %pad_maximum_fusion), channel_id=1, source_target_pairs={{0,320},{64,256},{128,448},{192,384},{256,64},{320,0},{384,192},{4... | collective-permute-start | bytes 393224 | tf_op jit(solution)/shard_map/ppermute | solution.py:235
  45.6 1.0 %copy-start.3 = (bf16[1,3,4,128,128]{4,3,2,1,0:T(8,128)(2,1)S(1)}, bf16[1,3,4,128,128]{4,3,2,1,0:T(8,128)(2,1)}, u32[]{:S(2)}) copy-start(bf16[1,3,4,128,128]{4,3,2,1,0:T(8,128)(2,1)} %param.21) | copy-start | bytes 1179652
  46.6 0.8 %copy-start.10 = (bf16[1,2,128,128]{3,2,1,0:T(8,128)(2,1)S(1)}, bf16[1,2,128,128]{3,2,1,0:T(8,128)(2,1)}, u32[]{:S(2)}) copy-start(bf16[1,2,128,128]{3,2,1,0:T(8,128)(2,1)} %param.20) | copy-start | bytes 196612
  50.8 0.6 copy-start.6
  51.4 5.0 %copy-start.4 = (bf16[1,1,8,128,128]{4,3,2,1,0:T(8,128)(2,1)S(1)}, bf16[1,1,8,128,128]{4,3,2,1,0:T(8,128)(2,1)}, u32[]{:S(2)}) copy-start(bf16[1,1,8,128,128]{4,3,2,1,0:T(8,128)(2,1)} %param.18) | copy-start | bytes 786436
  51.4 5.0 %copy-start.5 = (bf16[1,1,128,1024]{3,2,1,0:T(8,128)(2,1)S(1)}, bf16[1,1,128,1024]{3,2,1,0:T(8,128)(2,1)}, u32[]{:S(2)}) copy-start(bf16[1,1,128,1024]{3,2,1,0:T(8,128)(2,1)} %param.15) | copy-start | bytes 786436
  51.5 5.0 %copy-start.8 = (bf16[256,128]{1,0:T(8,128)(2,1)S(1)}, bf16[256,128]{1,0:T(8,128)(2,1)}, u32[]{:S(2)}) copy-start(bf16[256,128]{1,0:T(8,128)(2,1)} %copy-done.7) | copy-start | bytes 196612
  51.5 5.0 %copy-start.11 = (bf16[1,1,128,128]{3,2,1,0:T(8,128)(2,1)S(1)}, bf16[1,1,128,128]{3,2,1,0:T(8,128)(2,1)}, u32[]{:S(2)}) copy-start(bf16[1,1,128,128]{3,2,1,0:T(8,128)(2,1)} %param.17) | copy-start | bytes 98308
  51.5 5.0 %copy-start.12 = (s32[1,8]{1,0:T(1,128)S(1)}, s32[1,8]{1,0:T(1,128)}, u32[]{:S(2)}) copy-start(s32[1,8]{1,0:T(1,128)} %param.12) | copy-start | bytes 100
  51.5 12.6 %all-to-all-start.2 = ((bf16[8,32,128]{2,1,0:T(8,128)(2,1)}), bf16[8,32,128]{2,1,0:T(8,128)(2,1)S(1)}, u32[]{:S(2)}, u32[]{:S(2)}) async-start(bf16[8,32,128]{2,1,0:T(8,128)(2,1)} %copy-done.6), calls=%async_computation.2 | async-start | bytes 131072 | tf_op jit(solution)/shard_map/all_to_all | solution.py:263

commit v8 on v7

--- a/solution.py
+++ b/solution.py
@@ -121,8 +121,8 @@
         sent_ref[wide // 4 * 4 + k] = own
 
 
-def fold_kernel(couple_ref, upper_down, folded_ref):
-    down_ref = upper_down()
+def fold_kernel(upper_couple, upper_down, folded_ref):
+    couple_ref, down_ref = upper_couple(), upper_down()
     r = down_ref.shape[-1]
     flat = (4 * r, r)
     folded_ref[0] = couple_ref[0]
@@ -252,8 +252,8 @@
         fold_kernel,
         [(upper_couple.shape[1:], BF)],
         [],
-        [upper_couple[0]],
-        [upper_down[0]],
+        [],
+        [upper_couple[0], upper_down[0]],
         flops=24 * r * r * r,
         name="fold",
     )

time: 65.9 us -> 65.9 us (level)
  no operation moved by 1% of the time
where the time goes in v8:
time: 65.9 us; the launch traced here: 65.3 us
  starting transfers between devices  40.4 us (61%)
  waiting for transfers between devices  11.5 us (17%)
  Pallas kernels  7.54 us (11%)
  local copies, waits for them, and re-layouts  4.11 us (6%)
  other arithmetic  1.49 us (2%)
    ppermute x4, starting transfers between devices, partner(): return lax.ppermute(x, 'leaf', [(k, k ^ step) for k in range(n_leaf)])  15.2 us
    all_to_all x1, starting transfers between devices, shards(): parts = lax.all_to_all(lifted, 'leaf', 0, 0, tiled=True)  10.5 us
    all_to_all x1, starting transfers between devices, shards(): heard = lax.all_to_all(sent, 'wide', 0, 0, tiled=True)  10.5 us
    all_to_all x1, waiting for transfers between devices, shards(): far = lax.all_to_all(far, 'leaf', 0, 0, tiled=True)  5.38 us
    all_to_all x1, starting transfers between devices, shards(): far = lax.all_to_all(far, 'leaf', 0, 0, tiled=True)  4.22 us
    unnamed x26, local copies, waits for them, and re-layouts  4.11 us
    pallas_call x6, Pallas kernels, call(): pl.pallas_call(kernel, out_shape=[jax.ShapeDtypeStruct(s, t) for s, t in...  4.08 us
    all_to_all x1, waiting for transfers between devices, shards(): parts = lax.all_to_all(lifted, 'leaf', 0, 0, tiled=True)  3.58 us
  transfers between devices with their start and end apart: 7, of which 3 were waited for; matrix products, arithmetic and copies ran while one was open for 2% of the time, Pallas kernels for 6%

profile of v8, /device:TPU:16, one launch (start us, length us, event | category | flops | bytes accessed | tf_op | source)
XLA Modules:
  0.0 65.3 jit_solution(4776763576533760389)
XLA Ops:
  0.0 2.3 %first.1 = (bf16[8,32,128]{2,1,0:T(8,128)(2,1)}, bf16[256,128]{1,0:T(8,128)(2,1)}) custom-call(bf16[256,1024]{1,0:T(8,128)(2,1)} %bitcast.17, bf16[1024,128]{1,0:T(8,128)(2,1)} %bitcast.27, bf16[128,128]{1,0:T(8,128)(2,1)} %bitcast.29), custom_call_target="tpu_custom_call" | custom-call | flops 67108864 | bytes 524288 | tf_op jit(solution)/shard_map/first/pallas_call | solution.py:89
  2.3 0.0 copy-start
  2.3 10.5 %all-to-all-start = ((bf16[8,32,128]{2,1,0:T(8,128)(2,1)}), bf16[8,32,128]{2,1,0:T(8,128)(2,1)S(1)}, u32[]{:S(2)}, u32[]{:S(2)}) async-start(bf16[8,32,128]{2,1,0:T(8,128)(2,1)} %get-tuple-element.16), calls=%async_computation | async-start | bytes 131072 | tf_op jit(solution)/shard_map/all_to_all | solution.py:239
  12.8 3.9 %collective-permute-start = (bf16[256,128]{1,0:T(8,128)(2,1)}, bf16[256,128]{1,0:T(8,128)(2,1)S(1)}, u32[]{:S(2)}, u32[]{:S(2)}) collective-permute-start(bf16[256,128]{1,0:T(8,128)(2,1)} %get-tuple-element.22), channel_id=1, source_target_pairs={{0,64},{64,0},{128,192},{192,128},{256,320},{320,256},{384,448},{4... | collective-permute-start | bytes 196616 | tf_op jit(solution)/shard_map/ppermute | solution.py:235
  16.7 0.8 %copy-done.9 = bf16[1,2,128,128]{3,2,1,0:T(8,128)(2,1)S(1)} copy-done((bf16[1,2,128,128]{3,2,1,0:T(8,128)(2,1)S(1)}, bf16[1,2,128,128]{3,2,1,0:T(8,128)(2,1)}, u32[]{:S(2)}) %copy-start.9) | copy-done | bytes 65560
  17.6 3.6 %all-to-all-done.refs_1_ = bf16[8,32,128]{2,1,0:T(8,128)(2,1)S(1)} async-done(((bf16[8,32,128]{2,1,0:T(8,128)(2,1)}), bf16[8,32,128]{2,1,0:T(8,128)(2,1)S(1)}, u32[]{:S(2)}, u32[]{:S(2)}) %all-to-all-start) | async-done | bytes 65568 | tf_op jit(solution)/shard_map/all_to_all | solution.py:239
  21.1 0.3 up.1
  21.5 0.8 %copy-done.2 = bf16[64,32,128]{2,1,0:T(8,128)(2,1)} copy-done((bf16[64,32,128]{2,1,0:T(8,128)(2,1)}, bf16[64,32,128]{2,1,0:T(8,128)(2,1)S(1)}, u32[]{:S(2)}) %copy-start.2) | copy-done | bytes 524312
  22.3 10.5 %all-to-all-start.1 = ((bf16[64,32,128]{2,1,0:T(8,128)(2,1)}), bf16[64,32,128]{2,1,0:T(8,128)(2,1)S(1)}, u32[]{:S(2)}, u32[]{:S(2)}) async-start(bf16[64,32,128]{2,1,0:T(8,128)(2,1)} %copy-done.2), calls=%async_computation.1 | async-start | bytes 1048576 | tf_op jit(solution)/shard_map/all_to_all | solution.py:248
  32.7 1.5 %pad_maximum_fusion = bf16[2,256,128]{2,1,0:T(8,128)(2,1)} fusion(bf16[1,256,128]{2,1,0:T(8,128)(2,1)S(1)} %bitcast.22, bf16[1,256,128]{2,1,0:T(8,128)(2,1)} %bitcast.28), kind=kLoop, calls=%fused_computation | loop fusion | flops 65536 | bytes 262144 | tf_op jit(solution)/shard_map/stack | solution.py:249
  34.2 2.4 %collective-permute-start.3 = (bf16[2,256,128]{2,1,0:T(8,128)(2,1)}, bf16[2,256,128]{2,1,0:T(8,128)(2,1)}, u32[]{:S(2)}, u32[]{:S(2)}) collective-permute-start(bf16[2,256,128]{2,1,0:T(8,128)(2,1)} %pad_maximum_fusion), channel_id=1, source_target_pairs={{0,128},{64,192},{128,0},{192,64},{256,384},{320,448},{384,256},{4... | collective-permute-start | bytes 393224 | tf_op jit(solution)/shard_map/ppermute | solution.py:235
  36.6 4.8 %collective-permute-start.2 = (bf16[2,256,128]{2,1,0:T(8,128)(2,1)}, bf16[2,256,128]{2,1,0:T(8,128)(2,1)}, u32[]{:S(2)}, u32[]{:S(2)}) collective-permute-start(bf16[2,256,128]{2,1,0:T(8,128)(2,1)} %pad_maximum_fusion), channel_id=1, source_target_pairs={{0,384},{64,448},{128,256},{192,320},{256,128},{320,192},{384,0},{... | collective-permute-start | bytes 393224 | tf_op jit(solution)/shard_map/ppermute | solution.py:235
  41.4 4.2 %collective-permute-start.1 = (bf16[2,256,128]{2,1,0:T(8,128)(2,1)}, bf16[2,256,128]{2,1,0:T(8,128)(2,1)}, u32[]{:S(2)}, u32[]{:S(2)}) collective-permute-start(bf16[2,256,128]{2,1,0:T(8,128)(2,1)} %pad_maximum_fusion), channel_id=1, source_target_pairs={{0,320},{64,256},{128,448},{192,384},{256,64},{320,0},{384,192},{4... | collective-permute-start | bytes 393224 | tf_op jit(solution)/shard_map/ppermute | solution.py:235
  45.6 1.0 %copy-done.3 = bf16[1,3,4,128,128]{4,3,2,1,0:T(8,128)(2,1)S(1)} copy-done((bf16[1,3,4,128,128]{4,3,2,1,0:T(8,128)(2,1)S(1)}, bf16[1,3,4,128,128]{4,3,2,1,0:T(8,128)(2,1)}, u32[]{:S(2)}) %copy-start.3) | copy-done | bytes 393240
  46.6 0.8 %copy-done.10 = bf16[1,2,128,128]{3,2,1,0:T(8,128)(2,1)S(1)} copy-done((bf16[1,2,128,128]{3,2,1,0:T(8,128)(2,1)S(1)}, bf16[1,2,128,128]{3,2,1,0:T(8,128)(2,1)}, u32[]{:S(2)}) %copy-start.10) | copy-done | bytes 65560
  47.4 0.6 fold.1.refs_2_
  48.0 2.5 %all-to-all-done.1.refs_1_ = bf16[64,32,128]{2,1,0:T(8,128)(2,1)S(1)} async-done(((bf16[64,32,128]{2,1,0:T(8,128)(2,1)}), bf16[64,32,128]{2,1,0:T(8,128)(2,1)S(1)}, u32[]{:S(2)}, u32[]{:S(2)}) %all-to-all-start.1) | async-done | bytes 524320 | tf_op jit(solution)/shard_map/all_to_all | solution.py:248
  50.5 0.3 down.1
  50.8 0.6 copy-done.6
  51.5 4.2 %all-to-all-start.2 = ((bf16[8,32,128]{2,1,0:T(8,128)(2,1)}), bf16[8,32,128]{2,1,0:T(8,128)(2,1)S(1)}, u32[]{:S(2)}, u32[]{:S(2)}) async-start(bf16[8,32,128]{2,1,0:T(8,128)(2,1)} %copy-done.6), calls=%async_computation.2 | async-start | bytes 131072 | tf_op jit(solution)/shard_map/all_to_all | solution.py:263
  55.7 0.7 %dense.1.refs_6_ = f32[256,1024]{1,0:T(8,128)S(1)} custom-call(bf16[256,1024]{1,0:T(8,128)(2,1)S(1)} %bitcast.18, bf16[1024,1024]{1,0:T(8,128)(2,1)S(1)} %bitcast.16), custom_call_target="tpu_custom_call" | custom-call | flops 536870912 | bytes 2621440 | tf_op jit(solution)/shard_map/dense/pallas_call | solution.py:39
  56.5 2.2 %local.1 = (f32[256,1024]{1,0:T(8,128)S(1)}, bf16[128,1024]{1,0:T(8,128)(2,1)S(1)}) custom-call(s32[1]{0:T(128)} %bitcast.7.refs_0_, s32[8]{0:T(128)S(1)} %bitcast.26, bf16[256,128]{1,0:T(8,128)(2,1)S(1)} %copy-done.8, bf16[2,256,128]{2,1,0:T(8,128)(2,1)} %collective-permute-done.1.refs_3_, bf16[2,256,128]{2,1,0:T(8,128)(2,1)} %collective-permute-done.2.refs_4_, ...), custom_call_target="tpu_custom_call" | custom-call | flops 67108864 | bytes 2064384 | tf_op jit(solution)/shard_map/local/pallas_call | solution.py:39
  58.7 5.4 %all-to-all-done.2.far_ref = bf16[8,32,128]{2,1,0:T(8,128)(2,1)S(1)} async-done(((bf16[8,32,128]{2,1,0:T(8,128)(2,1)}), bf16[8,32,128]{2,1,0:T(8,128)(2,1)S(1)}, u32[]{:S(2)}, u32[]{:S(2)}) %all-to-all-start.2) | async-done | bytes 65568 | tf_op jit(solution)/shard_map/all_to_all | solution.py:263
  64.1 1.2 %last.1 = f32[256,1024]{1,0:T(8,128)} custom-call(bf16[8,32,128]{2,1,0:T(8,128)(2,1)S(1)} %all-to-all-done.2.far_ref, f32[256,1024]{1,0:T(8,128)S(1)} %get-tuple-element.23.base_ref, bf16[128,1024]{1,0:T(8,128)(2,1)S(1)} %get-tuple-element.24.weight_ref), custom_call_target="tpu_custom_call" | custom-call | flops 67108864 | bytes 2097152 | tf_op jit(solution)/shard_map/last/pallas_call | solution.py:197
  (25 shorter events, 0.1 us)
Async XLA Ops:
  2.3 53.4 %copy-start = (bf16[1,1,1024,1024]{3,2,1,0:T(8,128)(2,1)S(1)}, bf16[1,1,1024,1024]{3,2,1,0:T(8,128)(2,1)}, u32[]{:S(2)}) copy-start(bf16[1,1,1024,1024]{3,2,1,0:T(8,128)(2,1)} %param.13) | copy-start | bytes 6291460
  2.3 53.4 %copy-start.1 = (bf16[1,1,256,1024]{3,2,1,0:T(8,128)(2,1)S(1)}, bf16[1,1,256,1024]{3,2,1,0:T(8,128)(2,1)}, u32[]{:S(2)}) copy-start(bf16[1,1,256,1024]{3,2,1,0:T(8,128)(2,1)} %param.11) | copy-start | bytes 1572868
  2.3 18.8 %all-to-all-start = ((bf16[8,32,128]{2,1,0:T(8,128)(2,1)}), bf16[8,32,128]{2,1,0:T(8,128)(2,1)S(1)}, u32[]{:S(2)}, u32[]{:S(2)}) async-start(bf16[8,32,128]{2,1,0:T(8,128)(2,1)} %get-tuple-element.16), calls=%async_computation | async-start | bytes 131072 | tf_op jit(solution)/shard_map/all_to_all | solution.py:239
  12.8 9.5 %collective-permute-start = (bf16[256,128]{1,0:T(8,128)(2,1)}, bf16[256,128]{1,0:T(8,128)(2,1)S(1)}, u32[]{:S(2)}, u32[]{:S(2)}) collective-permute-start(bf16[256,128]{1,0:T(8,128)(2,1)} %get-tuple-element.22), channel_id=1, source_target_pairs={{0,64},{64,0},{128,192},{192,128},{256,320},{320,256},{384,448},{4... | collective-permute-start | bytes 196616 | tf_op jit(solution)/shard_map/ppermute | solution.py:235
  16.7 0.8 %copy-start.9 = (bf16[1,2,128,128]{3,2,1,0:T(8,128)(2,1)S(1)}, bf16[1,2,128,128]{3,2,1,0:T(8,128)(2,1)}, u32[]{:S(2)}) copy-start(bf16[1,2,128,128]{3,2,1,0:T(8,128)(2,1)} %param.19) | copy-start | bytes 196612
  21.4 0.8 %copy-start.2 = (bf16[64,32,128]{2,1,0:T(8,128)(2,1)}, bf16[64,32,128]{2,1,0:T(8,128)(2,1)S(1)}, u32[]{:S(2)}) copy-start(bf16[64,32,128]{2,1,0:T(8,128)(2,1)S(1)} %up.1) | copy-start | bytes 1572868
  22.2 23.3 %copy-start.7 = (bf16[256,128]{1,0:T(8,128)(2,1)}, bf16[256,128]{1,0:T(8,128)(2,1)S(1)}, u32[]{:S(2)}) copy-start(bf16[256,128]{1,0:T(8,128)(2,1)S(1)} %collective-permute-done.refs_2_) | copy-start | bytes 196612
  22.3 28.3 %all-to-all-start.1 = ((bf16[64,32,128]{2,1,0:T(8,128)(2,1)}), bf16[64,32,128]{2,1,0:T(8,128)(2,1)S(1)}, u32[]{:S(2)}, u32[]{:S(2)}) async-start(bf16[64,32,128]{2,1,0:T(8,128)(2,1)} %copy-done.2), calls=%async_computation.1 | async-start | bytes 1048576 | tf_op jit(solution)/shard_map/all_to_all | solution.py:248
  34.2 22.2 %collective-permute-start.3 = (bf16[2,256,128]{2,1,0:T(8,128)(2,1)}, bf16[2,256,128]{2,1,0:T(8,128)(2,1)}, u32[]{:S(2)}, u32[]{:S(2)}) collective-permute-start(bf16[2,256,128]{2,1,0:T(8,128)(2,1)} %pad_maximum_fusion), channel_id=1, source_target_pairs={{0,128},{64,192},{128,0},{192,64},{256,384},{320,448},{384,256},{4... | collective-permute-start | bytes 393224 | tf_op jit(solution)/shard_map/ppermute | solution.py:235
  36.6 19.8 %collective-permute-start.2 = (bf16[2,256,128]{2,1,0:T(8,128)(2,1)}, bf16[2,256,128]{2,1,0:T(8,128)(2,1)}, u32[]{:S(2)}, u32[]{:S(2)}) collective-permute-start(bf16[2,256,128]{2,1,0:T(8,128)(2,1)} %pad_maximum_fusion), channel_id=1, source_target_pairs={{0,384},{64,448},{128,256},{192,320},{256,128},{320,192},{384,0},{... | collective-permute-start | bytes 393224 | tf_op jit(solution)/shard_map/ppermute | solution.py:235
  41.4 15.1 %collective-permute-start.1 = (bf16[2,256,128]{2,1,0:T(8,128)(2,1)}, bf16[2,256,128]{2,1,0:T(8,128)(2,1)}, u32[]{:S(2)}, u32[]{:S(2)}) collective-permute-start(bf16[2,256,128]{2,1,0:T(8,128)(2,1)} %pad_maximum_fusion), channel_id=1, source_target_pairs={{0,320},{64,256},{128,448},{192,384},{256,64},{320,0},{384,192},{4... | collective-permute-start | bytes 393224 | tf_op jit(solution)/shard_map/ppermute | solution.py:235
  45.6 1.0 %copy-start.3 = (bf16[1,3,4,128,128]{4,3,2,1,0:T(8,128)(2,1)S(1)}, bf16[1,3,4,128,128]{4,3,2,1,0:T(8,128)(2,1)}, u32[]{:S(2)}) copy-start(bf16[1,3,4,128,128]{4,3,2,1,0:T(8,128)(2,1)} %param.21) | copy-start | bytes 1179652
  46.6 0.8 %copy-start.10 = (bf16[1,2,128,128]{3,2,1,0:T(8,128)(2,1)S(1)}, bf16[1,2,128,128]{3,2,1,0:T(8,128)(2,1)}, u32[]{:S(2)}) copy-start(bf16[1,2,128,128]{3,2,1,0:T(8,128)(2,1)} %param.20) | copy-start | bytes 196612
  50.8 0.6 copy-start.6
  51.4 5.0 %copy-start.4 = (bf16[1,1,8,128,128]{4,3,2,1,0:T(8,128)(2,1)S(1)}, bf16[1,1,8,128,128]{4,3,2,1,0:T(8,128)(2,1)}, u32[]{:S(2)}) copy-start(bf16[1,1,8,128,128]{4,3,2,1,0:T(8,128)(2,1)} %param.18) | copy-start | bytes 786436
  51.4 5.0 %copy-start.5 = (bf16[1,1,128,1024]{3,2,1,0:T(8,128)(2,1)S(1)}, bf16[1,1,128,1024]{3,2,1,0:T(8,128)(2,1)}, u32[]{:S(2)}) copy-start(bf16[1,1,128,1024]{3,2,1,0:T(8,128)(2,1)} %param.15) | copy-start | bytes 786436
  51.5 5.0 %copy-start.8 = (bf16[256,128]{1,0:T(8,128)(2,1)S(1)}, bf16[256,128]{1,0:T(8,128)(2,1)}, u32[]{:S(2)}) copy-start(bf16[256,128]{1,0:T(8,128)(2,1)} %copy-done.7) | copy-start | bytes 196612
  51.5 5.0 %copy-start.11 = (bf16[1,1,128,128]{3,2,1,0:T(8,128)(2,1)S(1)}, bf16[1,1,128,128]{3,2,1,0:T(8,128)(2,1)}, u32[]{:S(2)}) copy-start(bf16[1,1,128,128]{3,2,1,0:T(8,128)(2,1)} %param.17) | copy-start | bytes 98308
  51.5 5.0 %copy-start.12 = (s32[1,8]{1,0:T(1,128)S(1)}, s32[1,8]{1,0:T(1,128)}, u32[]{:S(2)}) copy-start(s32[1,8]{1,0:T(1,128)} %param.12) | copy-start | bytes 100
  51.5 12.6 %all-to-all-start.2 = ((bf16[8,32,128]{2,1,0:T(8,128)(2,1)}), bf16[8,32,128]{2,1,0:T(8,128)(2,1)S(1)}, u32[]{:S(2)}, u32[]{:S(2)}) async-start(bf16[8,32,128]{2,1,0:T(8,128)(2,1)} %copy-done.6), calls=%async_computation.2 | async-start | bytes 131072 | tf_op jit(solution)/shard_map/all_to_all | solution.py:263
